TPU v7x, 256 devices: a whole 4x4x8 slice. The times are simulated.
256 devices in a mesh: dp: 16 (over x, y), zero: 16 (over z, core).
Axes of the slice: x: 4, y: 4, z: 8, core: 2. Of those that a mesh axis runs over, the one named last changes fastest.
Arguments:
- gradients: bfloat16 [16, 16, 384, 4096], P('dp', None, None, 'zero'), may hold values from -6 to 6
- momentum: bfloat16 [16, 384, 4096], P(None, None, 'zero'), may hold values from -6 to 6
- bucket_slot: int32 [16], replicated, may hold values from 0 to 15, each once
Outputs:
- new_moment: bfloat16 [16, 384, 4096], P(None, None, 'zero')
- update: bfloat16 [16, 384, 4096], P(None, None, 'zero')
Inputs may be any that keep to these rules, and one draw needn't show every extreme that they name: bucket_slot is a permutation of 0 to 15.
All inputs are finite; a program needn't handle non-finite values.
Results may differ from a plain program's by a relative error of at most 0.04.
Values may be sent and summed in bfloat16 or wider, within the bound.
No kernel may reach another device: no remote copies, remote signals or barrier semaphores. Data moves between devices by JAX's collectives and lax.ppermute only.
A program may use at most 128 MiB of HBM per device.

v0:
```python
import math

import jax
import jax.numpy as jnp
from jax import lax
from jax.sharding import PartitionSpec as P

D = 4096
ROWS = 384
ITERS = 5


momentum_decay = 0.95
coef_first = 3.4445
coef_second = -4.775
coef_third = 2.0315
rms_factor = 0.2
tiny_value = 1e-07


def newton_schulz(iterate):
    for repeat in range(ITERS):
        gram_matrix = jnp.einsum(
            "kij,klj->kil", iterate, iterate, preferred_element_type=jnp.float32
        ).astype(jnp.bfloat16)
        square = jnp.einsum(
            "kij,kjl->kil", gram_matrix, gram_matrix, preferred_element_type=jnp.float32
        )
        polynomial = (coef_second * gram_matrix.astype(jnp.float32) + coef_third * square).astype(
            jnp.bfloat16
        )
        product = jnp.einsum(
            "kij,kjl->kil", polynomial, iterate, preferred_element_type=jnp.float32
        )
        iterate = (coef_first * iterate.astype(jnp.float32) + product).astype(jnp.bfloat16)
    factor = rms_factor * math.sqrt(max(ROWS, D))
    return (factor * iterate.astype(jnp.float32)).astype(jnp.bfloat16)


def per_device(gradients, momentum, bucket_slot):
    matrix_count, row_count, width_local = momentum.shape
    replicas = lax.axis_size("dp")
    owners = lax.axis_size("zero")
    per_owner = matrix_count // owners
    ordered = jnp.take(gradients[0], bucket_slot, axis=0).astype(jnp.float32)
    average = lax.psum(ordered.astype(jnp.bfloat16), "dp").astype(jnp.float32) / replicas
    new_moment = (momentum_decay * momentum.astype(jnp.float32) + average).astype(jnp.bfloat16)
    direction = (average + momentum_decay * new_moment.astype(jnp.float32)).astype(jnp.bfloat16)
    grouped = direction.reshape(owners, per_owner, row_count, width_local)
    values = lax.all_to_all(grouped, "zero", split_axis=0, concat_axis=3, tiled=True)[0].astype(
        jnp.float32
    )
    norm_total = jnp.sqrt(jnp.sum(values * values, axis=(1, 2), keepdims=True))
    result = newton_schulz((values / (norm_total + tiny_value)).astype(jnp.bfloat16))[None]
    pieces = lax.all_to_all(result, "zero", split_axis=3, concat_axis=0, tiled=True)
    update = pieces.reshape(matrix_count, row_count, width_local)
    return (new_moment, update)


def solution(mesh):
    return jax.shard_map(
        per_device,
        mesh=mesh,
        in_specs=(P("dp", None, None, "zero"), P(None, None, "zero"), P()),
        out_specs=(P(None, None, "zero"), P(None, None, "zero")),
        check_vma=False,
    )
```

profile of v0, /device:TPU:2, one launch (start us, length us, event | category | flops | bytes accessed | tf_op | source)
XLA Modules:
  0.0 450.4 jit_solution(7451846443635532806)
XLA Ops:
  7.2 0.0 all-reduce.2.cloned.1.call-start
  7.2 0.8 compare_and_fusion
  8.0 0.7 compare_select_fusion
  8.8 0.3 copy-done
  9.1 2.4 gather_fusion
  11.5 3.9 broadcast_select_fusion
  15.4 0.0 all-reduce.2.cloned.1.call-update
  15.4 108.1 %all-reduce.2.cloned.1.call-done = bf16[16,384,256]{2,1,0:T(8,128)(2,1)} async-done(((bf16[16,384,256]{2,1,0:T(8,128)(2,1)}), bf16[16,384,256]{2,1,0:T(8,128)(2,1)}) %all-reduce.2.cloned.1.call-update) | async-done | bytes 3145744 | tf_op jit(solution)/shard_map/psum | solution.py:46
  123.5 5.3 %fusion.3 = (bf16[16,1,384,256]{3,2,1,0:T(8,128)(2,1)S(1)}, bf16[16,384,256]{2,1,0:T(8,128)(2,1)}) fusion(bf16[16,384,256]{2,1,0:T(8,128)(2,1)} %all-reduce.2.cloned.1.call-done, bf16[16,384,256]{2,1,0:T(8,128)(2,1)S(1)} %copy-done.2), kind=kLoop, calls=%fused_computation.15 | loop fusion | flops 15728640 | bytes 12582912 | tf_op jit(solution)/shard_map/reshape | solution.py:49
  128.8 79.1 %all_to_all.24 = bf16[16,1,384,256]{3,2,1,0:T(8,128)(2,1)S(1)} all-to-all(bf16[16,1,384,256]{3,2,1,0:T(8,128)(2,1)S(1)} %get-tuple-element.4), channel_id=1, replica_groups=mesh['dp'=16,'zero'=16] {'zero'}, dimensions={0} | all-to-all | bytes 6291456 | tf_op jit(solution)/shard_map/all_to_all | solution.py:50
  207.9 2.2 fusion
  210.9 2.3 fusion.53
  213.2 4.6 %copy.15 = bf16[1,1,384,16,256]{2,4,3,1,0:T(8,128)(2,1)} copy(bf16[1,1,384,16,256]{4,2,3,1,0:T(8,128)(2,1)} %fusion.53) | data formatting | bytes 6291456 | tf_op jit(solution)/shard_map/convert_element_type | solution.py:54
  217.8 4.6 %copy.16 = bf16[384,4096]{1,0:T(8,128)(2,1)} copy(bf16[384,4096]{0,1:T(8,128)(2,1)} %bitcast.63) | data formatting | bytes 6291456 | tf_op jit(solution)/shard_map/convert_element_type | solution.py:35
  222.4 1.8 fusion.19
  224.3 5.3 %add_convert_fusion.4 = bf16[384,4096]{1,0:T(8,128)(2,1)S(1)} fusion(bf16[384,4096]{1,0:T(8,128)(2,1)} %copy.16, bf16[384,4096]{0,1:T(8,128)(2,1)} %bitcast.64, bf16[384,384]{1,0:T(8,128)(2,1)S(1)} %fusion.19), kind=kOutput, calls=%fused_computation.10 | convolution fusion | flops 1328234496 | bytes 9732096 | tf_op jit(solution)/shard_map/kij,kjl->kil/dot_general | solution.py:32
  229.5 1.8 convolution_convert_fusion.3
  231.4 3.5 add_convert_fusion.3
  234.9 4.8 %convolution_convert_fusion.2 = bf16[384,384]{1,0:T(8,128)(2,1)S(1)} fusion(bf16[384,4096]{1,0:T(8,128)(2,1)} %add_convert_fusion.3), kind=kOutput, calls=%fused_computation.38 | convolution fusion | flops 1208107008 | bytes 3440640 | tf_op jit(solution)/shard_map/kij,klj->kil/dot_general | solution.py:23
  239.7 3.5 add_convert_fusion.2
  243.2 4.8 %convolution_convert_fusion.1 = bf16[384,384]{1,0:T(8,128)(2,1)S(1)} fusion(bf16[384,4096]{1,0:T(8,128)(2,1)} %add_convert_fusion.2), kind=kOutput, calls=%fused_computation.37 | convolution fusion | flops 1208107008 | bytes 3440640 | tf_op jit(solution)/shard_map/kij,klj->kil/dot_general | solution.py:23
  248.0 3.5 add_convert_fusion.1
  251.6 4.6 %convolution_convert_fusion = bf16[384,384]{1,0:T(8,128)(2,1)S(1)} fusion(bf16[384,4096]{1,0:T(8,128)(2,1)} %add_convert_fusion.1), kind=kOutput, calls=%fused_computation.36 | convolution fusion | flops 1208107008 | bytes 3440640 | tf_op jit(solution)/shard_map/kij,klj->kil/dot_general | solution.py:23
  256.2 4.9 %fusion.2 = bf16[1,1,384,4096]{3,2,1,0:T(8,128)(2,1)S(1)} fusion(bf16[384,4096]{1,0:T(8,128)(2,1)} %add_convert_fusion.1, bf16[384,384]{1,0:T(8,128)(2,1)S(1)} %convolution_convert_fusion), kind=kOutput, calls=%fused_computation.14 | convolution fusion | flops 1332953088 | bytes 6586368 | tf_op jit(solution)/shard_map/kij,kjl->kil/dot_general | solution.py:32
  261.1 10.8 %copy.17 = bf16[1,1,384,4096]{2,1,0,3:T(2,128)(2,1)} copy(bf16[1,1,384,4096]{3,2,1,0:T(8,128)(2,1)S(1)} %fusion.2) | data formatting | bytes 6291456 | tf_op jit(solution)/shard_map/broadcast_in_dim | solution.py:54
  272.0 0.5 broadcast.115
  272.5 68.6 %reduce.4 = bf16[4096,384]{1,0:T(8,128)(2,1)} reduce(bf16[4096,1,1,384]{3,2,1,0:T(2,128)(2,1)} %bitcast.61, bf16[]{:T(256)} %broadcast.115), dimensions={1,2}, to_apply=%bitcast.35.reduce_sub_computation | reduce | bytes 6291458
  341.1 4.6 %reshape.196 = bf16[16,2,49152]{2,1,0:T(2,128)(2,1)S(1)} reshape(bf16[4096,384]{1,0:T(8,128)(2,1)} %reduce.4) | data formatting | bytes 6291456
  345.8 76.5 %all_to_all.25 = bf16[16,2,49152]{2,1,0:T(2,128)(2,1)} all-to-all(bf16[16,2,49152]{2,1,0:T(2,128)(2,1)S(1)} %reshape.196), channel_id=1, replica_groups=mesh['dp'=16,'zero'=16] {'zero'}, dimensions={0} | all-to-all | bytes 6291456 | tf_op jit(solution)/shard_map/all_to_all | solution.py:55
  422.2 11.5 %reshape.197 = bf16[4096,1,1,384]{3,2,1,0:T(2,128)(2,1)} reshape(bf16[16,2,49152]{2,1,0:T(2,128)(2,1)} %all_to_all.25) | data formatting | bytes 6291456
  433.7 5.0 %copy.19 = bf16[1,1,384,4096]{2,3,0,1:T(8,128)(2,1)} copy(bf16[1,1,384,4096]{2,1,0,3:T(2,128)(2,1)} %bitcast.62) | data formatting | bytes 6291456
  438.7 4.8 %copy.18 = bf16[16,384,256]{2,1,0:T(8,128)(2,1)} copy(bf16[16,384,256]{1,2,0:T(8,128)(2,1)} %bitcast.65) | data formatting | bytes 6291456
  (10 shorter events, 0.0 us)
Async XLA Ops:
  7.2 1.9 copy-start
  7.2 116.3 %all-reduce.2.cloned.1.call-start = ((), (), s32[]{:S(2)}) async-start(), calls=%async_computation.2 | async-start | bytes 6291456 | tf_op jit(solution)/shard_map/psum | solution.py:46
  15.4 108.1 %copy-start.2 = (bf16[16,384,256]{2,1,0:T(8,128)(2,1)S(1)}, bf16[16,384,256]{2,1,0:T(8,128)(2,1)}, u32[]{:S(2)}) copy-start(bf16[16,384,256]{2,1,0:T(8,128)(2,1)} %param.4) | copy-start | bytes 9437188
  234.9 4.8 %copy-start.3 = (bf16[384,4096]{1,0:T(8,128)(2,1)S(1)}, bf16[384,4096]{1,0:T(8,128)(2,1)}, u32[]{:S(2)}) copy-start(bf16[384,4096]{1,0:T(8,128)(2,1)} %add_convert_fusion.3) | copy-start | bytes 9437188
  243.2 4.8 %copy-start.4 = (bf16[384,4096]{1,0:T(8,128)(2,1)S(1)}, bf16[384,4096]{1,0:T(8,128)(2,1)}, u32[]{:S(2)}) copy-start(bf16[384,4096]{1,0:T(8,128)(2,1)} %add_convert_fusion.2) | copy-start | bytes 9437188
  438.7 4.8 %copy-start.1 = (bf16[1,16,384,256]{3,2,1,0:T(8,128)(2,1)S(1)}, bf16[1,16,384,256]{3,2,1,0:T(8,128)(2,1)}, u32[]{:S(2)}) copy-start(bf16[1,16,384,256]{3,2,1,0:T(8,128)(2,1)} %param.3) | copy-start | bytes 9437188
Sparse Core Ops, SparseCore 0:
  15.6 107.9 all-reduce.1
where the time goes:
time: 455 us; the launch traced here: 450 us
  blocking collectives  156 us (34%)
  waiting for transfers between devices  108 us (24%)
  other arithmetic  83.9 us (18%)
  local copies, waits for them, and re-layouts  49.3 us (11%)
  matrix products  38.6 us (8%)
  between operations  14.8 us (3%)
    psum x1, waiting for transfers between devices, per_device(): lax.psum(ordered.astype(jnp.bfloat16), 'dp').astype(jnp.float32) / replicas  108 us
    all_to_all x1, blocking collectives, per_device(): lax.all_to_all(grouped, 'zero', split_axis=0, concat_axis=3, tiled=True)[0]  79.1 us
    all_to_all x1, blocking collectives, per_device(): lax.all_to_all(result, 'zero', split_axis=3, concat_axis=0, tiled=True)  76.5 us
    unnamed x1, other arithmetic  68.6 us
    unnamed x15, local copies, waits for them, and re-layouts  26.7 us
    dot_general x5, matrix products, newton_schulz(): jnp.einsum('kij,kjl->kil', polynomial, iterate, preferred_element_type=jn...  20.8 us
    dot_general x5, matrix products, newton_schulz(): jnp.einsum('kij,klj->kil', iterate, iterate, preferred_element_type=jnp.f...  17.9 us
    broadcast_in_dim x1, local copies, waits for them, and re-layouts, per_device(): newton_schulz((values / (norm_total + tiny_value)).astype(jnp.bfloat16))  10.8 us
  transfers between devices with their start and end apart: 1, of which 1 were waited for; matrix products, arithmetic and copies ran while one was open for 0% of the time, Pallas kernels for 0%

commit v1 on v0

v1 whole, which is shorter than its diff:
```python
import functools
import math

import jax
import jax.numpy as jnp
from jax import lax
from jax.experimental import pallas as pl
from jax.experimental.pallas import tpu as pltpu
from jax.sharding import PartitionSpec as P

D = 4096
ROWS = 384
ITERS = 5

momentum_decay = 0.95
coef_first = 3.4445
coef_second = -4.775
coef_third = 2.0315
rms_factor = 0.2
tiny_value = 1e-07

BF16 = jnp.bfloat16
F32 = jnp.float32
SIDE = 4
HALF = ROWS // 2


def gray(position):
    return position ^ (position >> 1)


def all_pairs(mesh_sizes, target):
    replicas, owners = mesh_sizes
    pairs = []
    for dp in range(replicas):
        for zero in range(owners):
            x, y, z, core = target(dp // SIDE, dp % SIDE, zero // 2, zero % 2)
            pairs.append((dp * owners + zero, (x * SIDE + y) * owners + z * 2 + core))
    return pairs


def cube_pairs(mesh_sizes, dim):
    flip = (1, 3)[dim % 2]

    def target(x, y, z, core):
        along_x = (dim < 2) == (core == 0)
        return (x ^ flip, y, z, core) if along_x else (x, y ^ flip, z, core)

    return all_pairs(mesh_sizes, target)


def send(value, pairs):
    return lax.ppermute(value, ("dp", "zero"), pairs)


ORDERS = ((0, 1, 2, 3), (1, 0, 3, 2))


def cube_place(dp, core):
    x, y = gray(dp // SIDE), gray(dp % SIDE)
    return jnp.where(core == 0, x | (y << 2), y | (x << 2))


def cube_device(bits, core):
    first, second = gray(bits & 3), gray(bits >> 2)
    return jnp.where(core == 0, first * SIDE + second, second * SIDE + first)


def reduce_scatter(ordered, sizes):
    held = []
    for part, order in enumerate(ORDERS):
        rows = ordered[:, part * HALF : (part + 1) * HALF, :]
        rows = rows.reshape(2, 2, 2, 2, *rows.shape[1:])
        held.append((rows, [3, 2, 1, 0]))
    for step in range(4):
        sent, kept = [], []
        for (value, dims), order in zip(held, ORDERS):
            axis = dims.index(order[step])
            sent.append(lax.index_in_dim(value, 1, axis, keepdims=False).astype(BF16))
            kept.append(lax.index_in_dim(value, 0, axis, keepdims=False))
        received = [
            send(value, cube_pairs(sizes, order[step])) for value, order in zip(sent, ORDERS)
        ]
        held = [
            (mine.astype(F32) + other.astype(F32), [d for d in dims if d != order[step]])
            for mine, other, (_, dims), order in zip(kept, received, held, ORDERS)
        ]
    return [value for value, _ in held]


def assemble_kernel(place_ref, *refs):
    out_ref, sems = refs[-2], refs[-1]
    copies = []
    for part, order in enumerate(ORDERS):
        for late in range(2):
            source = refs[2 * part + late]
            for i in range(8):
                copies.append(
                    pltpu.make_async_copy(
                        source.at[i],
                        out_ref.at[place_ref[len(copies)], pl.ds(part * HALF, HALF)],
                        sems.at[len(copies)],
                    )
                )
                copies[-1].start()
    for copy in copies:
        copy.wait()


def all_gather(halves, sizes, me, core):
    held = [(half[None], []) for half in halves]
    for step in range(3, -1, -1):
        received = [
            send(value, cube_pairs(sizes, order[step]))
            for (value, _), order in zip(held, ORDERS)
        ]
        if step:
            held = [
                (jnp.concatenate([mine, other]), [order[step]] + dims)
                for (mine, dims), other, order in zip(held, received, ORDERS)
            ]
    places, pieces = [], []
    for (mine, dims), other, order in zip(held, received, ORDERS):
        pieces += [mine, other]
        for late in range(2):
            for i in range(8):
                relative = late << order[0]
                for at, dim in enumerate(dims):
                    relative |= ((i >> (2 - at)) & 1) << dim
                places.append(relative)
    places = cube_device(me ^ jnp.array(places, jnp.int32), core)
    width = halves[0].shape[-1]
    return pl.pallas_call(
        assemble_kernel,
        out_shape=jax.ShapeDtypeStruct((16, ROWS, width), BF16),
        grid_spec=pltpu.PrefetchScalarGridSpec(
            num_scalar_prefetch=1,
            grid=(),
            in_specs=[pl.BlockSpec(memory_space=pl.ANY)] * 4,
            out_specs=pl.BlockSpec(memory_space=pl.ANY),
            scratch_shapes=[pltpu.SemaphoreType.DMA((32,))],
        ),
        name="assemble",
    )(places, *pieces)


def split(value):
    high = value.astype(BF16)
    return high, (value - high.astype(F32)).astype(BF16)


def dot(a, b):
    return jnp.dot(a, b, preferred_element_type=F32)


def newton_schulz_kernel(mine_ref, other_ref, direction_ref, *out_refs):
    gram = mine_ref[...] + other_ref[...]
    row = lax.broadcasted_iota(jnp.int32, gram.shape, 0)
    column = lax.broadcasted_iota(jnp.int32, gram.shape, 1)
    total = jnp.sum(jnp.where(row == column, gram, 0.0))
    scale = 1.0 / (jnp.sqrt(jnp.full((1, 1), total, F32)) + tiny_value)
    gram = gram * scale * scale
    iterate = direction_ref[...].astype(F32)
    for repeat in range(ITERS):
        high, low = split(gram)
        polynomial = (coef_second * gram + coef_third * dot(high, high)).astype(BF16)
        x_high, x_low = split(iterate)
        product = dot(polynomial, x_high)
        if repeat:
            product += dot(polynomial, x_low)
        iterate = coef_first * iterate + product
        if repeat < ITERS - 1:
            left = coef_first * gram + (dot(polynomial, high) + dot(polynomial, low))
            high, low = split(left)
            gram = coef_first * left + (dot(high, polynomial) + dot(low, polynomial))
    factor = rms_factor * math.sqrt(max(ROWS, D))
    result = (iterate * (factor * scale)).astype(BF16)
    for part, ref in enumerate(out_refs):
        ref[...] = result[part * HALF : (part + 1) * HALF]


def newton_schulz(mine, other, direction):
    half = jax.ShapeDtypeStruct((HALF, direction.shape[1]), BF16)
    return pl.pallas_call(
        newton_schulz_kernel,
        out_shape=[half, half],
        compiler_params=pltpu.CompilerParams(vmem_limit_bytes=32 * 1024 * 1024),
        name="newton_schulz",
    )(mine, other, direction)


def gram_of(columns):
    return lax.dot_general(
        columns, columns, (((1,), (1,)), ((), ())), preferred_element_type=F32
    )


def per_device(sizes, gradients, momentum, bucket_slot):
    dp, zero = lax.axis_index("dp"), lax.axis_index("zero")
    replicas, owners = sizes
    core, chips = zero % 2, owners // 2
    me = cube_place(dp, core)
    slots = jnp.take(bucket_slot, cube_device(me ^ jnp.arange(16), core), mode="clip")
    ordered = jnp.take(gradients[0], slots, axis=0, mode="clip")
    with jax.named_scope("sum_over_replicas"):
        total = jnp.concatenate(reduce_scatter(ordered, sizes))
    average = total / replicas
    own = lax.dynamic_index_in_dim(momentum, dp, 0, keepdims=False).astype(F32)
    moment = (momentum_decay * own + average).astype(BF16)
    direction = (average + momentum_decay * moment.astype(F32)).astype(BF16)
    with jax.named_scope("moment_gather"):
        new_moment = lax.all_gather(moment, "dp", axis=0)
    swap = all_pairs(sizes, lambda x, y, z, c: (x, y, z, 1 - c))
    ring = all_pairs(sizes, lambda x, y, z, c: (x, y, (z + 1 - 2 * c) % chips, c))
    with jax.named_scope("gram_over_columns"):
        piece = jnp.concatenate([direction, send(direction, swap)], axis=1)
        gram = gram_of(direction)
        for step in range(1, chips // 2 + 1):
            if step == chips // 2:
                piece = piece[:, : direction.shape[1]]
            piece = send(piece, ring)
            gram = gram + gram_of(piece)
        other = send(gram, swap)
    halves = newton_schulz(gram, other, direction)
    with jax.named_scope("update_gather"):
        update = all_gather(halves, sizes, me, core)
    return (new_moment, update)


def solution(mesh):
    sizes = (mesh.shape["dp"], mesh.shape["zero"])
    return jax.shard_map(
        functools.partial(per_device, sizes),
        mesh=mesh,
        in_specs=(P("dp", None, None, "zero"), P(None, None, "zero"), P()),
        out_specs=(P(None, None, "zero"), P(None, None, "zero")),
        check_vma=False,
    )
```

time: 455 us -> 248 us (0.55)
  blocking collectives: 156 us -> 0 us
  Pallas kernels: 0 us -> 104 us
  other arithmetic: 83.9 us -> 6.8 us
  matrix products: 38.6 us -> 1.76 us
  local copies, waits for them, and re-layouts: 49.3 us -> 15.2 us
  waiting for transfers between devices: 108 us -> 81.2 us
  starting transfers between devices: 0.04 us -> 24.6 us
    all_to_all x2 -> x0, blocking collectives: 156 us -> none  [the longest x1 79.1 us: per_device(): lax.all_to_all(grouped, 'zero', split_axis=0, concat_axis=3, tiled=True)[0]]
    psum x1 -> x0, waiting for transfers between devices: 108 us -> none  [per_device(): lax.psum(ordered.astype(jnp.bfloat16), 'dp').astype(jnp.float32) / replicas]
    pallas_call x0 -> x2, Pallas kernels: none -> 104 us  [the longest x1 97.3 us: all_gather(): pl.pallas_call(assemble_kernel, out_shape=jax.ShapeDtypeStruct((16, ROWS,...]
    ppermute x0 -> x22, waiting for transfers between devices: none -> 81.2 us  [send(): return lax.ppermute(value, ('dp', 'zero'), pairs)]
    unnamed x1 -> x0, other arithmetic: 68.6 us -> none
    dot_general x10 -> x5, matrix products: 38.6 us -> 1.76 us  [gram_of(): lax.dot_general(columns, columns, (((1,), (1,)), ((), ())), preferred_ele...]
    ppermute x0 -> x22, starting transfers between devices: none -> 24.6 us  [send(): return lax.ppermute(value, ('dp', 'zero'), pairs)]
    unnamed x15 -> x17, local copies, waits for them, and re-layouts: 26.7 us -> 6.98 us
  transfers between devices with their start and end apart: 1 -> 23, of which waited for: 1 -> 19; matrix products, arithmetic and copies ran while one was open for 0% -> 4% of each run, Pallas kernels for 0% -> 42%
where the time goes in v1:
time: 248 us
  Pallas kernels  104 us (42%)
  waiting for transfers between devices  81.2 us (33%)
  starting transfers between devices  24.6 us (10%)
  local copies, waits for them, and re-layouts  15.2 us (6%)
  between operations  14.4 us (6%)
  other arithmetic  6.8 us (3%)
    pallas_call x1, Pallas kernels, all_gather(): pl.pallas_call(assemble_kernel, out_shape=jax.ShapeDtypeStruct((16, ROWS,...  97.3 us
    ppermute x22, waiting for transfers between devices, send(): return lax.ppermute(value, ('dp', 'zero'), pairs)  81.2 us
    ppermute x22, starting transfers between devices, send(): return lax.ppermute(value, ('dp', 'zero'), pairs)  24.6 us
    unnamed x17, local copies, waits for them, and re-layouts  6.98 us
    pallas_call x1, Pallas kernels, newton_schulz(): pl.pallas_call(newton_schulz_kernel, out_shape=[half, half], compiler_par...  6.47 us
  transfers between devices with their start and end apart: 23, of which 19 were waited for; matrix products, arithmetic and copies ran while one was open for 4% of the time, Pallas kernels for 42%

profile of v1, /device:TPU:2, one launch (start us, length us, event | category | flops | bytes accessed | tf_op | source)
XLA Modules:
  0.0 247.8 jit_solution(17981469922506499861)
XLA Ops:
  7.3 1.5 gather_fusion
  9.1 2.4 gather_fusion.1
  11.5 2.2 fusion.23
  15.6 2.3 collective-permute-start
  20.2 7.9 %collective-permute-done = bf16[2,2,2,192,256]{4,3,0,1,2:T(8,128)(2,1)} collective-permute-done((bf16[2,2,2,192,256]{4,3,0,1,2:T(8,128)(2,1)}, bf16[2,2,2,192,256]{4,3,0,1,2:T(8,128)(2,1)}, u32[]{:S(2)}, u32[]{:S(2)}) %collective-permute-start) | collective-permute-done | bytes 786464 | tf_op jit(solution)/shard_map/sum_over_replicas/ppermute | solution.py:53
  28.2 1.6 convert_add_fusion.1
  34.8 2.9 %collective-permute-done.1 = bf16[2,2,192,256]{3,2,0,1:T(8,128)(2,1)S(1)} collective-permute-done((bf16[2,2,192,256]{3,2,0,1:T(8,128)(2,1)S(1)}, bf16[2,2,192,256]{3,2,0,1:T(8,128)(2,1)S(1)}, u32[]{:S(2)}, u32[]{:S(2)}) %collective-permute-start.1) | collective-permute-done | bytes 393248 | tf_op jit(solution)/shard_map/sum_over_replicas/ppermute | solution.py:53
  39.3 4.0 %collective-permute-done.5 = bf16[2,2,192,256]{3,2,1,0:T(8,128)(2,1)S(1)} collective-permute-done((bf16[2,2,192,256]{3,2,1,0:T(8,128)(2,1)S(1)}, bf16[2,2,192,256]{3,2,1,0:T(8,128)(2,1)S(1)}, u32[]{:S(2)}, u32[]{:S(2)}) %collective-permute-start.5) | collective-permute-done | bytes 393248 | tf_op jit(solution)/shard_map/sum_over_replicas/ppermute | solution.py:53
  43.4 1.8 collective-permute-start.6
  45.2 1.6 collective-permute-start.3
  46.8 3.5 %collective-permute-done.6 = bf16[2,192,256]{2,1,0:T(8,128)(2,1)S(1)} collective-permute-done((bf16[2,192,256]{2,1,0:T(8,128)(2,1)S(1)}, bf16[2,192,256]{2,1,0:T(8,128)(2,1)S(1)}, u32[]{:S(2)}, u32[]{:S(2)}) %collective-permute-start.6) | collective-permute-done | bytes 196640 | tf_op jit(solution)/shard_map/sum_over_replicas/ppermute | solution.py:53
  51.4 3.7 %collective-permute-done.7 = bf16[192,256]{1,0:T(8,128)(2,1)S(1)} collective-permute-done((bf16[192,256]{1,0:T(8,128)(2,1)S(1)}, bf16[192,256]{1,0:T(8,128)(2,1)S(1)}, u32[]{:S(2)}, u32[]{:S(2)}) %collective-permute-start.7) | collective-permute-done | bytes 98336 | tf_op jit(solution)/shard_map/sum_over_replicas/ppermute | solution.py:53
  55.1 1.7 add_convert_fusion.2
  58.0 1.4 collective-permute-done.8
  60.1 9.7 %collective-permute-done.9 = bf16[384,512]{1,0:T(8,128)(2,1)S(1)} collective-permute-done((bf16[384,512]{1,0:T(8,128)(2,1)S(1)}, bf16[384,512]{1,0:T(8,128)(2,1)S(1)}, u32[]{:S(2)}, u32[]{:S(2)}) %collective-permute-start.9) | collective-permute-done | bytes 393248 | tf_op jit(solution)/shard_map/gram_over_columns/ppermute | solution.py:53
  69.8 9.0 %collective-permute-done.10 = bf16[384,512]{1,0:T(8,128)(2,1)S(1)} collective-permute-done((bf16[384,512]{1,0:T(8,128)(2,1)S(1)}, bf16[384,512]{1,0:T(8,128)(2,1)S(1)}, u32[]{:S(2)}, u32[]{:S(2)}) %collective-permute-start.10) | collective-permute-done | bytes 393248 | tf_op jit(solution)/shard_map/gram_over_columns/ppermute | solution.py:53
  79.5 8.3 %collective-permute-done.11 = bf16[384,512]{1,0:T(8,128)(2,1)S(1)} collective-permute-done((bf16[384,512]{1,0:T(8,128)(2,1)S(1)}, bf16[384,512]{1,0:T(8,128)(2,1)S(1)}, u32[]{:S(2)}, u32[]{:S(2)}) %collective-permute-start.11) | collective-permute-done | bytes 393248 | tf_op jit(solution)/shard_map/gram_over_columns/ppermute | solution.py:53
  88.3 6.5 %collective-permute-done.12 = bf16[384,256]{1,0:T(8,128)(2,1)S(1)} collective-permute-done((bf16[384,256]{1,0:T(8,128)(2,1)S(1)}, bf16[384,256]{1,0:T(8,128)(2,1)S(1)}, u32[]{:S(2)}, u32[]{:S(2)}) %collective-permute-start.12) | collective-permute-done | bytes 196640 | tf_op jit(solution)/shard_map/gram_over_columns/ppermute | solution.py:53
  95.7 2.0 collective-permute-done.13.other_ref
  97.7 6.5 %newton_schulz.1 = (bf16[192,256]{1,0:T(8,128)(2,1)S(1)}, bf16[192,256]{1,0:T(8,128)(2,1)S(1)}) custom-call(f32[384,384]{1,0:T(8,128)S(1)} %fusion.mine_ref, f32[384,384]{1,0:T(8,128)S(1)} %collective-permute-done.13.other_ref, bf16[384,256]{1,0:T(8,128)(2,1)S(1)} %add_convert_fusion.direction_ref), custom_call_target="tpu_custom_call" | custom-call | tf_op jit(solution)/shard_map/newton_schulz/pallas_call | solution.py:184
  105.1 2.3 collective-permute-start.14
  107.4 2.5 %collective-permute-done.18 = bf16[1,192,256]{2,1,0:T(8,128)(2,1)S(1)} collective-permute-done((bf16[1,192,256]{2,1,0:T(8,128)(2,1)S(1)}, bf16[1,192,256]{2,1,0:T(8,128)(2,1)S(1)}, u32[]{:S(2)}, u32[]{:S(2)}) %collective-permute-start.18) | collective-permute-done | bytes 98336 | tf_op jit(solution)/shard_map/update_gather/ppermute | solution.py:53
  110.0 2.2 collective-permute-start.19
  112.7 4.3 %collective-permute-done.19 = bf16[2,192,256]{2,1,0:T(8,128)(2,1)S(1)} collective-permute-done((bf16[2,192,256]{2,1,0:T(8,128)(2,1)S(1)}, bf16[2,192,256]{2,1,0:T(8,128)(2,1)S(1)}, u32[]{:S(2)}, u32[]{:S(2)}) %collective-permute-start.19) | collective-permute-done | bytes 196640 | tf_op jit(solution)/shard_map/update_gather/ppermute | solution.py:53
  117.0 1.5 collective-permute-start.20
  118.5 1.4 collective-permute-start.16
  120.0 4.9 %collective-permute-done.20 = bf16[4,192,256]{2,1,0:T(8,128)(2,1)S(1)} collective-permute-done((bf16[4,192,256]{2,1,0:T(8,128)(2,1)S(1)}, bf16[4,192,256]{2,1,0:T(8,128)(2,1)S(1)}, u32[]{:S(2)}, u32[]{:S(2)}) %collective-permute-start.20) | collective-permute-done | bytes 393248 | tf_op jit(solution)/shard_map/update_gather/ppermute | solution.py:53
  126.5 3.1 %collective-permute-start.17 = (bf16[8,192,256]{2,1,0:T(8,128)(2,1)S(1)}, bf16[8,192,256]{2,1,0:T(8,128)(2,1)}, u32[]{:S(2)}, u32[]{:S(2)}) collective-permute-start(bf16[8,192,256]{2,1,0:T(8,128)(2,1)S(1)} %pad_maximum_fusion.refs_0_), channel_id=1, source_target_pairs={{0,64},{1,17},{2,66},{3,19},{4,68},{5,21},{6,70},{7,23},{8,72},{9,... | collective-permute-start | bytes 2359304 | tf_op jit(solution)/shard_map/update_gather/ppermute | solution.py:53
  130.2 6.8 %collective-permute-done.21.refs_3_ = bf16[8,192,256]{2,1,0:T(8,128)(2,1)S(1)} collective-permute-done((bf16[8,192,256]{2,1,0:T(8,128)(2,1)S(1)}, bf16[8,192,256]{2,1,0:T(8,128)(2,1)S(1)}, u32[]{:S(2)}, u32[]{:S(2)}) %collective-permute-start.21) | collective-permute-done | bytes 786464 | tf_op jit(solution)/shard_map/update_gather/ppermute | solution.py:53
  137.9 1.8 collective-permute-done.17.refs_1_
  139.7 97.3 %assemble.1 = bf16[16,384,256]{2,1,0:T(8,128)(2,1)} custom-call(s32[32]{0:T(128)} %broadcast_select_fusion.place_ref, bf16[8,192,256]{2,1,0:T(8,128)(2,1)} %copy-done.2, bf16[8,192,256]{2,1,0:T(8,128)(2,1)} %collective-permute-done.17.refs_1_, bf16[8,192,256]{2,1,0:T(8,128)(2,1)} %copy-done.1, bf16[8,192,256]{2,1,0:T(8,128)(2,1)} %copy-done.5), custom_call_target="tpu_custom_call" | custom-call | tf_op jit(solution)/shard_map/update_gather/assemble/pallas_call | solution.py:133
  237.1 3.8 %copy.29 = bf16[16,384,256]{2,1,0:T(8,128)(2,1)} copy(bf16[16,384,256]{2,1,0:T(8,128)(2,1)} %all-gather.2.cloned.1.call-done) | data formatting | bytes 6291456
  (72 shorter events, 21.0 us)
Async XLA Ops:
  7.2 1.9 copy-start
  7.2 229.9 %all-gather.2.cloned.1.call-start = ((), (), s32[]{:S(2)}) async-start(), calls=%async_computation | async-start | bytes 3342336 | tf_op jit(solution)/shard_map/moment_gather/all_gather | solution.py:212
  15.6 12.6 %collective-permute-start = (bf16[2,2,2,192,256]{4,3,0,1,2:T(8,128)(2,1)}, bf16[2,2,2,192,256]{4,3,0,1,2:T(8,128)(2,1)}, u32[]{:S(2)}, u32[]{:S(2)}) collective-permute-start(bf16[2,2,2,192,256]{4,3,0,1,2:T(8,128)(2,1)} %bitcast.77), channel_id=1, source_target_pairs={{0,64},{1,17},{2,66},{3,19},{4,68},{5,21},{6,70},{7,23},{8,72},{9,... | collective-permute-start | bytes 2359304 | tf_op jit(solution)/shard_map/sum_over_replicas/ppermute | solution.py:53
  19.8 12.3 %collective-permute-start.4 = (bf16[2,2,2,192,256]{4,3,1,0,2:T(8,128)(2,1)}, bf16[2,2,2,192,256]{4,3,1,0,2:T(8,128)(2,1)}, u32[]{:S(2)}, u32[]{:S(2)}) collective-permute-start(bf16[2,2,2,192,256]{4,3,1,0,2:T(8,128)(2,1)} %bitcast.76), channel_id=1, source_target_pairs={{0,192},{1,49},{2,194},{3,51},{4,196},{5,53},{6,198},{7,55},{8,200... | collective-permute-start | bytes 2359304 | tf_op jit(solution)/shard_map/sum_over_replicas/ppermute | solution.py:53
  28.2 3.9 %copy-start.3 = (bf16[2,2,1,2,192,256]{5,4,3,2,1,0:T(8,128)(2,1)S(1)}, bf16[2,2,1,2,192,256]{5,4,3,2,1,0:T(8,128)(2,1)}, u32[]{:S(2)}) copy-start(bf16[2,2,1,2,192,256]{5,4,3,2,1,0:T(8,128)(2,1)} %get-tuple-element.10) | copy-start | bytes 2359300
  29.9 7.9 %collective-permute-start.1 = (bf16[2,2,192,256]{3,2,0,1:T(8,128)(2,1)S(1)}, bf16[2,2,192,256]{3,2,0,1:T(8,128)(2,1)S(1)}, u32[]{:S(2)}, u32[]{:S(2)}) collective-permute-start(bf16[2,2,192,256]{3,2,0,1:T(8,128)(2,1)S(1)} %fusion.3), channel_id=1, source_target_pairs={{0,192},{1,49},{2,194},{3,51},{4,196},{5,53},{6,198},{7,55},{8,200... | collective-permute-start | bytes 1179656 | tf_op jit(solution)/shard_map/sum_over_replicas/ppermute | solution.py:53
  33.5 9.8 %collective-permute-start.5 = (bf16[2,2,192,256]{3,2,1,0:T(8,128)(2,1)S(1)}, bf16[2,2,192,256]{3,2,1,0:T(8,128)(2,1)S(1)}, u32[]{:S(2)}, u32[]{:S(2)}) collective-permute-start(bf16[2,2,192,256]{3,2,1,0:T(8,128)(2,1)S(1)} %fusion.4), channel_id=1, source_target_pairs={{0,64},{1,17},{2,66},{3,19},{4,68},{5,21},{6,70},{7,23},{8,72},{9,... | collective-permute-start | bytes 1179656 | tf_op jit(solution)/shard_map/sum_over_replicas/ppermute | solution.py:53
  37.9 7.3 %collective-permute-start.2 = (bf16[2,192,256]{2,1,0:T(8,128)(2,1)S(1)}, bf16[2,192,256]{2,1,0:T(8,128)(2,1)S(1)}, u32[]{:S(2)}, u32[]{:S(2)}) collective-permute-start(bf16[2,192,256]{2,1,0:T(8,128)(2,1)S(1)} %fusion.11), channel_id=1, source_target_pairs={{0,16},{1,65},{2,18},{3,67},{4,20},{5,69},{6,22},{7,71},{8,24},{9,... | collective-permute-start | bytes 589832 | tf_op jit(solution)/shard_map/sum_over_replicas/ppermute | solution.py:53
  43.4 7.0 %collective-permute-start.6 = (bf16[2,192,256]{2,1,0:T(8,128)(2,1)S(1)}, bf16[2,192,256]{2,1,0:T(8,128)(2,1)S(1)}, u32[]{:S(2)}, u32[]{:S(2)}) collective-permute-start(bf16[2,192,256]{2,1,0:T(8,128)(2,1)S(1)} %fusion.12), channel_id=1, source_target_pairs={{0,48},{1,193},{2,50},{3,195},{4,52},{5,197},{6,54},{7,199},{8,56}... | collective-permute-start | bytes 589832 | tf_op jit(solution)/shard_map/sum_over_replicas/ppermute | solution.py:53
  45.2 6.2 %collective-permute-start.3 = (bf16[192,256]{1,0:T(8,128)(2,1)S(1)}, bf16[192,256]{1,0:T(8,128)(2,1)S(1)}, u32[]{:S(2)}, u32[]{:S(2)}) collective-permute-start(bf16[192,256]{1,0:T(8,128)(2,1)S(1)} %fusion.17), channel_id=1, source_target_pairs={{0,48},{1,193},{2,50},{3,195},{4,52},{5,197},{6,54},{7,199},{8,56}... | collective-permute-start | bytes 294920 | tf_op jit(solution)/shard_map/sum_over_replicas/ppermute | solution.py:53
  50.4 4.7 %collective-permute-start.7 = (bf16[192,256]{1,0:T(8,128)(2,1)S(1)}, bf16[192,256]{1,0:T(8,128)(2,1)S(1)}, u32[]{:S(2)}, u32[]{:S(2)}) collective-permute-start(bf16[192,256]{1,0:T(8,128)(2,1)S(1)} %fusion.18), channel_id=1, source_target_pairs={{0,16},{1,65},{2,18},{3,67},{4,20},{5,69},{6,22},{7,71},{8,24},{9,... | collective-permute-start | bytes 294920 | tf_op jit(solution)/shard_map/sum_over_replicas/ppermute | solution.py:53
  56.8 21.9 %copy-start.4 = (bf16[1,384,256]{2,1,0:T(8,128)(2,1)S(1)}, bf16[1,384,256]{2,1,0:T(8,128)(2,1)}, u32[]{:S(2)}) copy-start(bf16[1,384,256]{2,1,0:T(8,128)(2,1)} %add_convert_fusion.2) | copy-start | bytes 589828
  57.9 1.5 collective-permute-start.8
  59.5 10.3 %collective-permute-start.9 = (bf16[384,512]{1,0:T(8,128)(2,1)S(1)}, bf16[384,512]{1,0:T(8,128)(2,1)S(1)}, u32[]{:S(2)}, u32[]{:S(2)}) collective-permute-start(bf16[384,512]{1,0:T(8,128)(2,1)S(1)} %pad_maximum_fusion.2), channel_id=1, source_target_pairs={{0,2},{1,15},{2,4},{3,1},{4,6},{5,3},{6,8},{7,5},{8,10},{9,7},{10,... | collective-permute-start | bytes 1179656 | tf_op jit(solution)/shard_map/gram_over_columns/ppermute | solution.py:53
  69.8 9.0 %collective-permute-start.10 = (bf16[384,512]{1,0:T(8,128)(2,1)S(1)}, bf16[384,512]{1,0:T(8,128)(2,1)S(1)}, u32[]{:S(2)}, u32[]{:S(2)}) collective-permute-start(bf16[384,512]{1,0:T(8,128)(2,1)S(1)} %collective-permute-done.9), channel_id=1, source_target_pairs={{0,2},{1,15},{2,4},{3,1},{4,6},{5,3},{6,8},{7,5},{8,10},{9,7},{10,... | collective-permute-start | bytes 1179656 | tf_op jit(solution)/shard_map/gram_over_columns/ppermute | solution.py:53
  78.8 9.0 %collective-permute-start.11 = (bf16[384,512]{1,0:T(8,128)(2,1)S(1)}, bf16[384,512]{1,0:T(8,128)(2,1)S(1)}, u32[]{:S(2)}, u32[]{:S(2)}) collective-permute-start(bf16[384,512]{1,0:T(8,128)(2,1)S(1)} %collective-permute-done.10), channel_id=1, source_target_pairs={{0,2},{1,15},{2,4},{3,1},{4,6},{5,3},{6,8},{7,5},{8,10},{9,7},{10,... | collective-permute-start | bytes 1179656 | tf_op jit(solution)/shard_map/gram_over_columns/ppermute | solution.py:53
  87.8 7.0 %collective-permute-start.12 = (bf16[384,256]{1,0:T(8,128)(2,1)S(1)}, bf16[384,256]{1,0:T(8,128)(2,1)S(1)}, u32[]{:S(2)}, u32[]{:S(2)}) collective-permute-start(bf16[384,256]{1,0:T(8,128)(2,1)S(1)} %slice.104), channel_id=1, source_target_pairs={{0,2},{1,15},{2,4},{3,1},{4,6},{5,3},{6,8},{7,5},{8,10},{9,7},{10,... | collective-permute-start | bytes 589832 | tf_op jit(solution)/shard_map/gram_over_columns/ppermute | solution.py:53
  95.4 2.3 collective-permute-start.13
  104.2 5.8 %collective-permute-start.18 = (bf16[1,192,256]{2,1,0:T(8,128)(2,1)S(1)}, bf16[1,192,256]{2,1,0:T(8,128)(2,1)S(1)}, u32[]{:S(2)}, u32[]{:S(2)}) collective-permute-start(bf16[1,192,256]{2,1,0:T(8,128)(2,1)S(1)} %bitcast.83), channel_id=1, source_target_pairs={{0,16},{1,65},{2,18},{3,67},{4,20},{5,69},{6,22},{7,71},{8,24},{9,... | collective-permute-start | bytes 294920 | tf_op jit(solution)/shard_map/update_gather/ppermute | solution.py:53
  105.1 7.0 %collective-permute-start.14 = (bf16[1,192,256]{2,1,0:T(8,128)(2,1)S(1)}, bf16[1,192,256]{2,1,0:T(8,128)(2,1)S(1)}, u32[]{:S(2)}, u32[]{:S(2)}) collective-permute-start(bf16[1,192,256]{2,1,0:T(8,128)(2,1)S(1)} %bitcast.79), channel_id=1, source_target_pairs={{0,48},{1,193},{2,50},{3,195},{4,52},{5,197},{6,54},{7,199},{8,56}... | collective-permute-start | bytes 294920 | tf_op jit(solution)/shard_map/update_gather/ppermute | solution.py:53
  110.0 7.0 %collective-permute-start.19 = (bf16[2,192,256]{2,1,0:T(8,128)(2,1)S(1)}, bf16[2,192,256]{2,1,0:T(8,128)(2,1)S(1)}, u32[]{:S(2)}, u32[]{:S(2)}) collective-permute-start(bf16[2,192,256]{2,1,0:T(8,128)(2,1)S(1)} %pad_maximum_fusion.6), channel_id=1, source_target_pairs={{0,48},{1,193},{2,50},{3,195},{4,52},{5,197},{6,54},{7,199},{8,56}... | collective-permute-start | bytes 589832 | tf_op jit(solution)/shard_map/update_gather/ppermute | solution.py:53
  112.2 6.3 %collective-permute-start.15 = (bf16[2,192,256]{2,1,0:T(8,128)(2,1)S(1)}, bf16[2,192,256]{2,1,0:T(8,128)(2,1)S(1)}, u32[]{:S(2)}, u32[]{:S(2)}) collective-permute-start(bf16[2,192,256]{2,1,0:T(8,128)(2,1)S(1)} %pad_maximum_fusion.5), channel_id=1, source_target_pairs={{0,16},{1,65},{2,18},{3,67},{4,20},{5,69},{6,22},{7,71},{8,24},{9,... | collective-permute-start | bytes 589832 | tf_op jit(solution)/shard_map/update_gather/ppermute | solution.py:53
  117.0 7.9 %collective-permute-start.20 = (bf16[4,192,256]{2,1,0:T(8,128)(2,1)S(1)}, bf16[4,192,256]{2,1,0:T(8,128)(2,1)S(1)}, u32[]{:S(2)}, u32[]{:S(2)}) collective-permute-start(bf16[4,192,256]{2,1,0:T(8,128)(2,1)S(1)} %pad_maximum_fusion.4), channel_id=1, source_target_pairs={{0,64},{1,17},{2,66},{3,19},{4,68},{5,21},{6,70},{7,23},{8,72},{9,... | collective-permute-start | bytes 1179656 | tf_op jit(solution)/shard_map/update_gather/ppermute | solution.py:53
  118.5 11.1 %copy-start.6 = (s32[32]{0:T(128)S(1)}, s32[32]{0:T(128)}, u32[]{:S(2)}) copy-start(s32[32]{0:T(128)} %constant.63.clone) | copy-start | bytes 388
  118.5 7.9 %collective-permute-start.16 = (bf16[4,192,256]{2,1,0:T(8,128)(2,1)S(1)}, bf16[4,192,256]{2,1,0:T(8,128)(2,1)S(1)}, u32[]{:S(2)}, u32[]{:S(2)}) collective-permute-start(bf16[4,192,256]{2,1,0:T(8,128)(2,1)S(1)} %pad_maximum_fusion.3), channel_id=1, source_target_pairs={{0,192},{1,49},{2,194},{3,51},{4,196},{5,53},{6,198},{7,55},{8,200... | collective-permute-start | bytes 1179656 | tf_op jit(solution)/shard_map/update_gather/ppermute | solution.py:53
  124.9 1.6 copy-start.1
  124.9 12.1 %collective-permute-start.21 = (bf16[8,192,256]{2,1,0:T(8,128)(2,1)S(1)}, bf16[8,192,256]{2,1,0:T(8,128)(2,1)S(1)}, u32[]{:S(2)}, u32[]{:S(2)}) collective-permute-start(bf16[8,192,256]{2,1,0:T(8,128)(2,1)S(1)} %pad_maximum_fusion.1.refs_2_), channel_id=1, source_target_pairs={{0,192},{1,49},{2,194},{3,51},{4,196},{5,53},{6,198},{7,55},{8,200... | collective-permute-start | bytes 2359304 | tf_op jit(solution)/shard_map/update_gather/ppermute | solution.py:53
  126.5 10.5 %copy-start.2 = (bf16[8,192,256]{2,1,0:T(8,128)(2,1)}, bf16[8,192,256]{2,1,0:T(8,128)(2,1)S(1)}, u32[]{:S(2)}) copy-start(bf16[8,192,256]{2,1,0:T(8,128)(2,1)S(1)} %pad_maximum_fusion.refs_0_) | copy-start | bytes 2359300
  126.5 13.2 %collective-permute-start.17 = (bf16[8,192,256]{2,1,0:T(8,128)(2,1)S(1)}, bf16[8,192,256]{2,1,0:T(8,128)(2,1)}, u32[]{:S(2)}, u32[]{:S(2)}) collective-permute-start(bf16[8,192,256]{2,1,0:T(8,128)(2,1)S(1)} %pad_maximum_fusion.refs_0_), channel_id=1, source_target_pairs={{0,64},{1,17},{2,66},{3,19},{4,68},{5,21},{6,70},{7,23},{8,72},{9,... | collective-permute-start | bytes 2359304 | tf_op jit(solution)/shard_map/update_gather/ppermute | solution.py:53
  137.0 0.9 copy-start.5
Sparse Core Ops, SparseCore 0:
  57.0 54.5 all-gather.1

commit v2 on v1

v2 whole, which is shorter than its diff:
```python
import functools
import math

import jax
import jax.numpy as jnp
from jax import lax
from jax.experimental import pallas as pl
from jax.experimental.pallas import tpu as pltpu
from jax.sharding import PartitionSpec as P

D = 4096
ROWS = 384
ITERS = 5

momentum_decay = 0.95
coef_first = 3.4445
coef_second = -4.775
coef_third = 2.0315
rms_factor = 0.2
tiny_value = 1e-07

BF16 = jnp.bfloat16
F32 = jnp.float32
SIDE = 4
HALF = ROWS // 2


def gray(position):
    return position ^ (position >> 1)


def all_pairs(mesh_sizes, target):
    replicas, owners = mesh_sizes
    pairs = []
    for dp in range(replicas):
        for zero in range(owners):
            x, y, z, core = target(dp // SIDE, dp % SIDE, zero // 2, zero % 2)
            pairs.append((dp * owners + zero, (x * SIDE + y) * owners + z * 2 + core))
    return pairs


def cube_pairs(mesh_sizes, dim):
    flip = (1, 3)[dim % 2]

    def target(x, y, z, core):
        along_x = (dim < 2) == (core == 0)
        return (x ^ flip, y, z, core) if along_x else (x, y ^ flip, z, core)

    return all_pairs(mesh_sizes, target)


def send(value, pairs):
    return lax.ppermute(value, ("dp", "zero"), pairs)


ORDERS = ((0, 1, 2, 3), (1, 0, 3, 2))


def cube_place(dp, core):
    x, y = gray(dp // SIDE), gray(dp % SIDE)
    return jnp.where(core == 0, x | (y << 2), y | (x << 2))


def cube_device(bits, core):
    first, second = gray(bits & 3), gray(bits >> 2)
    return jnp.where(core == 0, first * SIDE + second, second * SIDE + first)


def vmem(count):
    return [pl.BlockSpec(memory_space=pltpu.VMEM)] * count


def pack_kernel(slot_ref, gradients_ref, *out_refs):
    for part, out_ref in enumerate(out_refs):
        for i in range(8):
            slot = slot_ref[part * 8 + i]
            out_ref[i] = gradients_ref[slot, part * HALF : (part + 1) * HALF]


def pack(slots, gradients):
    half = jax.ShapeDtypeStruct((8, HALF, gradients.shape[-1]), BF16)
    return pl.pallas_call(
        pack_kernel,
        out_shape=[half, half],
        in_specs=[pl.BlockSpec(memory_space=pltpu.SMEM)] + vmem(1),
        out_specs=vmem(2),
        compiler_params=pltpu.CompilerParams(vmem_limit_bytes=16 * 1024 * 1024),
        cost_estimate=pl.CostEstimate(flops=0, bytes_accessed=6 << 20, transcendentals=0),
        name="pack",
    )(slots, gradients)


def relative_bits(dims):
    places = []
    for i in range(1 << len(dims)):
        place = 0
        for at, dim in enumerate(dims):
            place |= ((i >> (len(dims) - 1 - at)) & 1) << dim
        places.append(place)
    return places


def reduce_scatter(gradients, slots, sizes):
    sent_places, kept_places = [], []
    for order in ORDERS:
        rest = relative_bits(order[1:])
        sent_places += [place | 1 << order[0] for place in rest]
        kept_places += rest
    sent = pack(jnp.take(slots, jnp.array(sent_places), mode="clip"), gradients)
    received = [send(value, cube_pairs(sizes, order[0])) for value, order in zip(sent, ORDERS)]
    kept = pack(jnp.take(slots, jnp.array(kept_places), mode="clip"), gradients)
    for step in range(1, 4):
        half = kept[0].shape[0] // 2
        sent = [
            (mine[half:].astype(F32) + other[half:].astype(F32)).astype(BF16)
            for mine, other in zip(kept, received)
        ]
        kept = [
            mine[:half].astype(F32) + other[:half].astype(F32)
            for mine, other in zip(kept, received)
        ]
        received = [
            send(value, cube_pairs(sizes, order[step])) for value, order in zip(sent, ORDERS)
        ]
    return [(mine + other.astype(F32))[0] for mine, other in zip(kept, received)]


def assemble_kernel(place_ref, *refs):
    out_ref, sems = refs[-2], refs[-1]
    copies = []
    for part in range(2):
        for i in range(8):
            copies.append(
                pltpu.make_async_copy(
                    refs[part].at[i],
                    out_ref.at[place_ref[part * 8 + i], pl.ds(part * HALF, HALF)],
                    sems.at[part * 8 + i],
                )
            )
            copies[-1].start()
    for copy in copies:
        copy.wait()


def assemble(places, pieces, onto=None):
    width = pieces[0].shape[-1]
    anywhere = pl.BlockSpec(memory_space=pl.ANY)
    extra = [] if onto is None else [onto]
    return pl.pallas_call(
        assemble_kernel,
        out_shape=jax.ShapeDtypeStruct((16, ROWS, width), BF16),
        in_specs=[pl.BlockSpec(memory_space=pltpu.SMEM)] + vmem(2) + [anywhere] * len(extra),
        out_specs=anywhere,
        scratch_shapes=[pltpu.SemaphoreType.DMA((16,))],
        input_output_aliases={3: 0} if extra else {},
        compiler_params=pltpu.CompilerParams(vmem_limit_bytes=16 * 1024 * 1024),
        cost_estimate=pl.CostEstimate(flops=0, bytes_accessed=3 << 20, transcendentals=0),
        name="assemble",
    )(places, *pieces, *extra)


def all_gather(halves, sizes, me, core):
    held = [half[None] for half in halves]
    for step in range(3, -1, -1):
        received = [
            send(value, cube_pairs(sizes, order[step])) for value, order in zip(held, ORDERS)
        ]
        if step:
            held = [jnp.concatenate([mine, other]) for mine, other in zip(held, received)]
    near, far = [], []
    for order in ORDERS:
        rest = relative_bits(order[1:])
        near += rest
        far += [place | 1 << order[0] for place in rest]
    out = assemble(cube_device(me ^ jnp.array(near, jnp.int32), core), held)
    return assemble(cube_device(me ^ jnp.array(far, jnp.int32), core), received, out)


def split(value):
    high = value.astype(BF16)
    return high, (value - high.astype(F32)).astype(BF16)


def dot(a, b):
    return jnp.dot(a, b, preferred_element_type=F32)


def newton_schulz_kernel(mine_ref, other_ref, direction_ref, *out_refs):
    gram = mine_ref[...] + other_ref[...]
    row = lax.broadcasted_iota(jnp.int32, gram.shape, 0)
    column = lax.broadcasted_iota(jnp.int32, gram.shape, 1)
    total = jnp.sum(jnp.where(row == column, gram, 0.0))
    scale = 1.0 / (jnp.sqrt(jnp.full((1, 1), total, F32)) + tiny_value)
    gram = gram * scale * scale
    iterate = direction_ref[...].astype(F32)
    for repeat in range(ITERS):
        high, low = split(gram)
        polynomial = (coef_second * high.astype(F32) + coef_third * dot(high, high)).astype(BF16)
        x_high, x_low = split(iterate)
        product = dot(polynomial, x_high)
        if repeat:
            product += dot(polynomial, x_low)
        iterate = coef_first * iterate + product
        if repeat < ITERS - 1:
            left = coef_first * gram + (dot(polynomial, high) + dot(polynomial, low))
            high, low = split(left)
            gram = coef_first * left + (dot(high, polynomial) + dot(low, polynomial))
    factor = rms_factor * math.sqrt(max(ROWS, D))
    result = (iterate * (factor * scale)).astype(BF16)
    for part, ref in enumerate(out_refs):
        ref[...] = result[part * HALF : (part + 1) * HALF]


def newton_schulz(mine, other, direction):
    half = jax.ShapeDtypeStruct((HALF, direction.shape[1]), BF16)
    return pl.pallas_call(
        newton_schulz_kernel,
        out_shape=[half, half],
        in_specs=vmem(3),
        out_specs=vmem(2),
        compiler_params=pltpu.CompilerParams(vmem_limit_bytes=32 * 1024 * 1024),
        cost_estimate=pl.CostEstimate(flops=3 << 30, bytes_accessed=2 << 20, transcendentals=0),
        name="newton_schulz",
    )(mine, other, direction)


def gram_of(columns):
    return lax.dot_general(
        columns, columns, (((1,), (1,)), ((), ())), preferred_element_type=F32
    )


def per_device(sizes, gradients, momentum, bucket_slot):
    dp, zero = lax.axis_index("dp"), lax.axis_index("zero")
    replicas, owners = sizes
    core, chips = zero % 2, owners // 2
    me = cube_place(dp, core)
    slots = jnp.take(bucket_slot, cube_device(me ^ jnp.arange(16), core), mode="clip")
    with jax.named_scope("sum_over_replicas"):
        total = jnp.concatenate(reduce_scatter(gradients[0], slots, sizes))
    average = total / replicas
    own = lax.dynamic_index_in_dim(momentum, dp, 0, keepdims=False).astype(F32)
    moment = (momentum_decay * own + average).astype(BF16)
    direction = (average + momentum_decay * moment.astype(F32)).astype(BF16)
    swap = all_pairs(sizes, lambda x, y, z, c: (x, y, z, 1 - c))
    ring = all_pairs(sizes, lambda x, y, z, c: (x, y, (z + 1 - 2 * c) % chips, c))
    with jax.named_scope("gram_over_columns"):
        same, cross = direction, send(direction, swap)
        gram = gram_of(direction)
        for step in range(1, chips // 2 + 1):
            same = send(same, ring)
            gram = gram + gram_of(same)
            if step < chips // 2:
                cross = send(cross, ring)
                gram = gram + gram_of(cross)
        other = send(gram, swap)
    halves = newton_schulz(gram, other, direction)
    with jax.named_scope("moment_gather"):
        new_moment = all_gather([moment[:HALF], moment[HALF:]], sizes, me, core)
    with jax.named_scope("update_gather"):
        update = all_gather(halves, sizes, me, core)
    return (new_moment, update)


def solution(mesh):
    sizes = (mesh.shape["dp"], mesh.shape["zero"])
    return jax.shard_map(
        functools.partial(per_device, sizes),
        mesh=mesh,
        in_specs=(P("dp", None, None, "zero"), P(None, None, "zero"), P()),
        out_specs=(P(None, None, "zero"), P(None, None, "zero")),
        check_vma=False,
    )
```

time: 248 us -> 138 us (0.56)
  Pallas kernels: 104 us -> 16.2 us
  between operations: 14.4 us -> 1.2 us
  starting transfers between devices: 24.6 us -> 37.6 us
  local copies, waits for them, and re-layouts: 15.2 us -> 3.91 us
  waiting for transfers between devices: 81.2 us -> 70 us
    pallas_call x2 -> x7, Pallas kernels: 104 us -> 16.2 us  [the longest x4 7.24 us: assemble(): pl.pallas_call(assemble_kernel, out_shape=jax.ShapeDtypeStruct((16, ROWS,...]
    ppermute x22 -> x33, starting transfers between devices: 24.6 us -> 37.6 us  [send(): return lax.ppermute(value, ('dp', 'zero'), pairs)]
    ppermute x22 -> x33, waiting for transfers between devices: 81.2 us -> 70 us  [send(): return lax.ppermute(value, ('dp', 'zero'), pairs)]
    unnamed x17 -> x10, local copies, waits for them, and re-layouts: 6.98 us -> 1.92 us
    slice x4 -> x0, local copies, waits for them, and re-layouts: 4.19 us -> none  [the longest x1 2.2 us: reduce_scatter(): rows = ordered[:, part * HALF:(part + 1) * HALF, :]]
    add x8 -> x2, other arithmetic: 3.2 us -> 0.06 us  [reduce_scatter(): mine + other.astype(F32)]
  transfers between devices with their start and end apart: 23 -> 33, of which waited for: 19 -> 21; matrix products, arithmetic and copies ran while one was open for 4% -> 5% of each run, Pallas kernels for 42% -> 9%
where the time goes in v2:
time: 138 us; the launch traced here: 137 us
  waiting for transfers between devices  70 us (51%)
  starting transfers between devices  37.6 us (27%)
  Pallas kernels  16.2 us (12%)
  other arithmetic  5.13 us (4%)
  local copies, waits for them, and re-layouts  3.91 us (3%)
  matrix products  3.35 us (2%)
    ppermute x33, waiting for transfers between devices, send(): return lax.ppermute(value, ('dp', 'zero'), pairs)  70 us
    ppermute x33, starting transfers between devices, send(): return lax.ppermute(value, ('dp', 'zero'), pairs)  37.6 us
    pallas_call x4, Pallas kernels, assemble(): pl.pallas_call(assemble_kernel, out_shape=jax.ShapeDtypeStruct((16, ROWS,...  7.24 us
    pallas_call x1, Pallas kernels, newton_schulz(): pl.pallas_call(newton_schulz_kernel, out_shape=[half, half], in_specs=vme...  6.51 us
    dot_general x8, matrix products, gram_of(): lax.dot_general(columns, columns, (((1,), (1,)), ((), ())), preferred_ele...  3.35 us
    convert_element_type x6, other arithmetic, reduce_scatter(): (mine[half:].astype(F32) + other[half:].astype(F32)).astype(BF16)  2.78 us
  transfers between devices with their start and end apart: 33, of which 21 were waited for; matrix products, arithmetic and copies ran while one was open for 5% of the time, Pallas kernels for 9%

profile of v2, /device:TPU:2, one launch (start us, length us, event | category | flops | bytes accessed | tf_op | source)
XLA Modules:
  0.0 137.4 jit_solution(10990015777782070773)
XLA Ops:
  2.7 1.9 %copy-done.1 = bf16[1,16,384,256]{3,2,1,0:T(8,128)(2,1)S(1)} copy-done((bf16[1,16,384,256]{3,2,1,0:T(8,128)(2,1)S(1)}, bf16[1,16,384,256]{3,2,1,0:T(8,128)(2,1)}, u32[]{:S(2)}) %copy-start.1) | copy-done | bytes 3145752
  6.4 2.3 %collective-permute-start = (bf16[8,192,256]{2,1,0:T(8,128)(2,1)}, bf16[8,192,256]{2,1,0:T(8,128)(2,1)}, u32[]{:S(2)}, u32[]{:S(2)}) collective-permute-start(bf16[8,192,256]{2,1,0:T(8,128)(2,1)} %get-tuple-element.9), channel_id=1, source_target_pairs={{0,64},{1,17},{2,66},{3,19},{4,68},{5,21},{6,70},{7,23},{8,72},{9,... | collective-permute-start | bytes 2359304 | tf_op jit(solution)/shard_map/sum_over_replicas/ppermute | solution.py:53
  10.4 8.5 %collective-permute-done = bf16[8,192,256]{2,1,0:T(8,128)(2,1)} collective-permute-done((bf16[8,192,256]{2,1,0:T(8,128)(2,1)}, bf16[8,192,256]{2,1,0:T(8,128)(2,1)}, u32[]{:S(2)}, u32[]{:S(2)}) %collective-permute-start) | collective-permute-done | bytes 786464 | tf_op jit(solution)/shard_map/sum_over_replicas/ppermute | solution.py:53
  22.9 1.9 %collective-permute-start.5 = (bf16[4,192,256]{2,1,0:T(8,128)(2,1)S(1)}, bf16[4,192,256]{2,1,0:T(8,128)(2,1)S(1)}, u32[]{:S(2)}, u32[]{:S(2)}) collective-permute-start(bf16[4,192,256]{2,1,0:T(8,128)(2,1)S(1)} %get-tuple-element.18), channel_id=1, source_target_pairs={{0,64},{1,17},{2,66},{3,19},{4,68},{5,21},{6,70},{7,23},{8,72},{9,... | collective-permute-start | bytes 1179656 | tf_op jit(solution)/shard_map/sum_over_replicas/ppermute | solution.py:53
  24.8 3.3 %collective-permute-done.1 = bf16[4,192,256]{2,1,0:T(8,128)(2,1)S(1)} collective-permute-done((bf16[4,192,256]{2,1,0:T(8,128)(2,1)S(1)}, bf16[4,192,256]{2,1,0:T(8,128)(2,1)S(1)}, u32[]{:S(2)}, u32[]{:S(2)}) %collective-permute-start.1) | collective-permute-done | bytes 393248 | tf_op jit(solution)/shard_map/sum_over_replicas/ppermute | solution.py:53
  29.6 2.4 %collective-permute-done.5 = bf16[4,192,256]{2,1,0:T(8,128)(2,1)S(1)} collective-permute-done((bf16[4,192,256]{2,1,0:T(8,128)(2,1)S(1)}, bf16[4,192,256]{2,1,0:T(8,128)(2,1)S(1)}, u32[]{:S(2)}, u32[]{:S(2)}) %collective-permute-start.5) | collective-permute-done | bytes 393248 | tf_op jit(solution)/shard_map/sum_over_replicas/ppermute | solution.py:53
  32.1 3.2 %collective-permute-start.6 = (bf16[2,192,256]{2,1,0:T(8,128)(2,1)S(1)}, bf16[2,192,256]{2,1,0:T(8,128)(2,1)S(1)}, u32[]{:S(2)}, u32[]{:S(2)}) collective-permute-start(bf16[2,192,256]{2,1,0:T(8,128)(2,1)S(1)} %get-tuple-element.22), channel_id=1, source_target_pairs={{0,48},{1,193},{2,50},{3,195},{4,52},{5,197},{6,54},{7,199},{8,56}... | collective-permute-start | bytes 589832 | tf_op jit(solution)/shard_map/sum_over_replicas/ppermute | solution.py:53
  36.8 2.2 %collective-permute-done.6 = bf16[2,192,256]{2,1,0:T(8,128)(2,1)S(1)} collective-permute-done((bf16[2,192,256]{2,1,0:T(8,128)(2,1)S(1)}, bf16[2,192,256]{2,1,0:T(8,128)(2,1)S(1)}, u32[]{:S(2)}, u32[]{:S(2)}) %collective-permute-start.6) | collective-permute-done | bytes 196640 | tf_op jit(solution)/shard_map/sum_over_replicas/ppermute | solution.py:53
  41.2 2.5 %collective-permute-done.7 = bf16[1,192,256]{2,1,0:T(8,128)(2,1)S(1)} collective-permute-done((bf16[1,192,256]{2,1,0:T(8,128)(2,1)S(1)}, bf16[1,192,256]{2,1,0:T(8,128)(2,1)S(1)}, u32[]{:S(2)}, u32[]{:S(2)}) %collective-permute-start.7) | collective-permute-done | bytes 98336 | tf_op jit(solution)/shard_map/sum_over_replicas/ppermute | solution.py:53
  44.8 2.0 %collective-permute-start.16 = (bf16[384,256]{1,0:T(8,128)(2,1)S(1)}, bf16[384,256]{1,0:T(8,128)(2,1)S(1)}, u32[]{:S(2)}, u32[]{:S(2)}) collective-permute-start(bf16[384,256]{1,0:T(8,128)(2,1)S(1)} %get-tuple-element.14.direction_ref), channel_id=1, source_target_pairs={{0,2},{1,15},{2,4},{3,1},{4,6},{5,3},{6,8},{7,5},{8,10},{9,7},{10,... | collective-permute-start | bytes 589832 | tf_op jit(solution)/shard_map/gram_over_columns/ppermute | solution.py:53
  48.2 6.2 %collective-permute-done.16 = bf16[384,256]{1,0:T(8,128)(2,1)S(1)} collective-permute-done((bf16[384,256]{1,0:T(8,128)(2,1)S(1)}, bf16[384,256]{1,0:T(8,128)(2,1)S(1)}, u32[]{:S(2)}, u32[]{:S(2)}) %collective-permute-start.16) | collective-permute-done | bytes 196640 | tf_op jit(solution)/shard_map/gram_over_columns/ppermute | solution.py:53
  54.7 6.6 %collective-permute-done.19 = bf16[384,256]{1,0:T(8,128)(2,1)S(1)} collective-permute-done((bf16[384,256]{1,0:T(8,128)(2,1)S(1)}, bf16[384,256]{1,0:T(8,128)(2,1)S(1)}, u32[]{:S(2)}, u32[]{:S(2)}) %collective-permute-start.19) | collective-permute-done | bytes 196640 | tf_op jit(solution)/shard_map/gram_over_columns/ppermute | solution.py:53
  61.6 1.8 %collective-permute-done.18 = bf16[384,256]{1,0:T(8,128)(2,1)S(1)} collective-permute-done((bf16[384,256]{1,0:T(8,128)(2,1)S(1)}, bf16[384,256]{1,0:T(8,128)(2,1)S(1)}, u32[]{:S(2)}, u32[]{:S(2)}) %collective-permute-start.18) | collective-permute-done | bytes 196640 | tf_op jit(solution)/shard_map/gram_over_columns/ppermute | solution.py:53
  63.7 4.5 %collective-permute-done.21 = bf16[384,256]{1,0:T(8,128)(2,1)S(1)} collective-permute-done((bf16[384,256]{1,0:T(8,128)(2,1)S(1)}, bf16[384,256]{1,0:T(8,128)(2,1)S(1)}, u32[]{:S(2)}, u32[]{:S(2)}) %collective-permute-start.21) | collective-permute-done | bytes 196640 | tf_op jit(solution)/shard_map/gram_over_columns/ppermute | solution.py:53
  68.5 1.8 %collective-permute-done.20 = bf16[384,256]{1,0:T(8,128)(2,1)S(1)} collective-permute-done((bf16[384,256]{1,0:T(8,128)(2,1)S(1)}, bf16[384,256]{1,0:T(8,128)(2,1)S(1)}, u32[]{:S(2)}, u32[]{:S(2)}) %collective-permute-start.20) | collective-permute-done | bytes 196640 | tf_op jit(solution)/shard_map/gram_over_columns/ppermute | solution.py:53
  70.6 4.5 %collective-permute-done.23 = bf16[384,256]{1,0:T(8,128)(2,1)S(1)} collective-permute-done((bf16[384,256]{1,0:T(8,128)(2,1)S(1)}, bf16[384,256]{1,0:T(8,128)(2,1)S(1)}, u32[]{:S(2)}, u32[]{:S(2)}) %collective-permute-start.23) | collective-permute-done | bytes 196640 | tf_op jit(solution)/shard_map/gram_over_columns/ppermute | solution.py:53
  75.3 1.8 %collective-permute-done.22 = bf16[384,256]{1,0:T(8,128)(2,1)S(1)} collective-permute-done((bf16[384,256]{1,0:T(8,128)(2,1)S(1)}, bf16[384,256]{1,0:T(8,128)(2,1)S(1)}, u32[]{:S(2)}, u32[]{:S(2)}) %collective-permute-start.22) | collective-permute-done | bytes 196640 | tf_op jit(solution)/shard_map/gram_over_columns/ppermute | solution.py:53
  78.7 2.2 %collective-permute-start.8 = (bf16[1,192,256]{2,1,0:T(8,128)(2,1)S(1)}, bf16[1,192,256]{2,1,0:T(8,128)(2,1)S(1)}, u32[]{:S(2)}, u32[]{:S(2)}) collective-permute-start(bf16[1,192,256]{2,1,0:T(8,128)(2,1)S(1)} %get-tuple-element.25), channel_id=1, source_target_pairs={{0,48},{1,193},{2,50},{3,195},{4,52},{5,197},{6,54},{7,199},{8,56}... | collective-permute-start | bytes 294920 | tf_op jit(solution)/shard_map/moment_gather/ppermute | solution.py:53
  82.3 3.2 %collective-permute-start.13 = (bf16[2,192,256]{2,1,0:T(8,128)(2,1)S(1)}, bf16[2,192,256]{2,1,0:T(8,128)(2,1)S(1)}, u32[]{:S(2)}, u32[]{:S(2)}) collective-permute-start(bf16[2,192,256]{2,1,0:T(8,128)(2,1)S(1)} %pad_maximum_fusion.9), channel_id=1, source_target_pairs={{0,48},{1,193},{2,50},{3,195},{4,52},{5,197},{6,54},{7,199},{8,56}... | collective-permute-start | bytes 589832 | tf_op jit(solution)/shard_map/moment_gather/ppermute | solution.py:53
  85.6 6.5 %newton_schulz.1 = (bf16[192,256]{1,0:T(8,128)(2,1)S(1)}, bf16[192,256]{1,0:T(8,128)(2,1)S(1)}) custom-call(f32[384,384]{1,0:T(8,128)S(1)} %fusion.mine_ref, f32[384,384]{1,0:T(8,128)S(1)} %collective-permute-done.24.other_ref, bf16[384,256]{1,0:T(8,128)(2,1)S(1)} %get-tuple-element.14.direction_ref), custom_call_target="tpu_custom_call" | custom-call | flops 3221225472 | bytes 2097152 | tf_op jit(solution)/shard_map/newton_schulz/pallas_call | solution.py:216
  92.1 2.1 %collective-permute-start.29 = (bf16[1,192,256]{2,1,0:T(8,128)(2,1)S(1)}, bf16[1,192,256]{2,1,0:T(8,128)(2,1)S(1)}, u32[]{:S(2)}, u32[]{:S(2)}) collective-permute-start(bf16[1,192,256]{2,1,0:T(8,128)(2,1)S(1)} %bitcast.39), channel_id=1, source_target_pairs={{0,16},{1,65},{2,18},{3,67},{4,20},{5,69},{6,22},{7,71},{8,24},{9,... | collective-permute-start | bytes 294920 | tf_op jit(solution)/shard_map/update_gather/ppermute | solution.py:53
  94.3 2.6 %collective-permute-start.14 = (bf16[4,192,256]{2,1,0:T(8,128)(2,1)S(1)}, bf16[4,192,256]{2,1,0:T(8,128)(2,1)S(1)}, u32[]{:S(2)}, u32[]{:S(2)}) collective-permute-start(bf16[4,192,256]{2,1,0:T(8,128)(2,1)S(1)} %pad_maximum_fusion.5), channel_id=1, source_target_pairs={{0,64},{1,17},{2,66},{3,19},{4,68},{5,21},{6,70},{7,23},{8,72},{9,... | collective-permute-start | bytes 1179656 | tf_op jit(solution)/shard_map/moment_gather/ppermute | solution.py:53
  98.1 2.1 %collective-permute-start.30 = (bf16[2,192,256]{2,1,0:T(8,128)(2,1)S(1)}, bf16[2,192,256]{2,1,0:T(8,128)(2,1)S(1)}, u32[]{:S(2)}, u32[]{:S(2)}) collective-permute-start(bf16[2,192,256]{2,1,0:T(8,128)(2,1)S(1)} %pad_maximum_fusion.11), channel_id=1, source_target_pairs={{0,48},{1,193},{2,50},{3,195},{4,52},{5,197},{6,54},{7,199},{8,56}... | collective-permute-start | bytes 589832 | tf_op jit(solution)/shard_map/update_gather/ppermute | solution.py:53
  100.2 2.5 %collective-permute-done.25 = bf16[1,192,256]{2,1,0:T(8,128)(2,1)S(1)} collective-permute-done((bf16[1,192,256]{2,1,0:T(8,128)(2,1)S(1)}, bf16[1,192,256]{2,1,0:T(8,128)(2,1)S(1)}, u32[]{:S(2)}, u32[]{:S(2)}) %collective-permute-start.25) | collective-permute-done | bytes 98336 | tf_op jit(solution)/shard_map/update_gather/ppermute | solution.py:53
  103.2 4.0 %collective-permute-done.30 = bf16[2,192,256]{2,1,0:T(8,128)(2,1)S(1)} collective-permute-done((bf16[2,192,256]{2,1,0:T(8,128)(2,1)S(1)}, bf16[2,192,256]{2,1,0:T(8,128)(2,1)S(1)}, u32[]{:S(2)}, u32[]{:S(2)}) %collective-permute-start.30) | collective-permute-done | bytes 196640 | tf_op jit(solution)/shard_map/update_gather/ppermute | solution.py:53
  107.2 2.5 %collective-permute-start.31 = (bf16[4,192,256]{2,1,0:T(8,128)(2,1)S(1)}, bf16[4,192,256]{2,1,0:T(8,128)(2,1)S(1)}, u32[]{:S(2)}, u32[]{:S(2)}) collective-permute-start(bf16[4,192,256]{2,1,0:T(8,128)(2,1)S(1)} %pad_maximum_fusion.7), channel_id=1, source_target_pairs={{0,64},{1,17},{2,66},{3,19},{4,68},{5,21},{6,70},{7,23},{8,72},{9,... | collective-permute-start | bytes 1179656 | tf_op jit(solution)/shard_map/update_gather/ppermute | solution.py:53
  110.9 2.1 %collective-permute-start.15 = (bf16[8,192,256]{2,1,0:T(8,128)(2,1)S(1)}, bf16[8,192,256]{2,1,0:T(8,128)(2,1)S(1)}, u32[]{:S(2)}, u32[]{:S(2)}) collective-permute-start(bf16[8,192,256]{2,1,0:T(8,128)(2,1)S(1)} %pad_maximum_fusion.1.refs_1_), channel_id=1, source_target_pairs={{0,192},{1,49},{2,194},{3,51},{4,196},{5,53},{6,198},{7,55},{8,200... | collective-permute-start | bytes 2359304 | tf_op jit(solution)/shard_map/moment_gather/ppermute | solution.py:53
  115.6 2.9 %collective-permute-done.27 = bf16[4,192,256]{2,1,0:T(8,128)(2,1)S(1)} collective-permute-done((bf16[4,192,256]{2,1,0:T(8,128)(2,1)S(1)}, bf16[4,192,256]{2,1,0:T(8,128)(2,1)S(1)}, u32[]{:S(2)}, u32[]{:S(2)}) %collective-permute-start.27) | collective-permute-done | bytes 393248 | tf_op jit(solution)/shard_map/update_gather/ppermute | solution.py:53
  119.9 1.8 %assemble.4.refs_2_ = bf16[16,384,256]{2,1,0:T(8,128)(2,1)} custom-call(s32[16]{0:T(128)S(1)} %get-tuple-element.26.place_ref, bf16[8,192,256]{2,1,0:T(8,128)(2,1)S(1)} %pad_maximum_fusion.refs_0_, bf16[8,192,256]{2,1,0:T(8,128)(2,1)S(1)} %pad_maximum_fusion.1.refs_1_), custom_call_target="tpu_custom_call" | custom-call | bytes 3145728 | tf_op jit(solution)/shard_map/moment_gather/assemble/pallas_call | solution.py:149
  121.7 5.2 %collective-permute-done.15.refs_1_ = bf16[8,192,256]{2,1,0:T(8,128)(2,1)S(1)} collective-permute-done((bf16[8,192,256]{2,1,0:T(8,128)(2,1)S(1)}, bf16[8,192,256]{2,1,0:T(8,128)(2,1)S(1)}, u32[]{:S(2)}, u32[]{:S(2)}) %collective-permute-start.15) | collective-permute-done | bytes 786464 | tf_op jit(solution)/shard_map/moment_gather/ppermute | solution.py:53
  128.8 1.8 %assemble.6.refs_2_ = bf16[16,384,256]{2,1,0:T(8,128)(2,1)} custom-call(s32[16]{0:T(128)S(1)} %get-tuple-element.26.place_ref, bf16[8,192,256]{2,1,0:T(8,128)(2,1)S(1)} %pad_maximum_fusion.2.refs_0_, bf16[8,192,256]{2,1,0:T(8,128)(2,1)S(1)} %pad_maximum_fusion.3.refs_1_), custom_call_target="tpu_custom_call" | custom-call | bytes 3145728 | tf_op jit(solution)/shard_map/update_gather/assemble/pallas_call | solution.py:149
  130.6 4.8 %collective-permute-done.32.refs_1_ = bf16[8,192,256]{2,1,0:T(8,128)(2,1)S(1)} collective-permute-done((bf16[8,192,256]{2,1,0:T(8,128)(2,1)S(1)}, bf16[8,192,256]{2,1,0:T(8,128)(2,1)S(1)}, u32[]{:S(2)}, u32[]{:S(2)}) %collective-permute-start.32) | collective-permute-done | bytes 786464 | tf_op jit(solution)/shard_map/update_gather/ppermute | solution.py:53
  (89 shorter events, 32.6 us)
Async XLA Ops:
  6.4 12.6 %collective-permute-start = (bf16[8,192,256]{2,1,0:T(8,128)(2,1)}, bf16[8,192,256]{2,1,0:T(8,128)(2,1)}, u32[]{:S(2)}, u32[]{:S(2)}) collective-permute-start(bf16[8,192,256]{2,1,0:T(8,128)(2,1)} %get-tuple-element.9), channel_id=1, source_target_pairs={{0,64},{1,17},{2,66},{3,19},{4,68},{5,21},{6,70},{7,23},{8,72},{9,... | collective-permute-start | bytes 2359304 | tf_op jit(solution)/shard_map/sum_over_replicas/ppermute | solution.py:53
  8.7 12.9 %collective-permute-start.4 = (bf16[8,192,256]{2,1,0:T(8,128)(2,1)}, bf16[8,192,256]{2,1,0:T(8,128)(2,1)}, u32[]{:S(2)}, u32[]{:S(2)}) collective-permute-start(bf16[8,192,256]{2,1,0:T(8,128)(2,1)} %get-tuple-element.11), channel_id=1, source_target_pairs={{0,192},{1,49},{2,194},{3,51},{4,196},{5,53},{6,198},{7,55},{8,200... | collective-permute-start | bytes 2359304 | tf_op jit(solution)/shard_map/sum_over_replicas/ppermute | solution.py:53
  20.2 7.9 %collective-permute-start.1 = (bf16[4,192,256]{2,1,0:T(8,128)(2,1)S(1)}, bf16[4,192,256]{2,1,0:T(8,128)(2,1)S(1)}, u32[]{:S(2)}, u32[]{:S(2)}) collective-permute-start(bf16[4,192,256]{2,1,0:T(8,128)(2,1)S(1)} %get-tuple-element.16), channel_id=1, source_target_pairs={{0,192},{1,49},{2,194},{3,51},{4,196},{5,53},{6,198},{7,55},{8,200... | collective-permute-start | bytes 1179656 | tf_op jit(solution)/shard_map/sum_over_replicas/ppermute | solution.py:53
  22.9 9.1 %collective-permute-start.5 = (bf16[4,192,256]{2,1,0:T(8,128)(2,1)S(1)}, bf16[4,192,256]{2,1,0:T(8,128)(2,1)S(1)}, u32[]{:S(2)}, u32[]{:S(2)}) collective-permute-start(bf16[4,192,256]{2,1,0:T(8,128)(2,1)S(1)} %get-tuple-element.18), channel_id=1, source_target_pairs={{0,64},{1,17},{2,66},{3,19},{4,68},{5,21},{6,70},{7,23},{8,72},{9,... | collective-permute-start | bytes 1179656 | tf_op jit(solution)/shard_map/sum_over_replicas/ppermute | solution.py:53
  28.2 7.0 %collective-permute-start.2 = (bf16[2,192,256]{2,1,0:T(8,128)(2,1)S(1)}, bf16[2,192,256]{2,1,0:T(8,128)(2,1)S(1)}, u32[]{:S(2)}, u32[]{:S(2)}) collective-permute-start(bf16[2,192,256]{2,1,0:T(8,128)(2,1)S(1)} %get-tuple-element.20), channel_id=1, source_target_pairs={{0,16},{1,65},{2,18},{3,67},{4,20},{5,69},{6,22},{7,71},{8,24},{9,... | collective-permute-start | bytes 589832 | tf_op jit(solution)/shard_map/sum_over_replicas/ppermute | solution.py:53
  32.1 7.0 %collective-permute-start.6 = (bf16[2,192,256]{2,1,0:T(8,128)(2,1)S(1)}, bf16[2,192,256]{2,1,0:T(8,128)(2,1)S(1)}, u32[]{:S(2)}, u32[]{:S(2)}) collective-permute-start(bf16[2,192,256]{2,1,0:T(8,128)(2,1)S(1)} %get-tuple-element.22), channel_id=1, source_target_pairs={{0,48},{1,193},{2,50},{3,195},{4,52},{5,197},{6,54},{7,199},{8,56}... | collective-permute-start | bytes 589832 | tf_op jit(solution)/shard_map/sum_over_replicas/ppermute | solution.py:53
  35.3 5.9 %collective-permute-start.3 = (bf16[1,192,256]{2,1,0:T(8,128)(2,1)S(1)}, bf16[1,192,256]{2,1,0:T(8,128)(2,1)S(1)}, u32[]{:S(2)}, u32[]{:S(2)}) collective-permute-start(bf16[1,192,256]{2,1,0:T(8,128)(2,1)S(1)} %fusion.11), channel_id=1, source_target_pairs={{0,48},{1,193},{2,50},{3,195},{4,52},{5,197},{6,54},{7,199},{8,56}... | collective-permute-start | bytes 294920 | tf_op jit(solution)/shard_map/sum_over_replicas/ppermute | solution.py:53
  44.8 9.6 %collective-permute-start.16 = (bf16[384,256]{1,0:T(8,128)(2,1)S(1)}, bf16[384,256]{1,0:T(8,128)(2,1)S(1)}, u32[]{:S(2)}, u32[]{:S(2)}) collective-permute-start(bf16[384,256]{1,0:T(8,128)(2,1)S(1)} %get-tuple-element.14.direction_ref), channel_id=1, source_target_pairs={{0,2},{1,15},{2,4},{3,1},{4,6},{5,3},{6,8},{7,5},{8,10},{9,7},{10,... | collective-permute-start | bytes 589832 | tf_op jit(solution)/shard_map/gram_over_columns/ppermute | solution.py:53
  46.8 7.6 %collective-permute-start.17 = (bf16[384,256]{1,0:T(8,128)(2,1)S(1)}, bf16[384,256]{1,0:T(8,128)(2,1)S(1)}, u32[]{:S(2)}, u32[]{:S(2)}) collective-permute-start(bf16[384,256]{1,0:T(8,128)(2,1)S(1)} %get-tuple-element.14.direction_ref), channel_id=1, source_target_pairs={{0,1},{1,0},{2,3},{3,2},{4,5},{5,4},{6,7},{7,6},{8,9},{9,8},{10,11... | collective-permute-start | bytes 589832 | tf_op jit(solution)/shard_map/gram_over_columns/ppermute | solution.py:53
  54.4 6.9 %collective-permute-start.19 = (bf16[384,256]{1,0:T(8,128)(2,1)S(1)}, bf16[384,256]{1,0:T(8,128)(2,1)S(1)}, u32[]{:S(2)}, u32[]{:S(2)}) collective-permute-start(bf16[384,256]{1,0:T(8,128)(2,1)S(1)} %collective-permute-done.16), channel_id=1, source_target_pairs={{0,2},{1,15},{2,4},{3,1},{4,6},{5,3},{6,8},{7,5},{8,10},{9,7},{10,... | collective-permute-start | bytes 589832 | tf_op jit(solution)/shard_map/gram_over_columns/ppermute | solution.py:53
  54.4 9.0 %collective-permute-start.18 = (bf16[384,256]{1,0:T(8,128)(2,1)S(1)}, bf16[384,256]{1,0:T(8,128)(2,1)S(1)}, u32[]{:S(2)}, u32[]{:S(2)}) collective-permute-start(bf16[384,256]{1,0:T(8,128)(2,1)S(1)} %collective-permute-done.17), channel_id=1, source_target_pairs={{0,2},{1,15},{2,4},{3,1},{4,6},{5,3},{6,8},{7,5},{8,10},{9,7},{10,... | collective-permute-start | bytes 589832 | tf_op jit(solution)/shard_map/gram_over_columns/ppermute | solution.py:53
  61.3 6.9 %collective-permute-start.21 = (bf16[384,256]{1,0:T(8,128)(2,1)S(1)}, bf16[384,256]{1,0:T(8,128)(2,1)S(1)}, u32[]{:S(2)}, u32[]{:S(2)}) collective-permute-start(bf16[384,256]{1,0:T(8,128)(2,1)S(1)} %collective-permute-done.19), channel_id=1, source_target_pairs={{0,2},{1,15},{2,4},{3,1},{4,6},{5,3},{6,8},{7,5},{8,10},{9,7},{10,... | collective-permute-start | bytes 589832 | tf_op jit(solution)/shard_map/gram_over_columns/ppermute | solution.py:53
  63.4 6.9 %collective-permute-start.20 = (bf16[384,256]{1,0:T(8,128)(2,1)S(1)}, bf16[384,256]{1,0:T(8,128)(2,1)S(1)}, u32[]{:S(2)}, u32[]{:S(2)}) collective-permute-start(bf16[384,256]{1,0:T(8,128)(2,1)S(1)} %collective-permute-done.18), channel_id=1, source_target_pairs={{0,2},{1,15},{2,4},{3,1},{4,6},{5,3},{6,8},{7,5},{8,10},{9,7},{10,... | collective-permute-start | bytes 589832 | tf_op jit(solution)/shard_map/gram_over_columns/ppermute | solution.py:53
  68.2 6.9 %collective-permute-start.23 = (bf16[384,256]{1,0:T(8,128)(2,1)S(1)}, bf16[384,256]{1,0:T(8,128)(2,1)S(1)}, u32[]{:S(2)}, u32[]{:S(2)}) collective-permute-start(bf16[384,256]{1,0:T(8,128)(2,1)S(1)} %collective-permute-done.21), channel_id=1, source_target_pairs={{0,2},{1,15},{2,4},{3,1},{4,6},{5,3},{6,8},{7,5},{8,10},{9,7},{10,... | collective-permute-start | bytes 589832 | tf_op jit(solution)/shard_map/gram_over_columns/ppermute | solution.py:53
  70.3 6.9 %collective-permute-start.22 = (bf16[384,256]{1,0:T(8,128)(2,1)S(1)}, bf16[384,256]{1,0:T(8,128)(2,1)S(1)}, u32[]{:S(2)}, u32[]{:S(2)}) collective-permute-start(bf16[384,256]{1,0:T(8,128)(2,1)S(1)} %collective-permute-done.20), channel_id=1, source_target_pairs={{0,2},{1,15},{2,4},{3,1},{4,6},{5,3},{6,8},{7,5},{8,10},{9,7},{10,... | collective-permute-start | bytes 589832 | tf_op jit(solution)/shard_map/gram_over_columns/ppermute | solution.py:53
  77.5 8.1 %collective-permute-start.24 = (f32[384,384]{1,0:T(8,128)S(1)}, f32[384,384]{1,0:T(8,128)S(1)}, u32[]{:S(2)}, u32[]{:S(2)}) collective-permute-start(f32[384,384]{1,0:T(8,128)S(1)} %fusion.mine_ref), channel_id=1, source_target_pairs={{0,1},{1,0},{2,3},{3,2},{4,5},{5,4},{6,7},{7,6},{8,9},{9,8},{10,11... | collective-permute-start | bytes 1769480 | tf_op jit(solution)/shard_map/gram_over_columns/ppermute | solution.py:53
  77.6 4.7 %collective-permute-start.12 = (bf16[1,192,256]{2,1,0:T(8,128)(2,1)S(1)}, bf16[1,192,256]{2,1,0:T(8,128)(2,1)S(1)}, u32[]{:S(2)}, u32[]{:S(2)}) collective-permute-start(bf16[1,192,256]{2,1,0:T(8,128)(2,1)S(1)} %get-tuple-element.24), channel_id=1, source_target_pairs={{0,16},{1,65},{2,18},{3,67},{4,20},{5,69},{6,22},{7,71},{8,24},{9,... | collective-permute-start | bytes 294920 | tf_op jit(solution)/shard_map/moment_gather/ppermute | solution.py:53
  78.7 6.8 %collective-permute-start.8 = (bf16[1,192,256]{2,1,0:T(8,128)(2,1)S(1)}, bf16[1,192,256]{2,1,0:T(8,128)(2,1)S(1)}, u32[]{:S(2)}, u32[]{:S(2)}) collective-permute-start(bf16[1,192,256]{2,1,0:T(8,128)(2,1)S(1)} %get-tuple-element.25), channel_id=1, source_target_pairs={{0,48},{1,193},{2,50},{3,195},{4,52},{5,197},{6,54},{7,199},{8,56}... | collective-permute-start | bytes 294920 | tf_op jit(solution)/shard_map/moment_gather/ppermute | solution.py:53
  82.3 11.9 %collective-permute-start.13 = (bf16[2,192,256]{2,1,0:T(8,128)(2,1)S(1)}, bf16[2,192,256]{2,1,0:T(8,128)(2,1)S(1)}, u32[]{:S(2)}, u32[]{:S(2)}) collective-permute-start(bf16[2,192,256]{2,1,0:T(8,128)(2,1)S(1)} %pad_maximum_fusion.9), channel_id=1, source_target_pairs={{0,48},{1,193},{2,50},{3,195},{4,52},{5,197},{6,54},{7,199},{8,56}... | collective-permute-start | bytes 589832 | tf_op jit(solution)/shard_map/moment_gather/ppermute | solution.py:53
  85.5 17.3 %collective-permute-start.9 = (bf16[2,192,256]{2,1,0:T(8,128)(2,1)S(1)}, bf16[2,192,256]{2,1,0:T(8,128)(2,1)S(1)}, u32[]{:S(2)}, u32[]{:S(2)}) collective-permute-start(bf16[2,192,256]{2,1,0:T(8,128)(2,1)S(1)} %pad_maximum_fusion.8), channel_id=1, source_target_pairs={{0,16},{1,65},{2,18},{3,67},{4,20},{5,69},{6,22},{7,71},{8,24},{9,... | collective-permute-start | bytes 589832 | tf_op jit(solution)/shard_map/moment_gather/ppermute | solution.py:53
  92.1 5.9 %collective-permute-start.29 = (bf16[1,192,256]{2,1,0:T(8,128)(2,1)S(1)}, bf16[1,192,256]{2,1,0:T(8,128)(2,1)S(1)}, u32[]{:S(2)}, u32[]{:S(2)}) collective-permute-start(bf16[1,192,256]{2,1,0:T(8,128)(2,1)S(1)} %bitcast.39), channel_id=1, source_target_pairs={{0,16},{1,65},{2,18},{3,67},{4,20},{5,69},{6,22},{7,71},{8,24},{9,... | collective-permute-start | bytes 294920 | tf_op jit(solution)/shard_map/update_gather/ppermute | solution.py:53
  94.3 16.5 %collective-permute-start.14 = (bf16[4,192,256]{2,1,0:T(8,128)(2,1)S(1)}, bf16[4,192,256]{2,1,0:T(8,128)(2,1)S(1)}, u32[]{:S(2)}, u32[]{:S(2)}) collective-permute-start(bf16[4,192,256]{2,1,0:T(8,128)(2,1)S(1)} %pad_maximum_fusion.5), channel_id=1, source_target_pairs={{0,64},{1,17},{2,66},{3,19},{4,68},{5,21},{6,70},{7,23},{8,72},{9,... | collective-permute-start | bytes 1179656 | tf_op jit(solution)/shard_map/moment_gather/ppermute | solution.py:53
  96.8 5.8 %collective-permute-start.25 = (bf16[1,192,256]{2,1,0:T(8,128)(2,1)S(1)}, bf16[1,192,256]{2,1,0:T(8,128)(2,1)S(1)}, u32[]{:S(2)}, u32[]{:S(2)}) collective-permute-start(bf16[1,192,256]{2,1,0:T(8,128)(2,1)S(1)} %bitcast.35), channel_id=1, source_target_pairs={{0,48},{1,193},{2,50},{3,195},{4,52},{5,197},{6,54},{7,199},{8,56}... | collective-permute-start | bytes 294920 | tf_op jit(solution)/shard_map/update_gather/ppermute | solution.py:53
  98.1 9.1 %collective-permute-start.30 = (bf16[2,192,256]{2,1,0:T(8,128)(2,1)S(1)}, bf16[2,192,256]{2,1,0:T(8,128)(2,1)S(1)}, u32[]{:S(2)}, u32[]{:S(2)}) collective-permute-start(bf16[2,192,256]{2,1,0:T(8,128)(2,1)S(1)} %pad_maximum_fusion.11), channel_id=1, source_target_pairs={{0,48},{1,193},{2,50},{3,195},{4,52},{5,197},{6,54},{7,199},{8,56}... | collective-permute-start | bytes 589832 | tf_op jit(solution)/shard_map/update_gather/ppermute | solution.py:53
  102.7 7.9 %collective-permute-start.26 = (bf16[2,192,256]{2,1,0:T(8,128)(2,1)S(1)}, bf16[2,192,256]{2,1,0:T(8,128)(2,1)S(1)}, u32[]{:S(2)}, u32[]{:S(2)}) collective-permute-start(bf16[2,192,256]{2,1,0:T(8,128)(2,1)S(1)} %pad_maximum_fusion.10), channel_id=1, source_target_pairs={{0,16},{1,65},{2,18},{3,67},{4,20},{5,69},{6,22},{7,71},{8,24},{9,... | collective-permute-start | bytes 589832 | tf_op jit(solution)/shard_map/update_gather/ppermute | solution.py:53
  102.8 10.1 %collective-permute-start.10 = (bf16[4,192,256]{2,1,0:T(8,128)(2,1)S(1)}, bf16[4,192,256]{2,1,0:T(8,128)(2,1)S(1)}, u32[]{:S(2)}, u32[]{:S(2)}) collective-permute-start(bf16[4,192,256]{2,1,0:T(8,128)(2,1)S(1)} %pad_maximum_fusion.4), channel_id=1, source_target_pairs={{0,192},{1,49},{2,194},{3,51},{4,196},{5,53},{6,198},{7,55},{8,200... | collective-permute-start | bytes 1179656 | tf_op jit(solution)/shard_map/moment_gather/ppermute | solution.py:53
  107.2 8.3 %collective-permute-start.31 = (bf16[4,192,256]{2,1,0:T(8,128)(2,1)S(1)}, bf16[4,192,256]{2,1,0:T(8,128)(2,1)S(1)}, u32[]{:S(2)}, u32[]{:S(2)}) collective-permute-start(bf16[4,192,256]{2,1,0:T(8,128)(2,1)S(1)} %pad_maximum_fusion.7), channel_id=1, source_target_pairs={{0,64},{1,17},{2,66},{3,19},{4,68},{5,21},{6,70},{7,23},{8,72},{9,... | collective-permute-start | bytes 1179656 | tf_op jit(solution)/shard_map/update_gather/ppermute | solution.py:53
  110.7 7.9 %collective-permute-start.27 = (bf16[4,192,256]{2,1,0:T(8,128)(2,1)S(1)}, bf16[4,192,256]{2,1,0:T(8,128)(2,1)S(1)}, u32[]{:S(2)}, u32[]{:S(2)}) collective-permute-start(bf16[4,192,256]{2,1,0:T(8,128)(2,1)S(1)} %pad_maximum_fusion.6), channel_id=1, source_target_pairs={{0,192},{1,49},{2,194},{3,51},{4,196},{5,53},{6,198},{7,55},{8,200... | collective-permute-start | bytes 1179656 | tf_op jit(solution)/shard_map/update_gather/ppermute | solution.py:53
  110.9 16.1 %collective-permute-start.15 = (bf16[8,192,256]{2,1,0:T(8,128)(2,1)S(1)}, bf16[8,192,256]{2,1,0:T(8,128)(2,1)S(1)}, u32[]{:S(2)}, u32[]{:S(2)}) collective-permute-start(bf16[8,192,256]{2,1,0:T(8,128)(2,1)S(1)} %pad_maximum_fusion.1.refs_1_), channel_id=1, source_target_pairs={{0,192},{1,49},{2,194},{3,51},{4,196},{5,53},{6,198},{7,55},{8,200... | collective-permute-start | bytes 2359304 | tf_op jit(solution)/shard_map/moment_gather/ppermute | solution.py:53
  113.0 13.9 %collective-permute-start.11 = (bf16[8,192,256]{2,1,0:T(8,128)(2,1)S(1)}, bf16[8,192,256]{2,1,0:T(8,128)(2,1)S(1)}, u32[]{:S(2)}, u32[]{:S(2)}) collective-permute-start(bf16[8,192,256]{2,1,0:T(8,128)(2,1)S(1)} %pad_maximum_fusion.refs_0_), channel_id=1, source_target_pairs={{0,64},{1,17},{2,66},{3,19},{4,68},{5,21},{6,70},{7,23},{8,72},{9,... | collective-permute-start | bytes 2359304 | tf_op jit(solution)/shard_map/moment_gather/ppermute | solution.py:53
  115.5 19.9 %collective-permute-start.32 = (bf16[8,192,256]{2,1,0:T(8,128)(2,1)S(1)}, bf16[8,192,256]{2,1,0:T(8,128)(2,1)S(1)}, u32[]{:S(2)}, u32[]{:S(2)}) collective-permute-start(bf16[8,192,256]{2,1,0:T(8,128)(2,1)S(1)} %pad_maximum_fusion.3.refs_1_), channel_id=1, source_target_pairs={{0,192},{1,49},{2,194},{3,51},{4,196},{5,53},{6,198},{7,55},{8,200... | collective-permute-start | bytes 2359304 | tf_op jit(solution)/shard_map/update_gather/ppermute | solution.py:53
  118.6 16.8 %collective-permute-start.28 = (bf16[8,192,256]{2,1,0:T(8,128)(2,1)S(1)}, bf16[8,192,256]{2,1,0:T(8,128)(2,1)S(1)}, u32[]{:S(2)}, u32[]{:S(2)}) collective-permute-start(bf16[8,192,256]{2,1,0:T(8,128)(2,1)S(1)} %pad_maximum_fusion.2.refs_0_), channel_id=1, source_target_pairs={{0,64},{1,17},{2,66},{3,19},{4,68},{5,21},{6,70},{7,23},{8,72},{9,... | collective-permute-start | bytes 2359304 | tf_op jit(solution)/shard_map/update_gather/ppermute | solution.py:53
  (6 other events, 30.2 us)

commit v3 on v2

v3 whole, which is shorter than its diff:
```python
import functools
import math

import jax
import jax.numpy as jnp
from jax import lax
from jax.experimental import pallas as pl
from jax.experimental.pallas import tpu as pltpu
from jax.sharding import PartitionSpec as P

D = 4096
ROWS = 384
ITERS = 5

momentum_decay = 0.95
coef_first = 3.4445
coef_second = -4.775
coef_third = 2.0315
rms_factor = 0.2
tiny_value = 1e-07

BF16 = jnp.bfloat16
F32 = jnp.float32
SIDE = 4
HALF = ROWS // 2


def gray(position):
    return position ^ (position >> 1)


def all_pairs(mesh_sizes, target):
    replicas, owners = mesh_sizes
    pairs = []
    for dp in range(replicas):
        for zero in range(owners):
            x, y, z, core = target(dp // SIDE, dp % SIDE, zero // 2, zero % 2)
            pairs.append((dp * owners + zero, (x * SIDE + y) * owners + z * 2 + core))
    return pairs


def cube_pairs(mesh_sizes, *dims):
    flip = 0
    for dim in dims:
        flip ^= (1, 3)[dim % 2]

    def target(x, y, z, core):
        along_x = (dims[0] < 2) == (core == 0)
        return (x ^ flip, y, z, core) if along_x else (x, y ^ flip, z, core)

    return all_pairs(mesh_sizes, target)


def send(value, pairs):
    return lax.ppermute(value, ("dp", "zero"), pairs)


HEADS = ((0, 1), (1, 0))
TAIL = ((), (3,), (2,), (2, 3))


def cube_place(dp, core):
    x, y = gray(dp // SIDE), gray(dp % SIDE)
    return jnp.where(core == 0, x | (y << 2), y | (x << 2))


def cube_device(bits, core):
    first, second = gray(bits & 3), gray(bits >> 2)
    return jnp.where(core == 0, first * SIDE + second, second * SIDE + first)


def vmem(count):
    return [pl.BlockSpec(memory_space=pltpu.VMEM)] * count


def anywhere(count):
    return [pl.BlockSpec(memory_space=pl.ANY)] * count


def places_of(*dims):
    base = sum(1 << dim for dim in dims)
    return [base + sum(1 << dim for dim in tail) for tail in TAIL]


def kernel_device(relative):
    core = lax.rem(lax.axis_index("zero"), 2)
    return cube_device(cube_place(lax.axis_index("dp"), core) ^ relative, core)


def pack_kernel(places, slot_ref, gradients_ref, *out_refs):
    for part, (out_ref, own_places) in enumerate(zip(out_refs, places)):
        for i, place in enumerate(own_places):
            slot = slot_ref[kernel_device(place)]
            out_ref[i] = gradients_ref[slot, part * HALF : (part + 1) * HALF]


def pack(bucket_slot, gradients, places):
    width = gradients.shape[-1]
    count = sum(len(p) for p in places)
    return pl.pallas_call(
        functools.partial(pack_kernel, places),
        out_shape=[jax.ShapeDtypeStruct((len(p), HALF, width), BF16) for p in places],
        in_specs=[pl.BlockSpec(memory_space=pltpu.SMEM)] + vmem(1),
        out_specs=vmem(2),
        compiler_params=pltpu.CompilerParams(vmem_limit_bytes=16 * 1024 * 1024),
        cost_estimate=pl.CostEstimate(
            flops=0, bytes_accessed=2 * count * HALF * width * 2, transcendentals=0
        ),
        name="pack",
    )(bucket_slot, gradients)


def reduce_scatter(gradients, bucket_slot, sizes):
    away = [places_of(first) + places_of(first, second) for first, second in HEADS]
    kept = [places_of() + places_of(second) for _, second in HEADS]
    received = [
        send(v, cube_pairs(sizes, first))
        for v, (first, _) in zip(pack(bucket_slot, gradients, away), HEADS)
    ]
    kept = pack(bucket_slot, gradients, kept)
    sent = [(m[4:].astype(F32) + o[4:].astype(F32)).astype(BF16) for m, o in zip(kept, received)]
    kept = [m[:4].astype(F32) + o[:4].astype(F32) for m, o in zip(kept, received)]
    received = [send(v, cube_pairs(sizes, second)) for v, (_, second) in zip(sent, HEADS)]
    total = jnp.concatenate([m[0] + o[0].astype(F32) for m, o in zip(kept, received)])
    for i in range(1, 4):
        block = [(m[i] + o[i].astype(F32)).astype(BF16) for m, o in zip(kept, received)]
        total = total + send(jnp.concatenate(block), cube_pairs(sizes, *TAIL[i])).astype(F32)
    return total


def assemble_kernel(places, *refs):
    out_ref, sems = refs[-2], refs[-1]
    copies = []
    for ref, (part, own_places) in zip(refs, places):
        for i, place in enumerate(own_places):
            copies.append(
                pltpu.make_async_copy(
                    ref.at[i],
                    out_ref.at[kernel_device(place), pl.ds(part * HALF, HALF)],
                    sems.at[len(copies)],
                )
            )
            copies[-1].start()
    for copy in copies:
        copy.wait()


def assemble(pieces, places, onto=None, before=()):
    width = pieces[0].shape[-1]
    extra = ([] if onto is None else [onto]) + list(before)
    count = sum(len(p) for _, p in places)
    return pl.pallas_call(
        functools.partial(assemble_kernel, places),
        out_shape=jax.ShapeDtypeStruct((16, ROWS, width), BF16),
        in_specs=vmem(len(pieces)) + anywhere(len(extra)),
        out_specs=anywhere(1)[0],
        scratch_shapes=[pltpu.SemaphoreType.DMA((count,))],
        input_output_aliases={} if onto is None else {len(pieces): 0},
        compiler_params=pltpu.CompilerParams(vmem_limit_bytes=16 * 1024 * 1024),
        cost_estimate=pl.CostEstimate(
            flops=0, bytes_accessed=2 * count * HALF * width * 2, transcendentals=0
        ),
        name="assemble",
    )(*pieces, *extra)


def join_kernel(*refs):
    for part, out_ref in enumerate(refs[-2:]):
        for i in range(4):
            out_ref[i] = refs[i][part * HALF : (part + 1) * HALF]


def join(pieces, before):
    half = jax.ShapeDtypeStruct((4, HALF, pieces[0].shape[-1]), BF16)
    return pl.pallas_call(
        join_kernel,
        out_shape=[half, half],
        in_specs=vmem(4) + anywhere(len(before)),
        out_specs=vmem(2),
        compiler_params=pltpu.CompilerParams(vmem_limit_bytes=16 * 1024 * 1024),
        cost_estimate=pl.CostEstimate(flops=0, bytes_accessed=2 << 20, transcendentals=0),
        name="join",
    )(*pieces, *before)


def all_gather(value, sizes, before=()):
    pieces = [value] + [send(value, cube_pairs(sizes, *TAIL[i])) for i in range(1, 4)]
    four = join(pieces, before)
    side = [send(v, cube_pairs(sizes, second)) for v, (_, second) in zip(four, HEADS)]
    eight = [jnp.concatenate([m, o]) for m, o in zip(four, side)]
    received = [send(v, cube_pairs(sizes, first)) for v, (first, _) in zip(eight, HEADS)]
    return four, eight, received


def in_order(held, received, before=()):
    near = [(part, places_of() + places_of(second)) for part, (_, second) in enumerate(HEADS)]
    far = [
        (part, places_of(first) + places_of(first, second))
        for part, (first, second) in enumerate(HEADS)
    ]
    return assemble(received, far, assemble(held, near), before)


def split(value):
    high = value.astype(BF16)
    return high, (value - high.astype(F32)).astype(BF16)


def dot(a, b):
    return jnp.dot(a, b, preferred_element_type=F32)


def newton_schulz_kernel(mine_ref, other_ref, direction_ref, out_ref):
    gram = mine_ref[...] + other_ref[...]
    row = lax.broadcasted_iota(jnp.int32, gram.shape, 0)
    column = lax.broadcasted_iota(jnp.int32, gram.shape, 1)
    total = jnp.sum(jnp.where(row == column, gram, 0.0))
    scale = 1.0 / (jnp.sqrt(jnp.full((1, 1), total, F32)) + tiny_value)
    gram = gram * scale * scale
    iterate = direction_ref[...].astype(F32)
    for repeat in range(ITERS):
        high, low = split(gram)
        polynomial = (coef_second * high.astype(F32) + coef_third * dot(high, high)).astype(BF16)
        x_high, x_low = split(iterate)
        product = dot(polynomial, x_high)
        if repeat:
            product += dot(polynomial, x_low)
        iterate = coef_first * iterate + product
        if repeat < ITERS - 1:
            left = coef_first * gram + (dot(polynomial, high) + dot(polynomial, low))
            high, low = split(left)
            gram = coef_first * left + (dot(high, polynomial) + dot(low, polynomial))
    factor = rms_factor * math.sqrt(max(ROWS, D))
    out_ref[...] = (iterate * (factor * scale)).astype(BF16)


def newton_schulz(mine, other, direction):
    return pl.pallas_call(
        newton_schulz_kernel,
        out_shape=jax.ShapeDtypeStruct(direction.shape, BF16),
        in_specs=vmem(3),
        out_specs=vmem(1)[0],
        compiler_params=pltpu.CompilerParams(vmem_limit_bytes=32 * 1024 * 1024),
        cost_estimate=pl.CostEstimate(flops=7 << 30, bytes_accessed=2 << 20, transcendentals=0),
        name="newton_schulz",
    )(mine, other, direction)


def gram_kernel(added, *refs):
    total = None
    for ref in refs[:added]:
        block = ref[...]
        term = lax.dot_general(
            block, block, (((1,), (1,)), ((), ())), preferred_element_type=F32
        )
        total = term if total is None else total + term
    if added < len(refs) - 1 and refs[added].dtype == F32:
        total += refs[added][...]
    refs[-1][...] = total


def gram_of(columns, gram=None, before=()):
    extra = [] if gram is None else [gram]
    return pl.pallas_call(
        functools.partial(gram_kernel, len(columns)),
        out_shape=jax.ShapeDtypeStruct((ROWS, ROWS), F32),
        in_specs=vmem(len(columns) + len(extra)) + anywhere(len(before)),
        out_specs=vmem(1)[0],
        compiler_params=pltpu.CompilerParams(vmem_limit_bytes=16 * 1024 * 1024),
        cost_estimate=pl.CostEstimate(
            flops=len(columns) << 28, bytes_accessed=2 << 20, transcendentals=0
        ),
        name="gram",
    )(*columns, *extra, *before)


def per_device(sizes, gradients, momentum, bucket_slot):
    dp = lax.axis_index("dp")
    replicas, owners = sizes
    chips = owners // 2
    with jax.named_scope("sum_over_replicas"):
        total = reduce_scatter(gradients[0], bucket_slot, sizes)
    average = total / replicas
    own = lax.dynamic_index_in_dim(momentum, dp, 0, keepdims=False).astype(F32)
    moment = (momentum_decay * own + average).astype(BF16)
    direction = (average + momentum_decay * moment.astype(F32)).astype(BF16)
    swap = all_pairs(sizes, lambda x, y, z, c: (x, y, z, 1 - c))
    ring, skip = [
        all_pairs(sizes, lambda x, y, z, c, hops=hops: (x, y, (z + hops * (1 - 2 * c)) % chips, c))
        for hops in (1, 2)
    ]
    with jax.named_scope("moment_gather"):
        four, eight, rest = all_gather(moment, sizes)
    with jax.named_scope("gram_over_columns"):
        same, cross = send(direction, ring), send(send(direction, swap), ring)
        gram = gram_of([direction])
        gram = gram_of([same, cross], gram)
        same, cross = send(same, ring), send(cross, ring)
        gram = gram_of([same, cross], gram, four)
        same, cross, opposite = send(same, ring), send(cross, ring), send(same, skip)
        gram = gram_of([same, cross, opposite], gram, eight)
        other = send(gram, swap)
    update = newton_schulz(gram, other, direction)
    with jax.named_scope("update_gather"):
        _, *updates = all_gather(update, sizes, rest)
    new_moment = in_order(eight, rest)
    update = in_order(*updates, [new_moment])
    return (new_moment, update)


def solution(mesh):
    sizes = (mesh.shape["dp"], mesh.shape["zero"])
    return jax.shard_map(
        functools.partial(per_device, sizes),
        mesh=mesh,
        in_specs=(P("dp", None, None, "zero"), P(None, None, "zero"), P()),
        out_specs=(P(None, None, "zero"), P(None, None, "zero")),
        check_vma=False,
    )
```

time: 138 us -> 121 us (0.88)
  waiting for transfers between devices: 70 us -> 52.4 us
  starting transfers between devices: 37.6 us -> 47.9 us
  other arithmetic: 5.13 us -> 1.68 us
  matrix products: 3.35 us -> 0 us
  Pallas kernels: 16.2 us -> 14.6 us
    ppermute x33 -> x30, waiting for transfers between devices: 70 us -> 52.4 us  [send(): return lax.ppermute(value, ('dp', 'zero'), pairs)]
    ppermute x33 -> x30, starting transfers between devices: 37.6 us -> 47.9 us  [send(): return lax.ppermute(value, ('dp', 'zero'), pairs)]
    dot_general x8 -> x0, matrix products: 3.35 us -> none  [gram_of(): lax.dot_general(columns, columns, (((1,), (1,)), ((), ())), preferred_ele...]
    convert_element_type x6 -> x2, other arithmetic: 2.78 us -> 0.37 us  [reduce_scatter(): (m[4:].astype(F32) + o[4:].astype(F32)).astype(BF16)]
    gather x3 -> x0, local copies, waits for them, and re-layouts: 1.98 us -> none  [the longest x1 0.67 us: reduce_scatter(): sent = pack(jnp.take(slots, jnp.array(sent_places), mode='clip'), gradients)]
    pallas_call x7 -> x13, Pallas kernels: 16.2 us -> 14.6 us  [the longest x1 6.52 us: newton_schulz(): pl.pallas_call(newton_schulz_kernel, out_shape=jax.ShapeDtypeStruct(direc...]
  transfers between devices with their start and end apart: 33 -> 30, of which waited for: 21 -> 18; matrix products, arithmetic and copies ran while one was open for 5% -> 1% of each run, Pallas kernels for 9% -> 10%
where the time goes in v3:
time: 121 us; the launch traced here: 120 us
  waiting for transfers between devices  52.4 us (43%)
  starting transfers between devices  47.9 us (40%)
  Pallas kernels  14.6 us (12%)
  local copies, waits for them, and re-layouts  2.76 us (2%)
  other arithmetic  1.68 us (1%)
    ppermute x30, waiting for transfers between devices, send(): return lax.ppermute(value, ('dp', 'zero'), pairs)  52.4 us
    ppermute x30, starting transfers between devices, send(): return lax.ppermute(value, ('dp', 'zero'), pairs)  47.9 us
    pallas_call x1, Pallas kernels, newton_schulz(): pl.pallas_call(newton_schulz_kernel, out_shape=jax.ShapeDtypeStruct(direc...  6.52 us
    pallas_call x4, Pallas kernels, assemble(): pl.pallas_call(functools.partial(assemble_kernel, places), out_shape=jax....  5.11 us
    unnamed x10, local copies, waits for them, and re-layouts  2.65 us
  transfers between devices with their start and end apart: 30, of which 18 were waited for; matrix products, arithmetic and copies ran while one was open for 1% of the time, Pallas kernels for 10%

profile of v3, /device:TPU:2, one launch (start us, length us, event | category | flops | bytes accessed | tf_op | source)
XLA Modules:
  0.0 120.4 jit_solution(9351948120856685233)
XLA Ops:
  0.6 1.9 %copy-done.1 = bf16[1,16,384,256]{3,2,1,0:T(8,128)(2,1)S(1)} copy-done((bf16[1,16,384,256]{3,2,1,0:T(8,128)(2,1)S(1)}, bf16[1,16,384,256]{3,2,1,0:T(8,128)(2,1)}, u32[]{:S(2)}) %copy-start.1) | copy-done | bytes 3145752
  5.4 1.8 %collective-permute-start = (bf16[8,192,256]{2,1,0:T(8,128)(2,1)S(1)}, bf16[8,192,256]{2,1,0:T(8,128)(2,1)S(1)}, u32[]{:S(2)}, u32[]{:S(2)}) collective-permute-start(bf16[8,192,256]{2,1,0:T(8,128)(2,1)S(1)} %get-tuple-element.11), channel_id=1, source_target_pairs={{0,64},{1,17},{2,66},{3,19},{4,68},{5,21},{6,70},{7,23},{8,72},{9,... | collective-permute-start | bytes 2359304 | tf_op jit(solution)/shard_map/sum_over_replicas/ppermute | solution.py:55
  7.9 8.0 %collective-permute-done.2 = bf16[8,192,256]{2,1,0:T(8,128)(2,1)S(1)} collective-permute-done((bf16[8,192,256]{2,1,0:T(8,128)(2,1)S(1)}, bf16[8,192,256]{2,1,0:T(8,128)(2,1)S(1)}, u32[]{:S(2)}, u32[]{:S(2)}) %collective-permute-start.2) | collective-permute-done | bytes 786464 | tf_op jit(solution)/shard_map/sum_over_replicas/ppermute | solution.py:55
  16.1 3.6 %collective-permute-start.3 = (bf16[4,192,256]{2,1,0:T(8,128)(2,1)S(1)}, bf16[4,192,256]{2,1,0:T(8,128)(2,1)S(1)}, u32[]{:S(2)}, u32[]{:S(2)}) collective-permute-start(bf16[4,192,256]{2,1,0:T(8,128)(2,1)S(1)} %get-tuple-element.22), channel_id=1, source_target_pairs={{0,64},{1,17},{2,66},{3,19},{4,68},{5,21},{6,70},{7,23},{8,72},{9,... | collective-permute-start | bytes 1179656 | tf_op jit(solution)/shard_map/sum_over_replicas/ppermute | solution.py:55
  20.4 5.1 %collective-permute-done.3 = bf16[4,192,256]{2,1,0:T(8,128)(2,1)S(1)} collective-permute-done((bf16[4,192,256]{2,1,0:T(8,128)(2,1)S(1)}, bf16[4,192,256]{2,1,0:T(8,128)(2,1)S(1)}, u32[]{:S(2)}, u32[]{:S(2)}) %collective-permute-start.3) | collective-permute-done | bytes 393248 | tf_op jit(solution)/shard_map/sum_over_replicas/ppermute | solution.py:55
  25.5 2.2 %collective-permute-done.1 = bf16[4,192,256]{2,1,0:T(8,128)(2,1)S(1)} collective-permute-done((bf16[4,192,256]{2,1,0:T(8,128)(2,1)S(1)}, bf16[4,192,256]{2,1,0:T(8,128)(2,1)S(1)}, u32[]{:S(2)}, u32[]{:S(2)}) %collective-permute-start.1) | collective-permute-done | bytes 393248 | tf_op jit(solution)/shard_map/sum_over_replicas/ppermute | solution.py:55
  27.9 1.7 %collective-permute-start.6 = (bf16[384,256]{1,0:T(8,128)(2,1)S(1)}, bf16[384,256]{1,0:T(8,128)(2,1)S(1)}, u32[]{:S(2)}, u32[]{:S(2)}) collective-permute-start(bf16[384,256]{1,0:T(8,128)(2,1)S(1)} %pad_maximum_fusion.2), channel_id=1, source_target_pairs={{0,32},{1,129},{2,34},{3,131},{4,36},{5,133},{6,38},{7,135},{8,40}... | collective-permute-start | bytes 589832 | tf_op jit(solution)/shard_map/sum_over_replicas/ppermute | solution.py:55
  30.3 1.9 %collective-permute-start.4 = (bf16[384,256]{1,0:T(8,128)(2,1)S(1)}, bf16[384,256]{1,0:T(8,128)(2,1)S(1)}, u32[]{:S(2)}, u32[]{:S(2)}) collective-permute-start(bf16[384,256]{1,0:T(8,128)(2,1)S(1)} %pad_maximum_fusion), channel_id=1, source_target_pairs={{0,48},{1,193},{2,50},{3,195},{4,52},{5,197},{6,54},{7,199},{8,56}... | collective-permute-start | bytes 589832 | tf_op jit(solution)/shard_map/sum_over_replicas/ppermute | solution.py:55
  32.2 2.9 %collective-permute-done.6 = bf16[384,256]{1,0:T(8,128)(2,1)S(1)} collective-permute-done((bf16[384,256]{1,0:T(8,128)(2,1)S(1)}, bf16[384,256]{1,0:T(8,128)(2,1)S(1)}, u32[]{:S(2)}, u32[]{:S(2)}) %collective-permute-start.6) | collective-permute-done | bytes 196640 | tf_op jit(solution)/shard_map/sum_over_replicas/ppermute | solution.py:55
  38.5 1.9 %collective-permute-start.7 = (bf16[384,256]{1,0:T(8,128)(2,1)S(1)}, bf16[384,256]{1,0:T(8,128)(2,1)S(1)}, u32[]{:S(2)}, u32[]{:S(2)}) collective-permute-start(bf16[384,256]{1,0:T(8,128)(2,1)S(1)} %get-tuple-element.19.refs_0_), channel_id=1, source_target_pairs={{0,48},{1,193},{2,50},{3,195},{4,52},{5,197},{6,54},{7,199},{8,56}... | collective-permute-start | bytes 589832 | tf_op jit(solution)/shard_map/moment_gather/ppermute | solution.py:55
  40.4 2.9 %collective-permute-start.9 = (bf16[384,256]{1,0:T(8,128)(2,1)S(1)}, bf16[384,256]{1,0:T(8,128)(2,1)S(1)}, u32[]{:S(2)}, u32[]{:S(2)}) collective-permute-start(bf16[384,256]{1,0:T(8,128)(2,1)S(1)} %get-tuple-element.19.refs_0_), channel_id=1, source_target_pairs={{0,32},{1,129},{2,34},{3,131},{4,36},{5,133},{6,38},{7,135},{8,40}... | collective-permute-start | bytes 589832 | tf_op jit(solution)/shard_map/moment_gather/ppermute | solution.py:55
  43.3 1.9 %collective-permute-start.14 = (bf16[384,256]{1,0:T(8,128)(2,1)S(1)}, bf16[384,256]{1,0:T(8,128)(2,1)S(1)}, u32[]{:S(2)}, u32[]{:S(2)}) collective-permute-start(bf16[384,256]{1,0:T(8,128)(2,1)S(1)} %get-tuple-element.18.refs_0_.direction_ref), channel_id=1, source_target_pairs={{0,2},{1,15},{2,4},{3,1},{4,6},{5,3},{6,8},{7,5},{8,10},{9,7},{10,... | collective-permute-start | bytes 589832 | tf_op jit(solution)/shard_map/gram_over_columns/ppermute | solution.py:55
  45.2 1.9 %collective-permute-start.18 = (bf16[384,256]{1,0:T(8,128)(2,1)S(1)}, bf16[384,256]{1,0:T(8,128)(2,1)S(1)}, u32[]{:S(2)}, u32[]{:S(2)}) collective-permute-start(bf16[384,256]{1,0:T(8,128)(2,1)S(1)} %collective-permute-done.17), channel_id=1, source_target_pairs={{0,2},{1,15},{2,4},{3,1},{4,6},{5,3},{6,8},{7,5},{8,10},{9,7},{10,... | collective-permute-start | bytes 589832 | tf_op jit(solution)/shard_map/gram_over_columns/ppermute | solution.py:55
  47.1 1.9 %collective-permute-done.9.refs_3_ = bf16[384,256]{1,0:T(8,128)(2,1)S(1)} collective-permute-done((bf16[384,256]{1,0:T(8,128)(2,1)S(1)}, bf16[384,256]{1,0:T(8,128)(2,1)S(1)}, u32[]{:S(2)}, u32[]{:S(2)}) %collective-permute-start.9) | collective-permute-done | bytes 196640 | tf_op jit(solution)/shard_map/moment_gather/ppermute | solution.py:55
  49.1 2.1 %collective-permute-start.10 = (bf16[4,192,256]{2,1,0:T(8,128)(2,1)S(1)}, bf16[4,192,256]{2,1,0:T(8,128)(2,1)S(1)}, u32[]{:S(2)}, u32[]{:S(2)}) collective-permute-start(bf16[4,192,256]{2,1,0:T(8,128)(2,1)S(1)} %get-tuple-element.14.refs_3_), channel_id=1, source_target_pairs={{0,192},{1,49},{2,194},{3,51},{4,196},{5,53},{6,198},{7,55},{8,200... | collective-permute-start | bytes 1179656 | tf_op jit(solution)/shard_map/moment_gather/ppermute | solution.py:55
  51.5 1.9 %collective-permute-start.12 = (bf16[4,192,256]{2,1,0:T(8,128)(2,1)S(1)}, bf16[4,192,256]{2,1,0:T(8,128)(2,1)S(1)}, u32[]{:S(2)}, u32[]{:S(2)}) collective-permute-start(bf16[4,192,256]{2,1,0:T(8,128)(2,1)S(1)} %get-tuple-element.15.refs_4_), channel_id=1, source_target_pairs={{0,64},{1,17},{2,66},{3,19},{4,68},{5,21},{6,70},{7,23},{8,72},{9,... | collective-permute-start | bytes 1179656 | tf_op jit(solution)/shard_map/moment_gather/ppermute | solution.py:55
  53.4 1.9 %collective-permute-start.15 = (bf16[384,256]{1,0:T(8,128)(2,1)S(1)}, bf16[384,256]{1,0:T(8,128)(2,1)S(1)}, u32[]{:S(2)}, u32[]{:S(2)}) collective-permute-start(bf16[384,256]{1,0:T(8,128)(2,1)S(1)} %collective-permute-done.14.refs_0_), channel_id=1, source_target_pairs={{0,2},{1,15},{2,4},{3,1},{4,6},{5,3},{6,8},{7,5},{8,10},{9,7},{10,... | collective-permute-start | bytes 589832 | tf_op jit(solution)/shard_map/gram_over_columns/ppermute | solution.py:55
  55.3 1.9 %collective-permute-start.19 = (bf16[384,256]{1,0:T(8,128)(2,1)S(1)}, bf16[384,256]{1,0:T(8,128)(2,1)S(1)}, u32[]{:S(2)}, u32[]{:S(2)}) collective-permute-start(bf16[384,256]{1,0:T(8,128)(2,1)S(1)} %collective-permute-done.18.refs_1_), channel_id=1, source_target_pairs={{0,2},{1,15},{2,4},{3,1},{4,6},{5,3},{6,8},{7,5},{8,10},{9,7},{10,... | collective-permute-start | bytes 589832 | tf_op jit(solution)/shard_map/gram_over_columns/ppermute | solution.py:55
  57.3 5.6 %collective-permute-done.15.refs_0_ = bf16[384,256]{1,0:T(8,128)(2,1)S(1)} collective-permute-done((bf16[384,256]{1,0:T(8,128)(2,1)S(1)}, bf16[384,256]{1,0:T(8,128)(2,1)S(1)}, u32[]{:S(2)}, u32[]{:S(2)}) %collective-permute-start.15) | collective-permute-done | bytes 196640 | tf_op jit(solution)/shard_map/gram_over_columns/ppermute | solution.py:55
  62.9 2.0 %collective-permute-start.21 = (bf16[384,256]{1,0:T(8,128)(2,1)S(1)}, bf16[384,256]{1,0:T(8,128)(2,1)S(1)}, u32[]{:S(2)}, u32[]{:S(2)}) collective-permute-start(bf16[384,256]{1,0:T(8,128)(2,1)S(1)} %collective-permute-done.15.refs_0_), channel_id=1, source_target_pairs={{0,4},{1,13},{2,6},{3,15},{4,8},{5,1},{6,10},{7,3},{8,12},{9,5},{1... | collective-permute-start | bytes 589832 | tf_op jit(solution)/shard_map/gram_over_columns/ppermute | solution.py:55
  65.3 3.8 %collective-permute-start.20 = (bf16[384,256]{1,0:T(8,128)(2,1)S(1)}, bf16[384,256]{1,0:T(8,128)(2,1)S(1)}, u32[]{:S(2)}, u32[]{:S(2)}) collective-permute-start(bf16[384,256]{1,0:T(8,128)(2,1)S(1)} %collective-permute-done.19.refs_1_), channel_id=1, source_target_pairs={{0,2},{1,15},{2,4},{3,1},{4,6},{5,3},{6,8},{7,5},{8,10},{9,7},{10,... | collective-permute-start | bytes 589832 | tf_op jit(solution)/shard_map/gram_over_columns/ppermute | solution.py:55
  69.8 3.1 %collective-permute-done.21.refs_2_ = bf16[384,256]{1,0:T(8,128)(2,1)S(1)} collective-permute-done((bf16[384,256]{1,0:T(8,128)(2,1)S(1)}, bf16[384,256]{1,0:T(8,128)(2,1)S(1)}, u32[]{:S(2)}, u32[]{:S(2)}) %collective-permute-start.21) | collective-permute-done | bytes 196640 | tf_op jit(solution)/shard_map/gram_over_columns/ppermute | solution.py:55
  72.9 3.2 %collective-permute-done.20.refs_1_ = bf16[384,256]{1,0:T(8,128)(2,1)S(1)} collective-permute-done((bf16[384,256]{1,0:T(8,128)(2,1)S(1)}, bf16[384,256]{1,0:T(8,128)(2,1)S(1)}, u32[]{:S(2)}, u32[]{:S(2)}) %collective-permute-start.20) | collective-permute-done | bytes 196640 | tf_op jit(solution)/shard_map/gram_over_columns/ppermute | solution.py:55
  78.7 6.5 %newton_schulz.1.refs_0_ = bf16[384,256]{1,0:T(8,128)(2,1)S(1)} custom-call(f32[384,384]{1,0:T(8,128)S(1)} %gram.7.mine_ref, f32[384,384]{1,0:T(8,128)S(1)} %collective-permute-done.22.other_ref, bf16[384,256]{1,0:T(8,128)(2,1)S(1)} %get-tuple-element.18.refs_0_.direction_ref), custom_call_target="tpu_custom_call" | custom-call | flops 7516192768 | bytes 2097152 | tf_op jit(solution)/shard_map/newton_schulz/pallas_call | solution.py:238
  86.7 3.3 %collective-permute-start.25 = (bf16[384,256]{1,0:T(8,128)(2,1)S(1)}, bf16[384,256]{1,0:T(8,128)(2,1)S(1)}, u32[]{:S(2)}, u32[]{:S(2)}) collective-permute-start(bf16[384,256]{1,0:T(8,128)(2,1)S(1)} %newton_schulz.1.refs_0_), channel_id=1, source_target_pairs={{0,32},{1,129},{2,34},{3,131},{4,36},{5,133},{6,38},{7,135},{8,40}... | collective-permute-start | bytes 589832 | tf_op jit(solution)/shard_map/update_gather/ppermute | solution.py:55
  90.0 2.2 %collective-permute-done.23.refs_1_ = bf16[384,256]{1,0:T(8,128)(2,1)S(1)} collective-permute-done((bf16[384,256]{1,0:T(8,128)(2,1)S(1)}, bf16[384,256]{1,0:T(8,128)(2,1)S(1)}, u32[]{:S(2)}, u32[]{:S(2)}) %collective-permute-start.23) | collective-permute-done | bytes 196640 | tf_op jit(solution)/shard_map/update_gather/ppermute | solution.py:55
  92.3 3.5 %collective-permute-done.25.refs_3_ = bf16[384,256]{1,0:T(8,128)(2,1)S(1)} collective-permute-done((bf16[384,256]{1,0:T(8,128)(2,1)S(1)}, bf16[384,256]{1,0:T(8,128)(2,1)S(1)}, u32[]{:S(2)}, u32[]{:S(2)}) %collective-permute-start.25) | collective-permute-done | bytes 196640 | tf_op jit(solution)/shard_map/update_gather/ppermute | solution.py:55
  97.0 2.3 %collective-permute-start.28 = (bf16[4,192,256]{2,1,0:T(8,128)(2,1)S(1)}, bf16[4,192,256]{2,1,0:T(8,128)(2,1)S(1)}, u32[]{:S(2)}, u32[]{:S(2)}) collective-permute-start(bf16[4,192,256]{2,1,0:T(8,128)(2,1)S(1)} %get-tuple-element.17), channel_id=1, source_target_pairs={{0,64},{1,17},{2,66},{3,19},{4,68},{5,21},{6,70},{7,23},{8,72},{9,... | collective-permute-start | bytes 1179656 | tf_op jit(solution)/shard_map/update_gather/ppermute | solution.py:55
  99.3 4.3 %collective-permute-done.26 = bf16[4,192,256]{2,1,0:T(8,128)(2,1)S(1)} collective-permute-done((bf16[4,192,256]{2,1,0:T(8,128)(2,1)S(1)}, bf16[4,192,256]{2,1,0:T(8,128)(2,1)S(1)}, u32[]{:S(2)}, u32[]{:S(2)}) %collective-permute-start.26) | collective-permute-done | bytes 393248 | tf_op jit(solution)/shard_map/update_gather/ppermute | solution.py:55
  103.7 3.1 %collective-permute-start.27 = (bf16[8,192,256]{2,1,0:T(8,128)(2,1)S(1)}, bf16[8,192,256]{2,1,0:T(8,128)(2,1)S(1)}, u32[]{:S(2)}, u32[]{:S(2)}) collective-permute-start(bf16[8,192,256]{2,1,0:T(8,128)(2,1)S(1)} %constant_dynamic-update-slice_fusion.4.refs_0_), channel_id=1, source_target_pairs={{0,64},{1,17},{2,66},{3,19},{4,68},{5,21},{6,70},{7,23},{8,72},{9,... | collective-permute-start | bytes 2359304 | tf_op jit(solution)/shard_map/update_gather/ppermute | solution.py:55
  111.8 5.1 %collective-permute-done.27.refs_0_ = bf16[8,192,256]{2,1,0:T(8,128)(2,1)S(1)} collective-permute-done((bf16[8,192,256]{2,1,0:T(8,128)(2,1)S(1)}, bf16[8,192,256]{2,1,0:T(8,128)(2,1)S(1)}, u32[]{:S(2)}, u32[]{:S(2)}) %collective-permute-start.27) | collective-permute-done | bytes 786464 | tf_op jit(solution)/shard_map/update_gather/ppermute | solution.py:55
  116.8 2.1 %collective-permute-done.29.refs_1_ = bf16[8,192,256]{2,1,0:T(8,128)(2,1)S(1)} collective-permute-done((bf16[8,192,256]{2,1,0:T(8,128)(2,1)S(1)}, bf16[8,192,256]{2,1,0:T(8,128)(2,1)S(1)}, u32[]{:S(2)}, u32[]{:S(2)}) %collective-permute-start.29) | collective-permute-done | bytes 786464 | tf_op jit(solution)/shard_map/update_gather/ppermute | solution.py:55
  (63 shorter events, 21.9 us)
Async XLA Ops:
  0.6 1.9 %copy-start.1 = (bf16[1,16,384,256]{3,2,1,0:T(8,128)(2,1)S(1)}, bf16[1,16,384,256]{3,2,1,0:T(8,128)(2,1)}, u32[]{:S(2)}) copy-start(bf16[1,16,384,256]{3,2,1,0:T(8,128)(2,1)} %param.3) | copy-start | bytes 9437188
  3.9 12.1 %collective-permute-start.2 = (bf16[8,192,256]{2,1,0:T(8,128)(2,1)S(1)}, bf16[8,192,256]{2,1,0:T(8,128)(2,1)S(1)}, u32[]{:S(2)}, u32[]{:S(2)}) collective-permute-start(bf16[8,192,256]{2,1,0:T(8,128)(2,1)S(1)} %get-tuple-element.13), channel_id=1, source_target_pairs={{0,192},{1,49},{2,194},{3,51},{4,196},{5,53},{6,198},{7,55},{8,200... | collective-permute-start | bytes 2359304 | tf_op jit(solution)/shard_map/sum_over_replicas/ppermute | solution.py:55
  5.4 14.3 %collective-permute-start = (bf16[8,192,256]{2,1,0:T(8,128)(2,1)S(1)}, bf16[8,192,256]{2,1,0:T(8,128)(2,1)S(1)}, u32[]{:S(2)}, u32[]{:S(2)}) collective-permute-start(bf16[8,192,256]{2,1,0:T(8,128)(2,1)S(1)} %get-tuple-element.11), channel_id=1, source_target_pairs={{0,64},{1,17},{2,66},{3,19},{4,68},{5,21},{6,70},{7,23},{8,72},{9,... | collective-permute-start | bytes 2359304 | tf_op jit(solution)/shard_map/sum_over_replicas/ppermute | solution.py:55
  16.1 9.3 %collective-permute-start.3 = (bf16[4,192,256]{2,1,0:T(8,128)(2,1)S(1)}, bf16[4,192,256]{2,1,0:T(8,128)(2,1)S(1)}, u32[]{:S(2)}, u32[]{:S(2)}) collective-permute-start(bf16[4,192,256]{2,1,0:T(8,128)(2,1)S(1)} %get-tuple-element.22), channel_id=1, source_target_pairs={{0,64},{1,17},{2,66},{3,19},{4,68},{5,21},{6,70},{7,23},{8,72},{9,... | collective-permute-start | bytes 1179656 | tf_op jit(solution)/shard_map/sum_over_replicas/ppermute | solution.py:55
  19.9 7.9 %collective-permute-start.1 = (bf16[4,192,256]{2,1,0:T(8,128)(2,1)S(1)}, bf16[4,192,256]{2,1,0:T(8,128)(2,1)S(1)}, u32[]{:S(2)}, u32[]{:S(2)}) collective-permute-start(bf16[4,192,256]{2,1,0:T(8,128)(2,1)S(1)} %get-tuple-element.20), channel_id=1, source_target_pairs={{0,192},{1,49},{2,194},{3,51},{4,196},{5,53},{6,198},{7,55},{8,200... | collective-permute-start | bytes 1179656 | tf_op jit(solution)/shard_map/sum_over_replicas/ppermute | solution.py:55
  27.9 7.3 %collective-permute-start.6 = (bf16[384,256]{1,0:T(8,128)(2,1)S(1)}, bf16[384,256]{1,0:T(8,128)(2,1)S(1)}, u32[]{:S(2)}, u32[]{:S(2)}) collective-permute-start(bf16[384,256]{1,0:T(8,128)(2,1)S(1)} %pad_maximum_fusion.2), channel_id=1, source_target_pairs={{0,32},{1,129},{2,34},{3,131},{4,36},{5,133},{6,38},{7,135},{8,40}... | collective-permute-start | bytes 589832 | tf_op jit(solution)/shard_map/sum_over_replicas/ppermute | solution.py:55
  29.5 6.4 %collective-permute-start.5 = (bf16[384,256]{1,0:T(8,128)(2,1)S(1)}, bf16[384,256]{1,0:T(8,128)(2,1)S(1)}, u32[]{:S(2)}, u32[]{:S(2)}) collective-permute-start(bf16[384,256]{1,0:T(8,128)(2,1)S(1)} %pad_maximum_fusion.1), channel_id=1, source_target_pairs={{0,16},{1,65},{2,18},{3,67},{4,20},{5,69},{6,22},{7,71},{8,24},{9,... | collective-permute-start | bytes 589832 | tf_op jit(solution)/shard_map/sum_over_replicas/ppermute | solution.py:55
  30.3 7.0 %collective-permute-start.4 = (bf16[384,256]{1,0:T(8,128)(2,1)S(1)}, bf16[384,256]{1,0:T(8,128)(2,1)S(1)}, u32[]{:S(2)}, u32[]{:S(2)}) collective-permute-start(bf16[384,256]{1,0:T(8,128)(2,1)S(1)} %pad_maximum_fusion), channel_id=1, source_target_pairs={{0,48},{1,193},{2,50},{3,195},{4,52},{5,197},{6,54},{7,199},{8,56}... | collective-permute-start | bytes 589832 | tf_op jit(solution)/shard_map/sum_over_replicas/ppermute | solution.py:55
  38.4 6.8 %collective-permute-start.17 = (bf16[384,256]{1,0:T(8,128)(2,1)S(1)}, bf16[384,256]{1,0:T(8,128)(2,1)S(1)}, u32[]{:S(2)}, u32[]{:S(2)}) collective-permute-start(bf16[384,256]{1,0:T(8,128)(2,1)S(1)} %get-tuple-element.18.refs_0_.direction_ref), channel_id=1, source_target_pairs={{0,1},{1,0},{2,3},{3,2},{4,5},{5,4},{6,7},{7,6},{8,9},{9,8},{10,11... | collective-permute-start | bytes 589832 | tf_op jit(solution)/shard_map/gram_over_columns/ppermute | solution.py:55
  38.5 8.6 %collective-permute-start.7 = (bf16[384,256]{1,0:T(8,128)(2,1)S(1)}, bf16[384,256]{1,0:T(8,128)(2,1)S(1)}, u32[]{:S(2)}, u32[]{:S(2)}) collective-permute-start(bf16[384,256]{1,0:T(8,128)(2,1)S(1)} %get-tuple-element.19.refs_0_), channel_id=1, source_target_pairs={{0,48},{1,193},{2,50},{3,195},{4,52},{5,197},{6,54},{7,199},{8,56}... | collective-permute-start | bytes 589832 | tf_op jit(solution)/shard_map/moment_gather/ppermute | solution.py:55
  40.4 6.7 %collective-permute-start.8 = (bf16[384,256]{1,0:T(8,128)(2,1)S(1)}, bf16[384,256]{1,0:T(8,128)(2,1)S(1)}, u32[]{:S(2)}, u32[]{:S(2)}) collective-permute-start(bf16[384,256]{1,0:T(8,128)(2,1)S(1)} %get-tuple-element.19.refs_0_), channel_id=1, source_target_pairs={{0,16},{1,65},{2,18},{3,67},{4,20},{5,69},{6,22},{7,71},{8,24},{9,... | collective-permute-start | bytes 589832 | tf_op jit(solution)/shard_map/moment_gather/ppermute | solution.py:55
  40.4 8.6 %collective-permute-start.9 = (bf16[384,256]{1,0:T(8,128)(2,1)S(1)}, bf16[384,256]{1,0:T(8,128)(2,1)S(1)}, u32[]{:S(2)}, u32[]{:S(2)}) collective-permute-start(bf16[384,256]{1,0:T(8,128)(2,1)S(1)} %get-tuple-element.19.refs_0_), channel_id=1, source_target_pairs={{0,32},{1,129},{2,34},{3,131},{4,36},{5,133},{6,38},{7,135},{8,40}... | collective-permute-start | bytes 589832 | tf_op jit(solution)/shard_map/moment_gather/ppermute | solution.py:55
  43.3 10.1 %collective-permute-start.14 = (bf16[384,256]{1,0:T(8,128)(2,1)S(1)}, bf16[384,256]{1,0:T(8,128)(2,1)S(1)}, u32[]{:S(2)}, u32[]{:S(2)}) collective-permute-start(bf16[384,256]{1,0:T(8,128)(2,1)S(1)} %get-tuple-element.18.refs_0_.direction_ref), channel_id=1, source_target_pairs={{0,2},{1,15},{2,4},{3,1},{4,6},{5,3},{6,8},{7,5},{8,10},{9,7},{10,... | collective-permute-start | bytes 589832 | tf_op jit(solution)/shard_map/gram_over_columns/ppermute | solution.py:55
  45.2 10.1 %collective-permute-start.18 = (bf16[384,256]{1,0:T(8,128)(2,1)S(1)}, bf16[384,256]{1,0:T(8,128)(2,1)S(1)}, u32[]{:S(2)}, u32[]{:S(2)}) collective-permute-start(bf16[384,256]{1,0:T(8,128)(2,1)S(1)} %collective-permute-done.17), channel_id=1, source_target_pairs={{0,2},{1,15},{2,4},{3,1},{4,6},{5,3},{6,8},{7,5},{8,10},{9,7},{10,... | collective-permute-start | bytes 589832 | tf_op jit(solution)/shard_map/gram_over_columns/ppermute | solution.py:55
  49.1 20.0 %collective-permute-start.10 = (bf16[4,192,256]{2,1,0:T(8,128)(2,1)S(1)}, bf16[4,192,256]{2,1,0:T(8,128)(2,1)S(1)}, u32[]{:S(2)}, u32[]{:S(2)}) collective-permute-start(bf16[4,192,256]{2,1,0:T(8,128)(2,1)S(1)} %get-tuple-element.14.refs_3_), channel_id=1, source_target_pairs={{0,192},{1,49},{2,194},{3,51},{4,196},{5,53},{6,198},{7,55},{8,200... | collective-permute-start | bytes 1179656 | tf_op jit(solution)/shard_map/moment_gather/ppermute | solution.py:55
  51.5 18.0 %collective-permute-start.12 = (bf16[4,192,256]{2,1,0:T(8,128)(2,1)S(1)}, bf16[4,192,256]{2,1,0:T(8,128)(2,1)S(1)}, u32[]{:S(2)}, u32[]{:S(2)}) collective-permute-start(bf16[4,192,256]{2,1,0:T(8,128)(2,1)S(1)} %get-tuple-element.15.refs_4_), channel_id=1, source_target_pairs={{0,64},{1,17},{2,66},{3,19},{4,68},{5,21},{6,70},{7,23},{8,72},{9,... | collective-permute-start | bytes 1179656 | tf_op jit(solution)/shard_map/moment_gather/ppermute | solution.py:55
  53.4 9.5 %collective-permute-start.15 = (bf16[384,256]{1,0:T(8,128)(2,1)S(1)}, bf16[384,256]{1,0:T(8,128)(2,1)S(1)}, u32[]{:S(2)}, u32[]{:S(2)}) collective-permute-start(bf16[384,256]{1,0:T(8,128)(2,1)S(1)} %collective-permute-done.14.refs_0_), channel_id=1, source_target_pairs={{0,2},{1,15},{2,4},{3,1},{4,6},{5,3},{6,8},{7,5},{8,10},{9,7},{10,... | collective-permute-start | bytes 589832 | tf_op jit(solution)/shard_map/gram_over_columns/ppermute | solution.py:55
  55.3 10.0 %collective-permute-start.19 = (bf16[384,256]{1,0:T(8,128)(2,1)S(1)}, bf16[384,256]{1,0:T(8,128)(2,1)S(1)}, u32[]{:S(2)}, u32[]{:S(2)}) collective-permute-start(bf16[384,256]{1,0:T(8,128)(2,1)S(1)} %collective-permute-done.18.refs_1_), channel_id=1, source_target_pairs={{0,2},{1,15},{2,4},{3,1},{4,6},{5,3},{6,8},{7,5},{8,10},{9,7},{10,... | collective-permute-start | bytes 589832 | tf_op jit(solution)/shard_map/gram_over_columns/ppermute | solution.py:55
  62.9 6.9 %collective-permute-start.16 = (bf16[384,256]{1,0:T(8,128)(2,1)S(1)}, bf16[384,256]{1,0:T(8,128)(2,1)S(1)}, u32[]{:S(2)}, u32[]{:S(2)}) collective-permute-start(bf16[384,256]{1,0:T(8,128)(2,1)S(1)} %collective-permute-done.15.refs_0_), channel_id=1, source_target_pairs={{0,2},{1,15},{2,4},{3,1},{4,6},{5,3},{6,8},{7,5},{8,10},{9,7},{10,... | collective-permute-start | bytes 589832 | tf_op jit(solution)/shard_map/gram_over_columns/ppermute | solution.py:55
  62.9 10.0 %collective-permute-start.21 = (bf16[384,256]{1,0:T(8,128)(2,1)S(1)}, bf16[384,256]{1,0:T(8,128)(2,1)S(1)}, u32[]{:S(2)}, u32[]{:S(2)}) collective-permute-start(bf16[384,256]{1,0:T(8,128)(2,1)S(1)} %collective-permute-done.15.refs_0_), channel_id=1, source_target_pairs={{0,4},{1,13},{2,6},{3,15},{4,8},{5,1},{6,10},{7,3},{8,12},{9,5},{1... | collective-permute-start | bytes 589832 | tf_op jit(solution)/shard_map/gram_over_columns/ppermute | solution.py:55
  65.3 10.8 %collective-permute-start.20 = (bf16[384,256]{1,0:T(8,128)(2,1)S(1)}, bf16[384,256]{1,0:T(8,128)(2,1)S(1)}, u32[]{:S(2)}, u32[]{:S(2)}) collective-permute-start(bf16[384,256]{1,0:T(8,128)(2,1)S(1)} %collective-permute-done.19.refs_1_), channel_id=1, source_target_pairs={{0,2},{1,15},{2,4},{3,1},{4,6},{5,3},{6,8},{7,5},{8,10},{9,7},{10,... | collective-permute-start | bytes 589832 | tf_op jit(solution)/shard_map/gram_over_columns/ppermute | solution.py:55
  76.6 2.1 %collective-permute-start.22 = (f32[384,384]{1,0:T(8,128)S(1)}, f32[384,384]{1,0:T(8,128)S(1)}, u32[]{:S(2)}, u32[]{:S(2)}) collective-permute-start(f32[384,384]{1,0:T(8,128)S(1)} %gram.7.mine_ref), channel_id=1, source_target_pairs={{0,1},{1,0},{2,3},{3,2},{4,5},{5,4},{6,7},{7,6},{8,9},{9,8},{10,11... | collective-permute-start | bytes 1769480 | tf_op jit(solution)/shard_map/gram_over_columns/ppermute | solution.py:55
  76.7 13.3 %collective-permute-start.11 = (bf16[8,192,256]{2,1,0:T(8,128)(2,1)S(1)}, bf16[8,192,256]{2,1,0:T(8,128)(2,1)S(1)}, u32[]{:S(2)}, u32[]{:S(2)}) collective-permute-start(bf16[8,192,256]{2,1,0:T(8,128)(2,1)S(1)} %constant_dynamic-update-slice_fusion.refs_0_.refs_4_), channel_id=1, source_target_pairs={{0,64},{1,17},{2,66},{3,19},{4,68},{5,21},{6,70},{7,23},{8,72},{9,... | collective-permute-start | bytes 2359304 | tf_op jit(solution)/shard_map/moment_gather/ppermute | solution.py:55
  77.0 13.0 %collective-permute-start.13 = (bf16[8,192,256]{2,1,0:T(8,128)(2,1)S(1)}, bf16[8,192,256]{2,1,0:T(8,128)(2,1)S(1)}, u32[]{:S(2)}, u32[]{:S(2)}) collective-permute-start(bf16[8,192,256]{2,1,0:T(8,128)(2,1)S(1)} %constant_dynamic-update-slice_fusion.2.refs_1_.refs_5_), channel_id=1, source_target_pairs={{0,192},{1,49},{2,194},{3,51},{4,196},{5,53},{6,198},{7,55},{8,200... | collective-permute-start | bytes 2359304 | tf_op jit(solution)/shard_map/moment_gather/ppermute | solution.py:55
  85.2 7.0 %collective-permute-start.23 = (bf16[384,256]{1,0:T(8,128)(2,1)S(1)}, bf16[384,256]{1,0:T(8,128)(2,1)S(1)}, u32[]{:S(2)}, u32[]{:S(2)}) collective-permute-start(bf16[384,256]{1,0:T(8,128)(2,1)S(1)} %newton_schulz.1.refs_0_), channel_id=1, source_target_pairs={{0,48},{1,193},{2,50},{3,195},{4,52},{5,197},{6,54},{7,199},{8,56}... | collective-permute-start | bytes 589832 | tf_op jit(solution)/shard_map/update_gather/ppermute | solution.py:55
  86.6 5.7 %collective-permute-start.24 = (bf16[384,256]{1,0:T(8,128)(2,1)S(1)}, bf16[384,256]{1,0:T(8,128)(2,1)S(1)}, u32[]{:S(2)}, u32[]{:S(2)}) collective-permute-start(bf16[384,256]{1,0:T(8,128)(2,1)S(1)} %newton_schulz.1.refs_0_), channel_id=1, source_target_pairs={{0,16},{1,65},{2,18},{3,67},{4,20},{5,69},{6,22},{7,71},{8,24},{9,... | collective-permute-start | bytes 589832 | tf_op jit(solution)/shard_map/update_gather/ppermute | solution.py:55
  86.7 9.1 %collective-permute-start.25 = (bf16[384,256]{1,0:T(8,128)(2,1)S(1)}, bf16[384,256]{1,0:T(8,128)(2,1)S(1)}, u32[]{:S(2)}, u32[]{:S(2)}) collective-permute-start(bf16[384,256]{1,0:T(8,128)(2,1)S(1)} %newton_schulz.1.refs_0_), channel_id=1, source_target_pairs={{0,32},{1,129},{2,34},{3,131},{4,36},{5,133},{6,38},{7,135},{8,40}... | collective-permute-start | bytes 589832 | tf_op jit(solution)/shard_map/update_gather/ppermute | solution.py:55
  95.8 7.9 %collective-permute-start.26 = (bf16[4,192,256]{2,1,0:T(8,128)(2,1)S(1)}, bf16[4,192,256]{2,1,0:T(8,128)(2,1)S(1)}, u32[]{:S(2)}, u32[]{:S(2)}) collective-permute-start(bf16[4,192,256]{2,1,0:T(8,128)(2,1)S(1)} %get-tuple-element.16), channel_id=1, source_target_pairs={{0,192},{1,49},{2,194},{3,51},{4,196},{5,53},{6,198},{7,55},{8,200... | collective-permute-start | bytes 1179656 | tf_op jit(solution)/shard_map/update_gather/ppermute | solution.py:55
  97.0 9.8 %collective-permute-start.28 = (bf16[4,192,256]{2,1,0:T(8,128)(2,1)S(1)}, bf16[4,192,256]{2,1,0:T(8,128)(2,1)S(1)}, u32[]{:S(2)}, u32[]{:S(2)}) collective-permute-start(bf16[4,192,256]{2,1,0:T(8,128)(2,1)S(1)} %get-tuple-element.17), channel_id=1, source_target_pairs={{0,64},{1,17},{2,66},{3,19},{4,68},{5,21},{6,70},{7,23},{8,72},{9,... | collective-permute-start | bytes 1179656 | tf_op jit(solution)/shard_map/update_gather/ppermute | solution.py:55
  103.7 13.1 %collective-permute-start.27 = (bf16[8,192,256]{2,1,0:T(8,128)(2,1)S(1)}, bf16[8,192,256]{2,1,0:T(8,128)(2,1)S(1)}, u32[]{:S(2)}, u32[]{:S(2)}) collective-permute-start(bf16[8,192,256]{2,1,0:T(8,128)(2,1)S(1)} %constant_dynamic-update-slice_fusion.4.refs_0_), channel_id=1, source_target_pairs={{0,64},{1,17},{2,66},{3,19},{4,68},{5,21},{6,70},{7,23},{8,72},{9,... | collective-permute-start | bytes 2359304 | tf_op jit(solution)/shard_map/update_gather/ppermute | solution.py:55
  106.9 12.1 %collective-permute-start.29 = (bf16[8,192,256]{2,1,0:T(8,128)(2,1)S(1)}, bf16[8,192,256]{2,1,0:T(8,128)(2,1)S(1)}, u32[]{:S(2)}, u32[]{:S(2)}) collective-permute-start(bf16[8,192,256]{2,1,0:T(8,128)(2,1)S(1)} %constant_dynamic-update-slice_fusion.6.refs_1_), channel_id=1, source_target_pairs={{0,192},{1,49},{2,194},{3,51},{4,196},{5,53},{6,198},{7,55},{8,200... | collective-permute-start | bytes 2359304 | tf_op jit(solution)/shard_map/update_gather/ppermute | solution.py:55
  110.5 8.5 %copy-start = (bf16[16,384,256]{2,1,0:T(8,128)(2,1)S(1)}, bf16[16,384,256]{2,1,0:T(8,128)(2,1)}, u32[]{:S(2)}) copy-start(bf16[16,384,256]{2,1,0:T(8,128)(2,1)} %assemble.5.refs_3_) | copy-start | bytes 9437188
  (1 other events, 0.7 us)

commit v4 on v3

--- a/solution.py
+++ b/solution.py
@@ -164,30 +164,59 @@
     )(*pieces, *extra)
 
 
-def join_kernel(*refs):
-    for part, out_ref in enumerate(refs[-2:]):
-        for i in range(4):
-            out_ref[i] = refs[i][part * HALF : (part + 1) * HALF]
-
-
-def join(pieces, before):
-    half = jax.ShapeDtypeStruct((4, HALF, pieces[0].shape[-1]), BF16)
-    return pl.pallas_call(
-        join_kernel,
-        out_shape=[half, half],
-        in_specs=vmem(4) + anywhere(len(before)),
-        out_specs=vmem(2),
+def copy_rows_kernel(plan, *refs):
+    outs = refs[len(refs) - 1 - max(out for out, *_ in plan) :]
+    for out, i, piece, rows in plan:
+        outs[out][i] = refs[piece][...] if rows is None else refs[piece][rows[0] : rows[1]]
+
+
+def copy_rows(plan, pieces, counts, rows, before, flops=0):
+    width = pieces[0].shape[-1]
+    return pl.pallas_call(
+        functools.partial(copy_rows_kernel, plan),
+        out_shape=[jax.ShapeDtypeStruct((count, rows, width), BF16) for count in counts],
+        in_specs=vmem(len(pieces)) + anywhere(len(before)),
+        out_specs=vmem(len(counts)),
+        compiler_params=pltpu.CompilerParams(vmem_limit_bytes=16 * 1024 * 1024),
+        cost_estimate=pl.CostEstimate(
+            flops=flops, bytes_accessed=4 * sum(counts) * rows * width, transcendentals=0
+        ),
+        name="copy_rows",
+    )(*pieces, *before)
+
+
+def join(pieces, before=()):
+    plan = [
+        (part, i, i, (part * HALF, (part + 1) * HALF)) for part in range(2) for i in range(4)
+    ]
+    return copy_rows(plan, pieces, [4, 4], HALF, before)
+
+
+def append_kernel(first_ref, second_ref, *refs):
+    out_ref = refs[-1]
+    count = first_ref.shape[0]
+    out_ref[:count] = first_ref[...]
+    out_ref[count:] = second_ref[...]
+
+
+def append(first, second, before):
+    shape = (first.shape[0] + second.shape[0], *first.shape[1:])
+    return pl.pallas_call(
+        append_kernel,
+        out_shape=jax.ShapeDtypeStruct(shape, first.dtype),
+        in_specs=vmem(2) + anywhere(len(before)),
+        out_specs=vmem(1)[0],
         compiler_params=pltpu.CompilerParams(vmem_limit_bytes=16 * 1024 * 1024),
         cost_estimate=pl.CostEstimate(flops=0, bytes_accessed=2 << 20, transcendentals=0),
-        name="join",
-    )(*pieces, *before)
+        name="append",
+    )(first, second, *before)
 
 
 def all_gather(value, sizes, before=()):
     pieces = [value] + [send(value, cube_pairs(sizes, *TAIL[i])) for i in range(1, 4)]
-    four = join(pieces, before)
+    four = join(pieces)
     side = [send(v, cube_pairs(sizes, second)) for v, (_, second) in zip(four, HEADS)]
-    eight = [jnp.concatenate([m, o]) for m, o in zip(four, side)]
+    eight = [append(m, o, before) for m, o in zip(four, side)]
     received = [send(v, cube_pairs(sizes, first)) for v, (first, _) in zip(eight, HEADS)]
     return four, eight, received
 
@@ -198,7 +227,9 @@
         (part, places_of(first) + places_of(first, second))
         for part, (first, second) in enumerate(HEADS)
     ]
-    return assemble(received, far, assemble(held, near), before)
+    out = assemble(held, near)
+    out = assemble(received[:1], far[:1], out)
+    return assemble(received[1:], far[1:], out, before)
 
 
 def split(value):
@@ -217,16 +248,14 @@
     total = jnp.sum(jnp.where(row == column, gram, 0.0))
     scale = 1.0 / (jnp.sqrt(jnp.full((1, 1), total, F32)) + tiny_value)
     gram = gram * scale * scale
-    iterate = direction_ref[...].astype(F32)
+    iterate = direction_ref[...]
     for repeat in range(ITERS):
         high, low = split(gram)
         polynomial = (coef_second * high.astype(F32) + coef_third * dot(high, high)).astype(BF16)
-        x_high, x_low = split(iterate)
-        product = dot(polynomial, x_high)
-        if repeat:
-            product += dot(polynomial, x_low)
-        iterate = coef_first * iterate + product
+        product = dot(polynomial, iterate)
+        iterate = coef_first * iterate.astype(F32) + product
         if repeat < ITERS - 1:
+            iterate = iterate.astype(BF16)
             left = coef_first * gram + (dot(polynomial, high) + dot(polynomial, low))
             high, low = split(left)
             gram = coef_first * left + (dot(high, polynomial) + dot(low, polynomial))
@@ -289,10 +318,12 @@
         all_pairs(sizes, lambda x, y, z, c, hops=hops: (x, y, (z + hops * (1 - 2 * c)) % chips, c))
         for hops in (1, 2)
     ]
-    with jax.named_scope("moment_gather"):
-        four, eight, rest = all_gather(moment, sizes)
     with jax.named_scope("gram_over_columns"):
-        same, cross = send(direction, ring), send(send(direction, swap), ring)
+        swapped = send(direction, swap)
+        same, cross = send(direction, ring), send(swapped, ring)
+        with jax.named_scope("moment_gather"):
+            held = copy_rows([(0, 0, 0, None)], [moment], [1], ROWS, [swapped], 8 << 30)[0][0]
+            four, eight, rest = all_gather(held, sizes)
         gram = gram_of([direction])
         gram = gram_of([same, cross], gram)
         same, cross = send(same, ring), send(cross, ring)

time: 121 us -> 115 us (0.950)
  waiting for transfers between devices: 52.4 us -> 48.7 us
  starting transfers between devices: 47.9 us -> 45.5 us
    ppermute x30, waiting for transfers between devices: 52.4 us -> 48.7 us  [send(): return lax.ppermute(value, ('dp', 'zero'), pairs)]
    ppermute x30, starting transfers between devices: 47.9 us -> 45.5 us  [send(): return lax.ppermute(value, ('dp', 'zero'), pairs)]
    pallas_call x4 -> x6, Pallas kernels: 5.11 us -> 6.35 us  [assemble(): pl.pallas_call(functools.partial(assemble_kernel, places), out_shape=jax....]
    unnamed x10 -> x6, local copies, waits for them, and re-layouts: 2.65 us -> 2.54 us
  transfers between devices with their start and end apart: 30 -> 30, of which waited for: 18 -> 18; matrix products, arithmetic and copies ran while one was open for 1% -> 0% of each run, Pallas kernels for 10% -> 12%
where the time goes in v4:
time: 115 us
  waiting for transfers between devices  48.7 us (42%)
  starting transfers between devices  45.5 us (40%)
  Pallas kernels  15.5 us (13%)
  local copies, waits for them, and re-layouts  2.54 us (2%)
  other arithmetic  1.68 us (1%)
    ppermute x30, waiting for transfers between devices, send(): return lax.ppermute(value, ('dp', 'zero'), pairs)  48.7 us
    ppermute x30, starting transfers between devices, send(): return lax.ppermute(value, ('dp', 'zero'), pairs)  45.5 us
    pallas_call x6, Pallas kernels, assemble(): pl.pallas_call(functools.partial(assemble_kernel, places), out_shape=jax....  6.35 us
    pallas_call x1, Pallas kernels, newton_schulz(): pl.pallas_call(newton_schulz_kernel, out_shape=jax.ShapeDtypeStruct(direc...  5.92 us
    unnamed x6, local copies, waits for them, and re-layouts  2.54 us
  transfers between devices with their start and end apart: 30, of which 18 were waited for; matrix products, arithmetic and copies ran while one was open for 0% of the time, Pallas kernels for 12%

profile of v4, /device:TPU:2, one launch (start us, length us, event | category | flops | bytes accessed | tf_op | source)
XLA Modules:
  0.0 114.9 jit_solution(14122502543149102699)
XLA Ops:
  0.6 1.9 %copy-done.1 = bf16[1,16,384,256]{3,2,1,0:T(8,128)(2,1)S(1)} copy-done((bf16[1,16,384,256]{3,2,1,0:T(8,128)(2,1)S(1)}, bf16[1,16,384,256]{3,2,1,0:T(8,128)(2,1)}, u32[]{:S(2)}) %copy-start.1) | copy-done | bytes 3145752
  3.9 1.6 %collective-permute-start.2 = (bf16[8,192,256]{2,1,0:T(8,128)(2,1)S(1)}, bf16[8,192,256]{2,1,0:T(8,128)(2,1)S(1)}, u32[]{:S(2)}, u32[]{:S(2)}) collective-permute-start(bf16[8,192,256]{2,1,0:T(8,128)(2,1)S(1)} %get-tuple-element.13), channel_id=1, source_target_pairs={{0,192},{1,49},{2,194},{3,51},{4,196},{5,53},{6,198},{7,55},{8,200... | collective-permute-start | bytes 2359304 | tf_op jit(solution)/shard_map/sum_over_replicas/ppermute | solution.py:55
  5.4 1.8 %collective-permute-start = (bf16[8,192,256]{2,1,0:T(8,128)(2,1)S(1)}, bf16[8,192,256]{2,1,0:T(8,128)(2,1)S(1)}, u32[]{:S(2)}, u32[]{:S(2)}) collective-permute-start(bf16[8,192,256]{2,1,0:T(8,128)(2,1)S(1)} %get-tuple-element.11), channel_id=1, source_target_pairs={{0,64},{1,17},{2,66},{3,19},{4,68},{5,21},{6,70},{7,23},{8,72},{9,... | collective-permute-start | bytes 2359304 | tf_op jit(solution)/shard_map/sum_over_replicas/ppermute | solution.py:55
  7.9 8.0 %collective-permute-done.2 = bf16[8,192,256]{2,1,0:T(8,128)(2,1)S(1)} collective-permute-done((bf16[8,192,256]{2,1,0:T(8,128)(2,1)S(1)}, bf16[8,192,256]{2,1,0:T(8,128)(2,1)S(1)}, u32[]{:S(2)}, u32[]{:S(2)}) %collective-permute-start.2) | collective-permute-done | bytes 786464 | tf_op jit(solution)/shard_map/sum_over_replicas/ppermute | solution.py:55
  16.1 3.6 %collective-permute-start.3 = (bf16[4,192,256]{2,1,0:T(8,128)(2,1)S(1)}, bf16[4,192,256]{2,1,0:T(8,128)(2,1)S(1)}, u32[]{:S(2)}, u32[]{:S(2)}) collective-permute-start(bf16[4,192,256]{2,1,0:T(8,128)(2,1)S(1)} %get-tuple-element.22), channel_id=1, source_target_pairs={{0,64},{1,17},{2,66},{3,19},{4,68},{5,21},{6,70},{7,23},{8,72},{9,... | collective-permute-start | bytes 1179656 | tf_op jit(solution)/shard_map/sum_over_replicas/ppermute | solution.py:55
  20.4 5.1 %collective-permute-done.3 = bf16[4,192,256]{2,1,0:T(8,128)(2,1)S(1)} collective-permute-done((bf16[4,192,256]{2,1,0:T(8,128)(2,1)S(1)}, bf16[4,192,256]{2,1,0:T(8,128)(2,1)S(1)}, u32[]{:S(2)}, u32[]{:S(2)}) %collective-permute-start.3) | collective-permute-done | bytes 393248 | tf_op jit(solution)/shard_map/sum_over_replicas/ppermute | solution.py:55
  25.5 2.2 %collective-permute-done.1 = bf16[4,192,256]{2,1,0:T(8,128)(2,1)S(1)} collective-permute-done((bf16[4,192,256]{2,1,0:T(8,128)(2,1)S(1)}, bf16[4,192,256]{2,1,0:T(8,128)(2,1)S(1)}, u32[]{:S(2)}, u32[]{:S(2)}) %collective-permute-start.1) | collective-permute-done | bytes 393248 | tf_op jit(solution)/shard_map/sum_over_replicas/ppermute | solution.py:55
  27.9 1.7 %collective-permute-start.6 = (bf16[384,256]{1,0:T(8,128)(2,1)S(1)}, bf16[384,256]{1,0:T(8,128)(2,1)S(1)}, u32[]{:S(2)}, u32[]{:S(2)}) collective-permute-start(bf16[384,256]{1,0:T(8,128)(2,1)S(1)} %pad_maximum_fusion.2), channel_id=1, source_target_pairs={{0,32},{1,129},{2,34},{3,131},{4,36},{5,133},{6,38},{7,135},{8,40}... | collective-permute-start | bytes 589832 | tf_op jit(solution)/shard_map/sum_over_replicas/ppermute | solution.py:55
  30.3 1.9 %collective-permute-start.4 = (bf16[384,256]{1,0:T(8,128)(2,1)S(1)}, bf16[384,256]{1,0:T(8,128)(2,1)S(1)}, u32[]{:S(2)}, u32[]{:S(2)}) collective-permute-start(bf16[384,256]{1,0:T(8,128)(2,1)S(1)} %pad_maximum_fusion), channel_id=1, source_target_pairs={{0,48},{1,193},{2,50},{3,195},{4,52},{5,197},{6,54},{7,199},{8,56}... | collective-permute-start | bytes 589832 | tf_op jit(solution)/shard_map/sum_over_replicas/ppermute | solution.py:55
  32.2 2.9 %collective-permute-done.6 = bf16[384,256]{1,0:T(8,128)(2,1)S(1)} collective-permute-done((bf16[384,256]{1,0:T(8,128)(2,1)S(1)}, bf16[384,256]{1,0:T(8,128)(2,1)S(1)}, u32[]{:S(2)}, u32[]{:S(2)}) %collective-permute-start.6) | collective-permute-done | bytes 196640 | tf_op jit(solution)/shard_map/sum_over_replicas/ppermute | solution.py:55
  36.0 1.3 %collective-permute-done.4 = bf16[384,256]{1,0:T(8,128)(2,1)S(1)} collective-permute-done((bf16[384,256]{1,0:T(8,128)(2,1)S(1)}, bf16[384,256]{1,0:T(8,128)(2,1)S(1)}, u32[]{:S(2)}, u32[]{:S(2)}) %collective-permute-start.4) | collective-permute-done | bytes 196640 | tf_op jit(solution)/shard_map/sum_over_replicas/ppermute | solution.py:55
  38.5 2.0 %collective-permute-start.15 = (bf16[384,256]{1,0:T(8,128)(2,1)S(1)}, bf16[384,256]{1,0:T(8,128)(2,1)S(1)}, u32[]{:S(2)}, u32[]{:S(2)}) collective-permute-start(bf16[384,256]{1,0:T(8,128)(2,1)S(1)} %get-tuple-element.18.refs_0_.direction_ref), channel_id=1, source_target_pairs={{0,2},{1,15},{2,4},{3,1},{4,6},{5,3},{6,8},{7,5},{8,10},{9,7},{10,... | collective-permute-start | bytes 589832 | tf_op jit(solution)/shard_map/gram_over_columns/ppermute | solution.py:55
  40.5 1.4 %collective-permute-start.8 = (bf16[384,256]{1,0:T(8,128)(2,1)S(1)}, bf16[384,256]{1,0:T(8,128)(2,1)S(1)}, u32[]{:S(2)}, u32[]{:S(2)}) collective-permute-start(bf16[384,256]{1,0:T(8,128)(2,1)S(1)} %bitcast.25), channel_id=1, source_target_pairs={{0,48},{1,193},{2,50},{3,195},{4,52},{5,197},{6,54},{7,199},{8,56}... | collective-permute-start | bytes 589832 | tf_op jit(solution)/shard_map/gram_over_columns/moment_gather/ppermute | solution.py:55
  42.1 3.2 %collective-permute-start.10 = (bf16[384,256]{1,0:T(8,128)(2,1)S(1)}, bf16[384,256]{1,0:T(8,128)(2,1)S(1)}, u32[]{:S(2)}, u32[]{:S(2)}) collective-permute-start(bf16[384,256]{1,0:T(8,128)(2,1)S(1)} %bitcast.27), channel_id=1, source_target_pairs={{0,32},{1,129},{2,34},{3,131},{4,36},{5,133},{6,38},{7,135},{8,40}... | collective-permute-start | bytes 589832 | tf_op jit(solution)/shard_map/gram_over_columns/moment_gather/ppermute | solution.py:55
  45.3 1.9 %collective-permute-start.18 = (bf16[384,256]{1,0:T(8,128)(2,1)S(1)}, bf16[384,256]{1,0:T(8,128)(2,1)S(1)}, u32[]{:S(2)}, u32[]{:S(2)}) collective-permute-start(bf16[384,256]{1,0:T(8,128)(2,1)S(1)} %collective-permute-done.7.refs_1_), channel_id=1, source_target_pairs={{0,2},{1,15},{2,4},{3,1},{4,6},{5,3},{6,8},{7,5},{8,10},{9,7},{10,... | collective-permute-start | bytes 589832 | tf_op jit(solution)/shard_map/gram_over_columns/ppermute | solution.py:55
  49.1 1.9 %collective-permute-done.10.refs_3_ = bf16[384,256]{1,0:T(8,128)(2,1)S(1)} collective-permute-done((bf16[384,256]{1,0:T(8,128)(2,1)S(1)}, bf16[384,256]{1,0:T(8,128)(2,1)S(1)}, u32[]{:S(2)}, u32[]{:S(2)}) %collective-permute-start.10) | collective-permute-done | bytes 196640 | tf_op jit(solution)/shard_map/gram_over_columns/moment_gather/ppermute | solution.py:55
  51.1 2.4 %collective-permute-start.11 = (bf16[4,192,256]{2,1,0:T(8,128)(2,1)S(1)}, bf16[4,192,256]{2,1,0:T(8,128)(2,1)S(1)}, u32[]{:S(2)}, u32[]{:S(2)}) collective-permute-start(bf16[4,192,256]{2,1,0:T(8,128)(2,1)S(1)} %get-tuple-element.14.first_ref.refs_4_), channel_id=1, source_target_pairs={{0,64},{1,17},{2,66},{3,19},{4,68},{5,21},{6,70},{7,23},{8,72},{9,... | collective-permute-start | bytes 1179656 | tf_op jit(solution)/shard_map/gram_over_columns/moment_gather/ppermute | solution.py:55
  54.5 1.9 %collective-permute-start.19 = (bf16[384,256]{1,0:T(8,128)(2,1)S(1)}, bf16[384,256]{1,0:T(8,128)(2,1)S(1)}, u32[]{:S(2)}, u32[]{:S(2)}) collective-permute-start(bf16[384,256]{1,0:T(8,128)(2,1)S(1)} %collective-permute-done.18.refs_1_), channel_id=1, source_target_pairs={{0,2},{1,15},{2,4},{3,1},{4,6},{5,3},{6,8},{7,5},{8,10},{9,7},{10,... | collective-permute-start | bytes 589832 | tf_op jit(solution)/shard_map/gram_over_columns/ppermute | solution.py:55
  56.4 1.9 %collective-permute-start.17 = (bf16[384,256]{1,0:T(8,128)(2,1)S(1)}, bf16[384,256]{1,0:T(8,128)(2,1)S(1)}, u32[]{:S(2)}, u32[]{:S(2)}) collective-permute-start(bf16[384,256]{1,0:T(8,128)(2,1)S(1)} %collective-permute-done.16.refs_0_), channel_id=1, source_target_pairs={{0,2},{1,15},{2,4},{3,1},{4,6},{5,3},{6,8},{7,5},{8,10},{9,7},{10,... | collective-permute-start | bytes 589832 | tf_op jit(solution)/shard_map/gram_over_columns/ppermute | solution.py:55
  58.3 3.9 %collective-permute-start.21 = (bf16[384,256]{1,0:T(8,128)(2,1)S(1)}, bf16[384,256]{1,0:T(8,128)(2,1)S(1)}, u32[]{:S(2)}, u32[]{:S(2)}) collective-permute-start(bf16[384,256]{1,0:T(8,128)(2,1)S(1)} %collective-permute-done.16.refs_0_), channel_id=1, source_target_pairs={{0,4},{1,13},{2,6},{3,15},{4,8},{5,1},{6,10},{7,3},{8,12},{9,5},{1... | collective-permute-start | bytes 589832 | tf_op jit(solution)/shard_map/gram_over_columns/ppermute | solution.py:55
  65.5 4.1 %collective-permute-done.21.refs_2_ = bf16[384,256]{1,0:T(8,128)(2,1)S(1)} collective-permute-done((bf16[384,256]{1,0:T(8,128)(2,1)S(1)}, bf16[384,256]{1,0:T(8,128)(2,1)S(1)}, u32[]{:S(2)}, u32[]{:S(2)}) %collective-permute-start.21) | collective-permute-done | bytes 196640 | tf_op jit(solution)/shard_map/gram_over_columns/ppermute | solution.py:55
  69.6 2.4 %collective-permute-done.20.refs_1_ = bf16[384,256]{1,0:T(8,128)(2,1)S(1)} collective-permute-done((bf16[384,256]{1,0:T(8,128)(2,1)S(1)}, bf16[384,256]{1,0:T(8,128)(2,1)S(1)}, u32[]{:S(2)}, u32[]{:S(2)}) %collective-permute-start.20) | collective-permute-done | bytes 196640 | tf_op jit(solution)/shard_map/gram_over_columns/ppermute | solution.py:55
  73.7 1.3 %collective-permute-start.14 = (bf16[8,192,256]{2,1,0:T(8,128)(2,1)S(1)}, bf16[8,192,256]{2,1,0:T(8,128)(2,1)S(1)}, u32[]{:S(2)}, u32[]{:S(2)}) collective-permute-start(bf16[8,192,256]{2,1,0:T(8,128)(2,1)S(1)} %append.5.refs_0_.refs_4_), channel_id=1, source_target_pairs={{0,64},{1,17},{2,66},{3,19},{4,68},{5,21},{6,70},{7,23},{8,72},{9,... | collective-permute-start | bytes 2359304 | tf_op jit(solution)/shard_map/gram_over_columns/moment_gather/ppermute | solution.py:55
  75.1 5.9 %newton_schulz.1.refs_0_ = bf16[384,256]{1,0:T(8,128)(2,1)S(1)} custom-call(f32[384,384]{1,0:T(8,128)S(1)} %gram.7.mine_ref, f32[384,384]{1,0:T(8,128)S(1)} %collective-permute-done.22.other_ref, bf16[384,256]{1,0:T(8,128)(2,1)S(1)} %get-tuple-element.18.refs_0_.direction_ref), custom_call_target="tpu_custom_call" | custom-call | flops 7516192768 | bytes 2097152 | tf_op jit(solution)/shard_map/newton_schulz/pallas_call | solution.py:267
  81.0 1.4 %collective-permute-start.23 = (bf16[384,256]{1,0:T(8,128)(2,1)S(1)}, bf16[384,256]{1,0:T(8,128)(2,1)S(1)}, u32[]{:S(2)}, u32[]{:S(2)}) collective-permute-start(bf16[384,256]{1,0:T(8,128)(2,1)S(1)} %newton_schulz.1.refs_0_), channel_id=1, source_target_pairs={{0,48},{1,193},{2,50},{3,195},{4,52},{5,197},{6,54},{7,199},{8,56}... | collective-permute-start | bytes 589832 | tf_op jit(solution)/shard_map/update_gather/ppermute | solution.py:55
  82.5 3.3 %collective-permute-start.25 = (bf16[384,256]{1,0:T(8,128)(2,1)S(1)}, bf16[384,256]{1,0:T(8,128)(2,1)S(1)}, u32[]{:S(2)}, u32[]{:S(2)}) collective-permute-start(bf16[384,256]{1,0:T(8,128)(2,1)S(1)} %newton_schulz.1.refs_0_), channel_id=1, source_target_pairs={{0,32},{1,129},{2,34},{3,131},{4,36},{5,133},{6,38},{7,135},{8,40}... | collective-permute-start | bytes 589832 | tf_op jit(solution)/shard_map/update_gather/ppermute | solution.py:55
  85.8 2.2 %collective-permute-done.23.refs_1_ = bf16[384,256]{1,0:T(8,128)(2,1)S(1)} collective-permute-done((bf16[384,256]{1,0:T(8,128)(2,1)S(1)}, bf16[384,256]{1,0:T(8,128)(2,1)S(1)}, u32[]{:S(2)}, u32[]{:S(2)}) %collective-permute-start.23) | collective-permute-done | bytes 196640 | tf_op jit(solution)/shard_map/update_gather/ppermute | solution.py:55
  88.1 3.4 %collective-permute-done.25.refs_3_ = bf16[384,256]{1,0:T(8,128)(2,1)S(1)} collective-permute-done((bf16[384,256]{1,0:T(8,128)(2,1)S(1)}, bf16[384,256]{1,0:T(8,128)(2,1)S(1)}, u32[]{:S(2)}, u32[]{:S(2)}) %collective-permute-start.25) | collective-permute-done | bytes 196640 | tf_op jit(solution)/shard_map/update_gather/ppermute | solution.py:55
  91.6 1.7 %collective-permute-start.28 = (bf16[4,192,256]{2,1,0:T(8,128)(2,1)S(1)}, bf16[4,192,256]{2,1,0:T(8,128)(2,1)S(1)}, u32[]{:S(2)}, u32[]{:S(2)}) collective-permute-start(bf16[4,192,256]{2,1,0:T(8,128)(2,1)S(1)} %get-tuple-element.17.first_ref), channel_id=1, source_target_pairs={{0,192},{1,49},{2,194},{3,51},{4,196},{5,53},{6,198},{7,55},{8,200... | collective-permute-start | bytes 1179656 | tf_op jit(solution)/shard_map/update_gather/ppermute | solution.py:55
  93.9 5.5 %collective-permute-done.28.second_ref = bf16[4,192,256]{2,1,0:T(8,128)(2,1)S(1)} collective-permute-done((bf16[4,192,256]{2,1,0:T(8,128)(2,1)S(1)}, bf16[4,192,256]{2,1,0:T(8,128)(2,1)S(1)}, u32[]{:S(2)}, u32[]{:S(2)}) %collective-permute-start.28) | collective-permute-done | bytes 393248 | tf_op jit(solution)/shard_map/update_gather/ppermute | solution.py:55
  99.5 2.2 %collective-permute-start.29 = (bf16[8,192,256]{2,1,0:T(8,128)(2,1)S(1)}, bf16[8,192,256]{2,1,0:T(8,128)(2,1)S(1)}, u32[]{:S(2)}, u32[]{:S(2)}) collective-permute-start(bf16[8,192,256]{2,1,0:T(8,128)(2,1)S(1)} %append.7.refs_0_), channel_id=1, source_target_pairs={{0,64},{1,17},{2,66},{3,19},{4,68},{5,21},{6,70},{7,23},{8,72},{9,... | collective-permute-start | bytes 2359304 | tf_op jit(solution)/shard_map/update_gather/ppermute | solution.py:55
  107.1 4.5 %collective-permute-done.29.refs_0_ = bf16[8,192,256]{2,1,0:T(8,128)(2,1)S(1)} collective-permute-done((bf16[8,192,256]{2,1,0:T(8,128)(2,1)S(1)}, bf16[8,192,256]{2,1,0:T(8,128)(2,1)S(1)}, u32[]{:S(2)}, u32[]{:S(2)}) %collective-permute-start.29) | collective-permute-done | bytes 786464 | tf_op jit(solution)/shard_map/update_gather/ppermute | solution.py:55
  (62 shorter events, 23.4 us)
Async XLA Ops:
  0.6 1.9 %copy-start.1 = (bf16[1,16,384,256]{3,2,1,0:T(8,128)(2,1)S(1)}, bf16[1,16,384,256]{3,2,1,0:T(8,128)(2,1)}, u32[]{:S(2)}) copy-start(bf16[1,16,384,256]{3,2,1,0:T(8,128)(2,1)} %param.3) | copy-start | bytes 9437188
  3.9 12.1 %collective-permute-start.2 = (bf16[8,192,256]{2,1,0:T(8,128)(2,1)S(1)}, bf16[8,192,256]{2,1,0:T(8,128)(2,1)S(1)}, u32[]{:S(2)}, u32[]{:S(2)}) collective-permute-start(bf16[8,192,256]{2,1,0:T(8,128)(2,1)S(1)} %get-tuple-element.13), channel_id=1, source_target_pairs={{0,192},{1,49},{2,194},{3,51},{4,196},{5,53},{6,198},{7,55},{8,200... | collective-permute-start | bytes 2359304 | tf_op jit(solution)/shard_map/sum_over_replicas/ppermute | solution.py:55
  5.4 14.3 %collective-permute-start = (bf16[8,192,256]{2,1,0:T(8,128)(2,1)S(1)}, bf16[8,192,256]{2,1,0:T(8,128)(2,1)S(1)}, u32[]{:S(2)}, u32[]{:S(2)}) collective-permute-start(bf16[8,192,256]{2,1,0:T(8,128)(2,1)S(1)} %get-tuple-element.11), channel_id=1, source_target_pairs={{0,64},{1,17},{2,66},{3,19},{4,68},{5,21},{6,70},{7,23},{8,72},{9,... | collective-permute-start | bytes 2359304 | tf_op jit(solution)/shard_map/sum_over_replicas/ppermute | solution.py:55
  16.1 9.3 %collective-permute-start.3 = (bf16[4,192,256]{2,1,0:T(8,128)(2,1)S(1)}, bf16[4,192,256]{2,1,0:T(8,128)(2,1)S(1)}, u32[]{:S(2)}, u32[]{:S(2)}) collective-permute-start(bf16[4,192,256]{2,1,0:T(8,128)(2,1)S(1)} %get-tuple-element.22), channel_id=1, source_target_pairs={{0,64},{1,17},{2,66},{3,19},{4,68},{5,21},{6,70},{7,23},{8,72},{9,... | collective-permute-start | bytes 1179656 | tf_op jit(solution)/shard_map/sum_over_replicas/ppermute | solution.py:55
  19.9 7.9 %collective-permute-start.1 = (bf16[4,192,256]{2,1,0:T(8,128)(2,1)S(1)}, bf16[4,192,256]{2,1,0:T(8,128)(2,1)S(1)}, u32[]{:S(2)}, u32[]{:S(2)}) collective-permute-start(bf16[4,192,256]{2,1,0:T(8,128)(2,1)S(1)} %get-tuple-element.20), channel_id=1, source_target_pairs={{0,192},{1,49},{2,194},{3,51},{4,196},{5,53},{6,198},{7,55},{8,200... | collective-permute-start | bytes 1179656 | tf_op jit(solution)/shard_map/sum_over_replicas/ppermute | solution.py:55
  27.9 7.3 %collective-permute-start.6 = (bf16[384,256]{1,0:T(8,128)(2,1)S(1)}, bf16[384,256]{1,0:T(8,128)(2,1)S(1)}, u32[]{:S(2)}, u32[]{:S(2)}) collective-permute-start(bf16[384,256]{1,0:T(8,128)(2,1)S(1)} %pad_maximum_fusion.2), channel_id=1, source_target_pairs={{0,32},{1,129},{2,34},{3,131},{4,36},{5,133},{6,38},{7,135},{8,40}... | collective-permute-start | bytes 589832 | tf_op jit(solution)/shard_map/sum_over_replicas/ppermute | solution.py:55
  29.5 6.4 %collective-permute-start.5 = (bf16[384,256]{1,0:T(8,128)(2,1)S(1)}, bf16[384,256]{1,0:T(8,128)(2,1)S(1)}, u32[]{:S(2)}, u32[]{:S(2)}) collective-permute-start(bf16[384,256]{1,0:T(8,128)(2,1)S(1)} %pad_maximum_fusion.1), channel_id=1, source_target_pairs={{0,16},{1,65},{2,18},{3,67},{4,20},{5,69},{6,22},{7,71},{8,24},{9,... | collective-permute-start | bytes 589832 | tf_op jit(solution)/shard_map/sum_over_replicas/ppermute | solution.py:55
  30.3 7.0 %collective-permute-start.4 = (bf16[384,256]{1,0:T(8,128)(2,1)S(1)}, bf16[384,256]{1,0:T(8,128)(2,1)S(1)}, u32[]{:S(2)}, u32[]{:S(2)}) collective-permute-start(bf16[384,256]{1,0:T(8,128)(2,1)S(1)} %pad_maximum_fusion), channel_id=1, source_target_pairs={{0,48},{1,193},{2,50},{3,195},{4,52},{5,197},{6,54},{7,199},{8,56}... | collective-permute-start | bytes 589832 | tf_op jit(solution)/shard_map/sum_over_replicas/ppermute | solution.py:55
  38.4 2.1 %collective-permute-start.7 = (bf16[384,256]{1,0:T(8,128)(2,1)S(1)}, bf16[384,256]{1,0:T(8,128)(2,1)S(1)}, u32[]{:S(2)}, u32[]{:S(2)}) collective-permute-start(bf16[384,256]{1,0:T(8,128)(2,1)S(1)} %get-tuple-element.18.refs_0_.direction_ref), channel_id=1, source_target_pairs={{0,1},{1,0},{2,3},{3,2},{4,5},{5,4},{6,7},{7,6},{8,9},{9,8},{10,11... | collective-permute-start | bytes 589832 | tf_op jit(solution)/shard_map/gram_over_columns/ppermute | solution.py:55
  38.5 9.6 %collective-permute-start.15 = (bf16[384,256]{1,0:T(8,128)(2,1)S(1)}, bf16[384,256]{1,0:T(8,128)(2,1)S(1)}, u32[]{:S(2)}, u32[]{:S(2)}) collective-permute-start(bf16[384,256]{1,0:T(8,128)(2,1)S(1)} %get-tuple-element.18.refs_0_.direction_ref), channel_id=1, source_target_pairs={{0,2},{1,15},{2,4},{3,1},{4,6},{5,3},{6,8},{7,5},{8,10},{9,7},{10,... | collective-permute-start | bytes 589832 | tf_op jit(solution)/shard_map/gram_over_columns/ppermute | solution.py:55
  40.5 8.6 %collective-permute-start.8 = (bf16[384,256]{1,0:T(8,128)(2,1)S(1)}, bf16[384,256]{1,0:T(8,128)(2,1)S(1)}, u32[]{:S(2)}, u32[]{:S(2)}) collective-permute-start(bf16[384,256]{1,0:T(8,128)(2,1)S(1)} %bitcast.25), channel_id=1, source_target_pairs={{0,48},{1,193},{2,50},{3,195},{4,52},{5,197},{6,54},{7,199},{8,56}... | collective-permute-start | bytes 589832 | tf_op jit(solution)/shard_map/gram_over_columns/moment_gather/ppermute | solution.py:55
  41.9 7.2 %collective-permute-start.9 = (bf16[384,256]{1,0:T(8,128)(2,1)S(1)}, bf16[384,256]{1,0:T(8,128)(2,1)S(1)}, u32[]{:S(2)}, u32[]{:S(2)}) collective-permute-start(bf16[384,256]{1,0:T(8,128)(2,1)S(1)} %bitcast.26), channel_id=1, source_target_pairs={{0,16},{1,65},{2,18},{3,67},{4,20},{5,69},{6,22},{7,71},{8,24},{9,... | collective-permute-start | bytes 589832 | tf_op jit(solution)/shard_map/gram_over_columns/moment_gather/ppermute | solution.py:55
  42.1 9.0 %collective-permute-start.10 = (bf16[384,256]{1,0:T(8,128)(2,1)S(1)}, bf16[384,256]{1,0:T(8,128)(2,1)S(1)}, u32[]{:S(2)}, u32[]{:S(2)}) collective-permute-start(bf16[384,256]{1,0:T(8,128)(2,1)S(1)} %bitcast.27), channel_id=1, source_target_pairs={{0,32},{1,129},{2,34},{3,131},{4,36},{5,133},{6,38},{7,135},{8,40}... | collective-permute-start | bytes 589832 | tf_op jit(solution)/shard_map/gram_over_columns/moment_gather/ppermute | solution.py:55
  45.3 9.2 %collective-permute-start.18 = (bf16[384,256]{1,0:T(8,128)(2,1)S(1)}, bf16[384,256]{1,0:T(8,128)(2,1)S(1)}, u32[]{:S(2)}, u32[]{:S(2)}) collective-permute-start(bf16[384,256]{1,0:T(8,128)(2,1)S(1)} %collective-permute-done.7.refs_1_), channel_id=1, source_target_pairs={{0,2},{1,15},{2,4},{3,1},{4,6},{5,3},{6,8},{7,5},{8,10},{9,7},{10,... | collective-permute-start | bytes 589832 | tf_op jit(solution)/shard_map/gram_over_columns/ppermute | solution.py:55
  48.1 8.3 %collective-permute-start.16 = (bf16[384,256]{1,0:T(8,128)(2,1)S(1)}, bf16[384,256]{1,0:T(8,128)(2,1)S(1)}, u32[]{:S(2)}, u32[]{:S(2)}) collective-permute-start(bf16[384,256]{1,0:T(8,128)(2,1)S(1)} %collective-permute-done.15.refs_0_), channel_id=1, source_target_pairs={{0,2},{1,15},{2,4},{3,1},{4,6},{5,3},{6,8},{7,5},{8,10},{9,7},{10,... | collective-permute-start | bytes 589832 | tf_op jit(solution)/shard_map/gram_over_columns/ppermute | solution.py:55
  51.1 13.4 %collective-permute-start.11 = (bf16[4,192,256]{2,1,0:T(8,128)(2,1)S(1)}, bf16[4,192,256]{2,1,0:T(8,128)(2,1)S(1)}, u32[]{:S(2)}, u32[]{:S(2)}) collective-permute-start(bf16[4,192,256]{2,1,0:T(8,128)(2,1)S(1)} %get-tuple-element.14.first_ref.refs_4_), channel_id=1, source_target_pairs={{0,64},{1,17},{2,66},{3,19},{4,68},{5,21},{6,70},{7,23},{8,72},{9,... | collective-permute-start | bytes 1179656 | tf_op jit(solution)/shard_map/gram_over_columns/moment_gather/ppermute | solution.py:55
  53.5 11.0 %collective-permute-start.13 = (bf16[4,192,256]{2,1,0:T(8,128)(2,1)S(1)}, bf16[4,192,256]{2,1,0:T(8,128)(2,1)S(1)}, u32[]{:S(2)}, u32[]{:S(2)}) collective-permute-start(bf16[4,192,256]{2,1,0:T(8,128)(2,1)S(1)} %get-tuple-element.15.first_ref.refs_3_), channel_id=1, source_target_pairs={{0,192},{1,49},{2,194},{3,51},{4,196},{5,53},{6,198},{7,55},{8,200... | collective-permute-start | bytes 1179656 | tf_op jit(solution)/shard_map/gram_over_columns/moment_gather/ppermute | solution.py:55
  54.5 8.9 %collective-permute-start.19 = (bf16[384,256]{1,0:T(8,128)(2,1)S(1)}, bf16[384,256]{1,0:T(8,128)(2,1)S(1)}, u32[]{:S(2)}, u32[]{:S(2)}) collective-permute-start(bf16[384,256]{1,0:T(8,128)(2,1)S(1)} %collective-permute-done.18.refs_1_), channel_id=1, source_target_pairs={{0,2},{1,15},{2,4},{3,1},{4,6},{5,3},{6,8},{7,5},{8,10},{9,7},{10,... | collective-permute-start | bytes 589832 | tf_op jit(solution)/shard_map/gram_over_columns/ppermute | solution.py:55
  56.4 9.1 %collective-permute-start.17 = (bf16[384,256]{1,0:T(8,128)(2,1)S(1)}, bf16[384,256]{1,0:T(8,128)(2,1)S(1)}, u32[]{:S(2)}, u32[]{:S(2)}) collective-permute-start(bf16[384,256]{1,0:T(8,128)(2,1)S(1)} %collective-permute-done.16.refs_0_), channel_id=1, source_target_pairs={{0,2},{1,15},{2,4},{3,1},{4,6},{5,3},{6,8},{7,5},{8,10},{9,7},{10,... | collective-permute-start | bytes 589832 | tf_op jit(solution)/shard_map/gram_over_columns/ppermute | solution.py:55
  58.3 11.3 %collective-permute-start.21 = (bf16[384,256]{1,0:T(8,128)(2,1)S(1)}, bf16[384,256]{1,0:T(8,128)(2,1)S(1)}, u32[]{:S(2)}, u32[]{:S(2)}) collective-permute-start(bf16[384,256]{1,0:T(8,128)(2,1)S(1)} %collective-permute-done.16.refs_0_), channel_id=1, source_target_pairs={{0,4},{1,13},{2,6},{3,15},{4,8},{5,1},{6,10},{7,3},{8,12},{9,5},{1... | collective-permute-start | bytes 589832 | tf_op jit(solution)/shard_map/gram_over_columns/ppermute | solution.py:55
  63.4 8.6 %collective-permute-start.20 = (bf16[384,256]{1,0:T(8,128)(2,1)S(1)}, bf16[384,256]{1,0:T(8,128)(2,1)S(1)}, u32[]{:S(2)}, u32[]{:S(2)}) collective-permute-start(bf16[384,256]{1,0:T(8,128)(2,1)S(1)} %collective-permute-done.19.refs_1_), channel_id=1, source_target_pairs={{0,2},{1,15},{2,4},{3,1},{4,6},{5,3},{6,8},{7,5},{8,10},{9,7},{10,... | collective-permute-start | bytes 589832 | tf_op jit(solution)/shard_map/gram_over_columns/ppermute | solution.py:55
  72.5 2.6 %collective-permute-start.22 = (f32[384,384]{1,0:T(8,128)S(1)}, f32[384,384]{1,0:T(8,128)S(1)}, u32[]{:S(2)}, u32[]{:S(2)}) collective-permute-start(f32[384,384]{1,0:T(8,128)S(1)} %gram.7.mine_ref), channel_id=1, source_target_pairs={{0,1},{1,0},{2,3},{3,2},{4,5},{5,4},{6,7},{7,6},{8,9},{9,8},{10,11... | collective-permute-start | bytes 1769480 | tf_op jit(solution)/shard_map/gram_over_columns/ppermute | solution.py:55
  72.6 21.4 %collective-permute-start.12 = (bf16[8,192,256]{2,1,0:T(8,128)(2,1)S(1)}, bf16[8,192,256]{2,1,0:T(8,128)(2,1)S(1)}, u32[]{:S(2)}, u32[]{:S(2)}) collective-permute-start(bf16[8,192,256]{2,1,0:T(8,128)(2,1)S(1)} %append.4.refs_1_.refs_5_), channel_id=1, source_target_pairs={{0,192},{1,49},{2,194},{3,51},{4,196},{5,53},{6,198},{7,55},{8,200... | collective-permute-start | bytes 2359304 | tf_op jit(solution)/shard_map/gram_over_columns/moment_gather/ppermute | solution.py:55
  73.7 20.2 %collective-permute-start.14 = (bf16[8,192,256]{2,1,0:T(8,128)(2,1)S(1)}, bf16[8,192,256]{2,1,0:T(8,128)(2,1)S(1)}, u32[]{:S(2)}, u32[]{:S(2)}) collective-permute-start(bf16[8,192,256]{2,1,0:T(8,128)(2,1)S(1)} %append.5.refs_0_.refs_4_), channel_id=1, source_target_pairs={{0,64},{1,17},{2,66},{3,19},{4,68},{5,21},{6,70},{7,23},{8,72},{9,... | collective-permute-start | bytes 2359304 | tf_op jit(solution)/shard_map/gram_over_columns/moment_gather/ppermute | solution.py:55
  81.0 7.0 %collective-permute-start.23 = (bf16[384,256]{1,0:T(8,128)(2,1)S(1)}, bf16[384,256]{1,0:T(8,128)(2,1)S(1)}, u32[]{:S(2)}, u32[]{:S(2)}) collective-permute-start(bf16[384,256]{1,0:T(8,128)(2,1)S(1)} %newton_schulz.1.refs_0_), channel_id=1, source_target_pairs={{0,48},{1,193},{2,50},{3,195},{4,52},{5,197},{6,54},{7,199},{8,56}... | collective-permute-start | bytes 589832 | tf_op jit(solution)/shard_map/update_gather/ppermute | solution.py:55
  82.4 5.7 %collective-permute-start.24 = (bf16[384,256]{1,0:T(8,128)(2,1)S(1)}, bf16[384,256]{1,0:T(8,128)(2,1)S(1)}, u32[]{:S(2)}, u32[]{:S(2)}) collective-permute-start(bf16[384,256]{1,0:T(8,128)(2,1)S(1)} %newton_schulz.1.refs_0_), channel_id=1, source_target_pairs={{0,16},{1,65},{2,18},{3,67},{4,20},{5,69},{6,22},{7,71},{8,24},{9,... | collective-permute-start | bytes 589832 | tf_op jit(solution)/shard_map/update_gather/ppermute | solution.py:55
  82.5 9.1 %collective-permute-start.25 = (bf16[384,256]{1,0:T(8,128)(2,1)S(1)}, bf16[384,256]{1,0:T(8,128)(2,1)S(1)}, u32[]{:S(2)}, u32[]{:S(2)}) collective-permute-start(bf16[384,256]{1,0:T(8,128)(2,1)S(1)} %newton_schulz.1.refs_0_), channel_id=1, source_target_pairs={{0,32},{1,129},{2,34},{3,131},{4,36},{5,133},{6,38},{7,135},{8,40}... | collective-permute-start | bytes 589832 | tf_op jit(solution)/shard_map/update_gather/ppermute | solution.py:55
  91.6 7.9 %collective-permute-start.28 = (bf16[4,192,256]{2,1,0:T(8,128)(2,1)S(1)}, bf16[4,192,256]{2,1,0:T(8,128)(2,1)S(1)}, u32[]{:S(2)}, u32[]{:S(2)}) collective-permute-start(bf16[4,192,256]{2,1,0:T(8,128)(2,1)S(1)} %get-tuple-element.17.first_ref), channel_id=1, source_target_pairs={{0,192},{1,49},{2,194},{3,51},{4,196},{5,53},{6,198},{7,55},{8,200... | collective-permute-start | bytes 1179656 | tf_op jit(solution)/shard_map/update_gather/ppermute | solution.py:55
  93.3 8.4 %collective-permute-start.26 = (bf16[4,192,256]{2,1,0:T(8,128)(2,1)S(1)}, bf16[4,192,256]{2,1,0:T(8,128)(2,1)S(1)}, u32[]{:S(2)}, u32[]{:S(2)}) collective-permute-start(bf16[4,192,256]{2,1,0:T(8,128)(2,1)S(1)} %get-tuple-element.16.first_ref), channel_id=1, source_target_pairs={{0,64},{1,17},{2,66},{3,19},{4,68},{5,21},{6,70},{7,23},{8,72},{9,... | collective-permute-start | bytes 1179656 | tf_op jit(solution)/shard_map/update_gather/ppermute | solution.py:55
  99.5 12.1 %collective-permute-start.29 = (bf16[8,192,256]{2,1,0:T(8,128)(2,1)S(1)}, bf16[8,192,256]{2,1,0:T(8,128)(2,1)S(1)}, u32[]{:S(2)}, u32[]{:S(2)}) collective-permute-start(bf16[8,192,256]{2,1,0:T(8,128)(2,1)S(1)} %append.7.refs_0_), channel_id=1, source_target_pairs={{0,64},{1,17},{2,66},{3,19},{4,68},{5,21},{6,70},{7,23},{8,72},{9,... | collective-permute-start | bytes 2359304 | tf_op jit(solution)/shard_map/update_gather/ppermute | solution.py:55
  101.7 12.1 %collective-permute-start.27 = (bf16[8,192,256]{2,1,0:T(8,128)(2,1)S(1)}, bf16[8,192,256]{2,1,0:T(8,128)(2,1)S(1)}, u32[]{:S(2)}, u32[]{:S(2)}) collective-permute-start(bf16[8,192,256]{2,1,0:T(8,128)(2,1)S(1)} %append.6.refs_1_), channel_id=1, source_target_pairs={{0,192},{1,49},{2,194},{3,51},{4,196},{5,53},{6,198},{7,55},{8,200... | collective-permute-start | bytes 2359304 | tf_op jit(solution)/shard_map/update_gather/ppermute | solution.py:55
  107.1 6.7 %copy-start = (bf16[16,384,256]{2,1,0:T(8,128)(2,1)S(1)}, bf16[16,384,256]{2,1,0:T(8,128)(2,1)}, u32[]{:S(2)}) copy-start(bf16[16,384,256]{2,1,0:T(8,128)(2,1)} %assemble.8.refs_2_) | copy-start | bytes 9437188
  (1 other events, 0.7 us)

commit v5 on v4

--- a/solution.py
+++ b/solution.py
@@ -256,9 +256,12 @@
         iterate = coef_first * iterate.astype(F32) + product
         if repeat < ITERS - 1:
             iterate = iterate.astype(BF16)
-            left = coef_first * gram + (dot(polynomial, high) + dot(polynomial, low))
-            high, low = split(left)
-            gram = coef_first * left + (dot(high, polynomial) + dot(low, polynomial))
+            left = coef_first * gram + dot(
+                jnp.concatenate([polynomial, polynomial], 1), jnp.concatenate([high, low], 0)
+            )
+            gram = coef_first * left + dot(
+                jnp.concatenate(split(left), 1), jnp.concatenate([polynomial, polynomial], 0)
+            )
     factor = rms_factor * math.sqrt(max(ROWS, D))
     out_ref[...] = (iterate * (factor * scale)).astype(BF16)
 

time: 115 us -> 115 us (level)
  transfers between devices with their start and end apart: 30 -> 30, of which waited for: 18 -> 17; matrix products, arithmetic and copies ran while one was open for 0% -> 0% of each run, Pallas kernels for 12% -> 11%
where the time goes in v5:
time: 115 us
  waiting for transfers between devices  48.9 us (43%)
  starting transfers between devices  45.8 us (40%)
  Pallas kernels  14.6 us (13%)
  local copies, waits for them, and re-layouts  2.54 us (2%)
  other arithmetic  1.68 us (1%)
    ppermute x30, waiting for transfers between devices, send(): return lax.ppermute(value, ('dp', 'zero'), pairs)  48.9 us
    ppermute x30, starting transfers between devices, send(): return lax.ppermute(value, ('dp', 'zero'), pairs)  45.8 us
    pallas_call x6, Pallas kernels, assemble(): pl.pallas_call(functools.partial(assemble_kernel, places), out_shape=jax....  6.35 us
    pallas_call x1, Pallas kernels, newton_schulz(): pl.pallas_call(newton_schulz_kernel, out_shape=jax.ShapeDtypeStruct(direc...  5.07 us
    unnamed x6, local copies, waits for them, and re-layouts  2.54 us
  transfers between devices with their start and end apart: 30, of which 17 were waited for; matrix products, arithmetic and copies ran while one was open for 0% of the time, Pallas kernels for 11%

profile of v5, /device:TPU:2, one launch (start us, length us, event | category | flops | bytes accessed | tf_op | source)
XLA Modules:
  0.0 114.6 jit_solution(7761105456667964626)
XLA Ops:
  0.6 1.9 %copy-done.1 = bf16[1,16,384,256]{3,2,1,0:T(8,128)(2,1)S(1)} copy-done((bf16[1,16,384,256]{3,2,1,0:T(8,128)(2,1)S(1)}, bf16[1,16,384,256]{3,2,1,0:T(8,128)(2,1)}, u32[]{:S(2)}) %copy-start.1) | copy-done | bytes 3145752
  3.9 1.6 %collective-permute-start.2 = (bf16[8,192,256]{2,1,0:T(8,128)(2,1)S(1)}, bf16[8,192,256]{2,1,0:T(8,128)(2,1)S(1)}, u32[]{:S(2)}, u32[]{:S(2)}) collective-permute-start(bf16[8,192,256]{2,1,0:T(8,128)(2,1)S(1)} %get-tuple-element.13), channel_id=1, source_target_pairs={{0,192},{1,49},{2,194},{3,51},{4,196},{5,53},{6,198},{7,55},{8,200... | collective-permute-start | bytes 2359304 | tf_op jit(solution)/shard_map/sum_over_replicas/ppermute | solution.py:55
  5.4 1.8 %collective-permute-start = (bf16[8,192,256]{2,1,0:T(8,128)(2,1)S(1)}, bf16[8,192,256]{2,1,0:T(8,128)(2,1)S(1)}, u32[]{:S(2)}, u32[]{:S(2)}) collective-permute-start(bf16[8,192,256]{2,1,0:T(8,128)(2,1)S(1)} %get-tuple-element.11), channel_id=1, source_target_pairs={{0,64},{1,17},{2,66},{3,19},{4,68},{5,21},{6,70},{7,23},{8,72},{9,... | collective-permute-start | bytes 2359304 | tf_op jit(solution)/shard_map/sum_over_replicas/ppermute | solution.py:55
  7.9 8.0 %collective-permute-done.2 = bf16[8,192,256]{2,1,0:T(8,128)(2,1)S(1)} collective-permute-done((bf16[8,192,256]{2,1,0:T(8,128)(2,1)S(1)}, bf16[8,192,256]{2,1,0:T(8,128)(2,1)S(1)}, u32[]{:S(2)}, u32[]{:S(2)}) %collective-permute-start.2) | collective-permute-done | bytes 786464 | tf_op jit(solution)/shard_map/sum_over_replicas/ppermute | solution.py:55
  16.1 3.6 %collective-permute-start.3 = (bf16[4,192,256]{2,1,0:T(8,128)(2,1)S(1)}, bf16[4,192,256]{2,1,0:T(8,128)(2,1)S(1)}, u32[]{:S(2)}, u32[]{:S(2)}) collective-permute-start(bf16[4,192,256]{2,1,0:T(8,128)(2,1)S(1)} %get-tuple-element.22), channel_id=1, source_target_pairs={{0,64},{1,17},{2,66},{3,19},{4,68},{5,21},{6,70},{7,23},{8,72},{9,... | collective-permute-start | bytes 1179656 | tf_op jit(solution)/shard_map/sum_over_replicas/ppermute | solution.py:55
  20.4 5.1 %collective-permute-done.3 = bf16[4,192,256]{2,1,0:T(8,128)(2,1)S(1)} collective-permute-done((bf16[4,192,256]{2,1,0:T(8,128)(2,1)S(1)}, bf16[4,192,256]{2,1,0:T(8,128)(2,1)S(1)}, u32[]{:S(2)}, u32[]{:S(2)}) %collective-permute-start.3) | collective-permute-done | bytes 393248 | tf_op jit(solution)/shard_map/sum_over_replicas/ppermute | solution.py:55
  25.5 2.2 %collective-permute-done.1 = bf16[4,192,256]{2,1,0:T(8,128)(2,1)S(1)} collective-permute-done((bf16[4,192,256]{2,1,0:T(8,128)(2,1)S(1)}, bf16[4,192,256]{2,1,0:T(8,128)(2,1)S(1)}, u32[]{:S(2)}, u32[]{:S(2)}) %collective-permute-start.1) | collective-permute-done | bytes 393248 | tf_op jit(solution)/shard_map/sum_over_replicas/ppermute | solution.py:55
  27.9 1.7 %collective-permute-start.6 = (bf16[384,256]{1,0:T(8,128)(2,1)S(1)}, bf16[384,256]{1,0:T(8,128)(2,1)S(1)}, u32[]{:S(2)}, u32[]{:S(2)}) collective-permute-start(bf16[384,256]{1,0:T(8,128)(2,1)S(1)} %pad_maximum_fusion.2), channel_id=1, source_target_pairs={{0,32},{1,129},{2,34},{3,131},{4,36},{5,133},{6,38},{7,135},{8,40}... | collective-permute-start | bytes 589832 | tf_op jit(solution)/shard_map/sum_over_replicas/ppermute | solution.py:55
  30.3 1.9 %collective-permute-start.4 = (bf16[384,256]{1,0:T(8,128)(2,1)S(1)}, bf16[384,256]{1,0:T(8,128)(2,1)S(1)}, u32[]{:S(2)}, u32[]{:S(2)}) collective-permute-start(bf16[384,256]{1,0:T(8,128)(2,1)S(1)} %pad_maximum_fusion), channel_id=1, source_target_pairs={{0,48},{1,193},{2,50},{3,195},{4,52},{5,197},{6,54},{7,199},{8,56}... | collective-permute-start | bytes 589832 | tf_op jit(solution)/shard_map/sum_over_replicas/ppermute | solution.py:55
  32.2 2.9 %collective-permute-done.6 = bf16[384,256]{1,0:T(8,128)(2,1)S(1)} collective-permute-done((bf16[384,256]{1,0:T(8,128)(2,1)S(1)}, bf16[384,256]{1,0:T(8,128)(2,1)S(1)}, u32[]{:S(2)}, u32[]{:S(2)}) %collective-permute-start.6) | collective-permute-done | bytes 196640 | tf_op jit(solution)/shard_map/sum_over_replicas/ppermute | solution.py:55
  36.0 1.3 %collective-permute-done.4 = bf16[384,256]{1,0:T(8,128)(2,1)S(1)} collective-permute-done((bf16[384,256]{1,0:T(8,128)(2,1)S(1)}, bf16[384,256]{1,0:T(8,128)(2,1)S(1)}, u32[]{:S(2)}, u32[]{:S(2)}) %collective-permute-start.4) | collective-permute-done | bytes 196640 | tf_op jit(solution)/shard_map/sum_over_replicas/ppermute | solution.py:55
  38.5 2.0 %collective-permute-start.15 = (bf16[384,256]{1,0:T(8,128)(2,1)S(1)}, bf16[384,256]{1,0:T(8,128)(2,1)S(1)}, u32[]{:S(2)}, u32[]{:S(2)}) collective-permute-start(bf16[384,256]{1,0:T(8,128)(2,1)S(1)} %get-tuple-element.18.refs_0_.direction_ref), channel_id=1, source_target_pairs={{0,2},{1,15},{2,4},{3,1},{4,6},{5,3},{6,8},{7,5},{8,10},{9,7},{10,... | collective-permute-start | bytes 589832 | tf_op jit(solution)/shard_map/gram_over_columns/ppermute | solution.py:55
  40.5 1.4 %collective-permute-start.8 = (bf16[384,256]{1,0:T(8,128)(2,1)S(1)}, bf16[384,256]{1,0:T(8,128)(2,1)S(1)}, u32[]{:S(2)}, u32[]{:S(2)}) collective-permute-start(bf16[384,256]{1,0:T(8,128)(2,1)S(1)} %bitcast.25), channel_id=1, source_target_pairs={{0,48},{1,193},{2,50},{3,195},{4,52},{5,197},{6,54},{7,199},{8,56}... | collective-permute-start | bytes 589832 | tf_op jit(solution)/shard_map/gram_over_columns/moment_gather/ppermute | solution.py:55
  42.1 3.2 %collective-permute-start.10 = (bf16[384,256]{1,0:T(8,128)(2,1)S(1)}, bf16[384,256]{1,0:T(8,128)(2,1)S(1)}, u32[]{:S(2)}, u32[]{:S(2)}) collective-permute-start(bf16[384,256]{1,0:T(8,128)(2,1)S(1)} %bitcast.27), channel_id=1, source_target_pairs={{0,32},{1,129},{2,34},{3,131},{4,36},{5,133},{6,38},{7,135},{8,40}... | collective-permute-start | bytes 589832 | tf_op jit(solution)/shard_map/gram_over_columns/moment_gather/ppermute | solution.py:55
  45.3 1.9 %collective-permute-start.18 = (bf16[384,256]{1,0:T(8,128)(2,1)S(1)}, bf16[384,256]{1,0:T(8,128)(2,1)S(1)}, u32[]{:S(2)}, u32[]{:S(2)}) collective-permute-start(bf16[384,256]{1,0:T(8,128)(2,1)S(1)} %collective-permute-done.7.refs_1_), channel_id=1, source_target_pairs={{0,2},{1,15},{2,4},{3,1},{4,6},{5,3},{6,8},{7,5},{8,10},{9,7},{10,... | collective-permute-start | bytes 589832 | tf_op jit(solution)/shard_map/gram_over_columns/ppermute | solution.py:55
  49.1 1.9 %collective-permute-done.10.refs_3_ = bf16[384,256]{1,0:T(8,128)(2,1)S(1)} collective-permute-done((bf16[384,256]{1,0:T(8,128)(2,1)S(1)}, bf16[384,256]{1,0:T(8,128)(2,1)S(1)}, u32[]{:S(2)}, u32[]{:S(2)}) %collective-permute-start.10) | collective-permute-done | bytes 196640 | tf_op jit(solution)/shard_map/gram_over_columns/moment_gather/ppermute | solution.py:55
  51.1 2.4 %collective-permute-start.11 = (bf16[4,192,256]{2,1,0:T(8,128)(2,1)S(1)}, bf16[4,192,256]{2,1,0:T(8,128)(2,1)S(1)}, u32[]{:S(2)}, u32[]{:S(2)}) collective-permute-start(bf16[4,192,256]{2,1,0:T(8,128)(2,1)S(1)} %get-tuple-element.14.first_ref.refs_4_), channel_id=1, source_target_pairs={{0,64},{1,17},{2,66},{3,19},{4,68},{5,21},{6,70},{7,23},{8,72},{9,... | collective-permute-start | bytes 1179656 | tf_op jit(solution)/shard_map/gram_over_columns/moment_gather/ppermute | solution.py:55
  54.5 1.9 %collective-permute-start.19 = (bf16[384,256]{1,0:T(8,128)(2,1)S(1)}, bf16[384,256]{1,0:T(8,128)(2,1)S(1)}, u32[]{:S(2)}, u32[]{:S(2)}) collective-permute-start(bf16[384,256]{1,0:T(8,128)(2,1)S(1)} %collective-permute-done.18.refs_1_), channel_id=1, source_target_pairs={{0,2},{1,15},{2,4},{3,1},{4,6},{5,3},{6,8},{7,5},{8,10},{9,7},{10,... | collective-permute-start | bytes 589832 | tf_op jit(solution)/shard_map/gram_over_columns/ppermute | solution.py:55
  56.4 1.9 %collective-permute-start.17 = (bf16[384,256]{1,0:T(8,128)(2,1)S(1)}, bf16[384,256]{1,0:T(8,128)(2,1)S(1)}, u32[]{:S(2)}, u32[]{:S(2)}) collective-permute-start(bf16[384,256]{1,0:T(8,128)(2,1)S(1)} %collective-permute-done.16.refs_0_), channel_id=1, source_target_pairs={{0,2},{1,15},{2,4},{3,1},{4,6},{5,3},{6,8},{7,5},{8,10},{9,7},{10,... | collective-permute-start | bytes 589832 | tf_op jit(solution)/shard_map/gram_over_columns/ppermute | solution.py:55
  58.3 3.9 %collective-permute-start.21 = (bf16[384,256]{1,0:T(8,128)(2,1)S(1)}, bf16[384,256]{1,0:T(8,128)(2,1)S(1)}, u32[]{:S(2)}, u32[]{:S(2)}) collective-permute-start(bf16[384,256]{1,0:T(8,128)(2,1)S(1)} %collective-permute-done.16.refs_0_), channel_id=1, source_target_pairs={{0,4},{1,13},{2,6},{3,15},{4,8},{5,1},{6,10},{7,3},{8,12},{9,5},{1... | collective-permute-start | bytes 589832 | tf_op jit(solution)/shard_map/gram_over_columns/ppermute | solution.py:55
  65.5 4.1 %collective-permute-done.21.refs_2_ = bf16[384,256]{1,0:T(8,128)(2,1)S(1)} collective-permute-done((bf16[384,256]{1,0:T(8,128)(2,1)S(1)}, bf16[384,256]{1,0:T(8,128)(2,1)S(1)}, u32[]{:S(2)}, u32[]{:S(2)}) %collective-permute-start.21) | collective-permute-done | bytes 196640 | tf_op jit(solution)/shard_map/gram_over_columns/ppermute | solution.py:55
  69.6 2.4 %collective-permute-done.20.refs_1_ = bf16[384,256]{1,0:T(8,128)(2,1)S(1)} collective-permute-done((bf16[384,256]{1,0:T(8,128)(2,1)S(1)}, bf16[384,256]{1,0:T(8,128)(2,1)S(1)}, u32[]{:S(2)}, u32[]{:S(2)}) %collective-permute-start.20) | collective-permute-done | bytes 196640 | tf_op jit(solution)/shard_map/gram_over_columns/ppermute | solution.py:55
  73.7 1.3 %collective-permute-start.14 = (bf16[8,192,256]{2,1,0:T(8,128)(2,1)S(1)}, bf16[8,192,256]{2,1,0:T(8,128)(2,1)S(1)}, u32[]{:S(2)}, u32[]{:S(2)}) collective-permute-start(bf16[8,192,256]{2,1,0:T(8,128)(2,1)S(1)} %append.5.refs_0_.refs_4_), channel_id=1, source_target_pairs={{0,64},{1,17},{2,66},{3,19},{4,68},{5,21},{6,70},{7,23},{8,72},{9,... | collective-permute-start | bytes 2359304 | tf_op jit(solution)/shard_map/gram_over_columns/moment_gather/ppermute | solution.py:55
  75.1 5.1 %newton_schulz.1.refs_0_ = bf16[384,256]{1,0:T(8,128)(2,1)S(1)} custom-call(f32[384,384]{1,0:T(8,128)S(1)} %gram.7.mine_ref, f32[384,384]{1,0:T(8,128)S(1)} %collective-permute-done.22.other_ref, bf16[384,256]{1,0:T(8,128)(2,1)S(1)} %get-tuple-element.18.refs_0_.direction_ref), custom_call_target="tpu_custom_call" | custom-call | flops 7516192768 | bytes 2097152 | tf_op jit(solution)/shard_map/newton_schulz/pallas_call | solution.py:270
  80.1 1.4 %collective-permute-start.23 = (bf16[384,256]{1,0:T(8,128)(2,1)S(1)}, bf16[384,256]{1,0:T(8,128)(2,1)S(1)}, u32[]{:S(2)}, u32[]{:S(2)}) collective-permute-start(bf16[384,256]{1,0:T(8,128)(2,1)S(1)} %newton_schulz.1.refs_0_), channel_id=1, source_target_pairs={{0,48},{1,193},{2,50},{3,195},{4,52},{5,197},{6,54},{7,199},{8,56}... | collective-permute-start | bytes 589832 | tf_op jit(solution)/shard_map/update_gather/ppermute | solution.py:55
  81.6 3.3 %collective-permute-start.25 = (bf16[384,256]{1,0:T(8,128)(2,1)S(1)}, bf16[384,256]{1,0:T(8,128)(2,1)S(1)}, u32[]{:S(2)}, u32[]{:S(2)}) collective-permute-start(bf16[384,256]{1,0:T(8,128)(2,1)S(1)} %newton_schulz.1.refs_0_), channel_id=1, source_target_pairs={{0,32},{1,129},{2,34},{3,131},{4,36},{5,133},{6,38},{7,135},{8,40}... | collective-permute-start | bytes 589832 | tf_op jit(solution)/shard_map/update_gather/ppermute | solution.py:55
  84.9 2.5 %collective-permute-done.23.refs_1_ = bf16[384,256]{1,0:T(8,128)(2,1)S(1)} collective-permute-done((bf16[384,256]{1,0:T(8,128)(2,1)S(1)}, bf16[384,256]{1,0:T(8,128)(2,1)S(1)}, u32[]{:S(2)}, u32[]{:S(2)}) %collective-permute-start.23) | collective-permute-done | bytes 196640 | tf_op jit(solution)/shard_map/update_gather/ppermute | solution.py:55
  87.4 3.3 %collective-permute-done.25.refs_3_ = bf16[384,256]{1,0:T(8,128)(2,1)S(1)} collective-permute-done((bf16[384,256]{1,0:T(8,128)(2,1)S(1)}, bf16[384,256]{1,0:T(8,128)(2,1)S(1)}, u32[]{:S(2)}, u32[]{:S(2)}) %collective-permute-start.25) | collective-permute-done | bytes 196640 | tf_op jit(solution)/shard_map/update_gather/ppermute | solution.py:55
  90.7 1.7 %collective-permute-start.28 = (bf16[4,192,256]{2,1,0:T(8,128)(2,1)S(1)}, bf16[4,192,256]{2,1,0:T(8,128)(2,1)S(1)}, u32[]{:S(2)}, u32[]{:S(2)}) collective-permute-start(bf16[4,192,256]{2,1,0:T(8,128)(2,1)S(1)} %get-tuple-element.17.first_ref), channel_id=1, source_target_pairs={{0,192},{1,49},{2,194},{3,51},{4,196},{5,53},{6,198},{7,55},{8,200... | collective-permute-start | bytes 1179656 | tf_op jit(solution)/shard_map/update_gather/ppermute | solution.py:55
  93.2 5.4 %collective-permute-done.28.second_ref = bf16[4,192,256]{2,1,0:T(8,128)(2,1)S(1)} collective-permute-done((bf16[4,192,256]{2,1,0:T(8,128)(2,1)S(1)}, bf16[4,192,256]{2,1,0:T(8,128)(2,1)S(1)}, u32[]{:S(2)}, u32[]{:S(2)}) %collective-permute-start.28) | collective-permute-done | bytes 393248 | tf_op jit(solution)/shard_map/update_gather/ppermute | solution.py:55
  98.7 2.7 %collective-permute-start.29 = (bf16[8,192,256]{2,1,0:T(8,128)(2,1)S(1)}, bf16[8,192,256]{2,1,0:T(8,128)(2,1)S(1)}, u32[]{:S(2)}, u32[]{:S(2)}) collective-permute-start(bf16[8,192,256]{2,1,0:T(8,128)(2,1)S(1)} %append.7.refs_0_), channel_id=1, source_target_pairs={{0,64},{1,17},{2,66},{3,19},{4,68},{5,21},{6,70},{7,23},{8,72},{9,... | collective-permute-start | bytes 2359304 | tf_op jit(solution)/shard_map/update_gather/ppermute | solution.py:55
  106.4 4.9 %collective-permute-done.29.refs_0_ = bf16[8,192,256]{2,1,0:T(8,128)(2,1)S(1)} collective-permute-done((bf16[8,192,256]{2,1,0:T(8,128)(2,1)S(1)}, bf16[8,192,256]{2,1,0:T(8,128)(2,1)S(1)}, u32[]{:S(2)}, u32[]{:S(2)}) %collective-permute-start.29) | collective-permute-done | bytes 786464 | tf_op jit(solution)/shard_map/update_gather/ppermute | solution.py:55
  (62 shorter events, 23.0 us)
Async XLA Ops:
  0.6 1.9 %copy-start.1 = (bf16[1,16,384,256]{3,2,1,0:T(8,128)(2,1)S(1)}, bf16[1,16,384,256]{3,2,1,0:T(8,128)(2,1)}, u32[]{:S(2)}) copy-start(bf16[1,16,384,256]{3,2,1,0:T(8,128)(2,1)} %param.3) | copy-start | bytes 9437188
  3.9 12.1 %collective-permute-start.2 = (bf16[8,192,256]{2,1,0:T(8,128)(2,1)S(1)}, bf16[8,192,256]{2,1,0:T(8,128)(2,1)S(1)}, u32[]{:S(2)}, u32[]{:S(2)}) collective-permute-start(bf16[8,192,256]{2,1,0:T(8,128)(2,1)S(1)} %get-tuple-element.13), channel_id=1, source_target_pairs={{0,192},{1,49},{2,194},{3,51},{4,196},{5,53},{6,198},{7,55},{8,200... | collective-permute-start | bytes 2359304 | tf_op jit(solution)/shard_map/sum_over_replicas/ppermute | solution.py:55
  5.4 14.3 %collective-permute-start = (bf16[8,192,256]{2,1,0:T(8,128)(2,1)S(1)}, bf16[8,192,256]{2,1,0:T(8,128)(2,1)S(1)}, u32[]{:S(2)}, u32[]{:S(2)}) collective-permute-start(bf16[8,192,256]{2,1,0:T(8,128)(2,1)S(1)} %get-tuple-element.11), channel_id=1, source_target_pairs={{0,64},{1,17},{2,66},{3,19},{4,68},{5,21},{6,70},{7,23},{8,72},{9,... | collective-permute-start | bytes 2359304 | tf_op jit(solution)/shard_map/sum_over_replicas/ppermute | solution.py:55
  16.1 9.3 %collective-permute-start.3 = (bf16[4,192,256]{2,1,0:T(8,128)(2,1)S(1)}, bf16[4,192,256]{2,1,0:T(8,128)(2,1)S(1)}, u32[]{:S(2)}, u32[]{:S(2)}) collective-permute-start(bf16[4,192,256]{2,1,0:T(8,128)(2,1)S(1)} %get-tuple-element.22), channel_id=1, source_target_pairs={{0,64},{1,17},{2,66},{3,19},{4,68},{5,21},{6,70},{7,23},{8,72},{9,... | collective-permute-start | bytes 1179656 | tf_op jit(solution)/shard_map/sum_over_replicas/ppermute | solution.py:55
  19.9 7.9 %collective-permute-start.1 = (bf16[4,192,256]{2,1,0:T(8,128)(2,1)S(1)}, bf16[4,192,256]{2,1,0:T(8,128)(2,1)S(1)}, u32[]{:S(2)}, u32[]{:S(2)}) collective-permute-start(bf16[4,192,256]{2,1,0:T(8,128)(2,1)S(1)} %get-tuple-element.20), channel_id=1, source_target_pairs={{0,192},{1,49},{2,194},{3,51},{4,196},{5,53},{6,198},{7,55},{8,200... | collective-permute-start | bytes 1179656 | tf_op jit(solution)/shard_map/sum_over_replicas/ppermute | solution.py:55
  27.9 7.3 %collective-permute-start.6 = (bf16[384,256]{1,0:T(8,128)(2,1)S(1)}, bf16[384,256]{1,0:T(8,128)(2,1)S(1)}, u32[]{:S(2)}, u32[]{:S(2)}) collective-permute-start(bf16[384,256]{1,0:T(8,128)(2,1)S(1)} %pad_maximum_fusion.2), channel_id=1, source_target_pairs={{0,32},{1,129},{2,34},{3,131},{4,36},{5,133},{6,38},{7,135},{8,40}... | collective-permute-start | bytes 589832 | tf_op jit(solution)/shard_map/sum_over_replicas/ppermute | solution.py:55
  29.5 6.4 %collective-permute-start.5 = (bf16[384,256]{1,0:T(8,128)(2,1)S(1)}, bf16[384,256]{1,0:T(8,128)(2,1)S(1)}, u32[]{:S(2)}, u32[]{:S(2)}) collective-permute-start(bf16[384,256]{1,0:T(8,128)(2,1)S(1)} %pad_maximum_fusion.1), channel_id=1, source_target_pairs={{0,16},{1,65},{2,18},{3,67},{4,20},{5,69},{6,22},{7,71},{8,24},{9,... | collective-permute-start | bytes 589832 | tf_op jit(solution)/shard_map/sum_over_replicas/ppermute | solution.py:55
  30.3 7.0 %collective-permute-start.4 = (bf16[384,256]{1,0:T(8,128)(2,1)S(1)}, bf16[384,256]{1,0:T(8,128)(2,1)S(1)}, u32[]{:S(2)}, u32[]{:S(2)}) collective-permute-start(bf16[384,256]{1,0:T(8,128)(2,1)S(1)} %pad_maximum_fusion), channel_id=1, source_target_pairs={{0,48},{1,193},{2,50},{3,195},{4,52},{5,197},{6,54},{7,199},{8,56}... | collective-permute-start | bytes 589832 | tf_op jit(solution)/shard_map/sum_over_replicas/ppermute | solution.py:55
  38.4 2.1 %collective-permute-start.7 = (bf16[384,256]{1,0:T(8,128)(2,1)S(1)}, bf16[384,256]{1,0:T(8,128)(2,1)S(1)}, u32[]{:S(2)}, u32[]{:S(2)}) collective-permute-start(bf16[384,256]{1,0:T(8,128)(2,1)S(1)} %get-tuple-element.18.refs_0_.direction_ref), channel_id=1, source_target_pairs={{0,1},{1,0},{2,3},{3,2},{4,5},{5,4},{6,7},{7,6},{8,9},{9,8},{10,11... | collective-permute-start | bytes 589832 | tf_op jit(solution)/shard_map/gram_over_columns/ppermute | solution.py:55
  38.5 9.6 %collective-permute-start.15 = (bf16[384,256]{1,0:T(8,128)(2,1)S(1)}, bf16[384,256]{1,0:T(8,128)(2,1)S(1)}, u32[]{:S(2)}, u32[]{:S(2)}) collective-permute-start(bf16[384,256]{1,0:T(8,128)(2,1)S(1)} %get-tuple-element.18.refs_0_.direction_ref), channel_id=1, source_target_pairs={{0,2},{1,15},{2,4},{3,1},{4,6},{5,3},{6,8},{7,5},{8,10},{9,7},{10,... | collective-permute-start | bytes 589832 | tf_op jit(solution)/shard_map/gram_over_columns/ppermute | solution.py:55
  40.5 8.6 %collective-permute-start.8 = (bf16[384,256]{1,0:T(8,128)(2,1)S(1)}, bf16[384,256]{1,0:T(8,128)(2,1)S(1)}, u32[]{:S(2)}, u32[]{:S(2)}) collective-permute-start(bf16[384,256]{1,0:T(8,128)(2,1)S(1)} %bitcast.25), channel_id=1, source_target_pairs={{0,48},{1,193},{2,50},{3,195},{4,52},{5,197},{6,54},{7,199},{8,56}... | collective-permute-start | bytes 589832 | tf_op jit(solution)/shard_map/gram_over_columns/moment_gather/ppermute | solution.py:55
  41.9 7.2 %collective-permute-start.9 = (bf16[384,256]{1,0:T(8,128)(2,1)S(1)}, bf16[384,256]{1,0:T(8,128)(2,1)S(1)}, u32[]{:S(2)}, u32[]{:S(2)}) collective-permute-start(bf16[384,256]{1,0:T(8,128)(2,1)S(1)} %bitcast.26), channel_id=1, source_target_pairs={{0,16},{1,65},{2,18},{3,67},{4,20},{5,69},{6,22},{7,71},{8,24},{9,... | collective-permute-start | bytes 589832 | tf_op jit(solution)/shard_map/gram_over_columns/moment_gather/ppermute | solution.py:55
  42.1 9.0 %collective-permute-start.10 = (bf16[384,256]{1,0:T(8,128)(2,1)S(1)}, bf16[384,256]{1,0:T(8,128)(2,1)S(1)}, u32[]{:S(2)}, u32[]{:S(2)}) collective-permute-start(bf16[384,256]{1,0:T(8,128)(2,1)S(1)} %bitcast.27), channel_id=1, source_target_pairs={{0,32},{1,129},{2,34},{3,131},{4,36},{5,133},{6,38},{7,135},{8,40}... | collective-permute-start | bytes 589832 | tf_op jit(solution)/shard_map/gram_over_columns/moment_gather/ppermute | solution.py:55
  45.3 9.2 %collective-permute-start.18 = (bf16[384,256]{1,0:T(8,128)(2,1)S(1)}, bf16[384,256]{1,0:T(8,128)(2,1)S(1)}, u32[]{:S(2)}, u32[]{:S(2)}) collective-permute-start(bf16[384,256]{1,0:T(8,128)(2,1)S(1)} %collective-permute-done.7.refs_1_), channel_id=1, source_target_pairs={{0,2},{1,15},{2,4},{3,1},{4,6},{5,3},{6,8},{7,5},{8,10},{9,7},{10,... | collective-permute-start | bytes 589832 | tf_op jit(solution)/shard_map/gram_over_columns/ppermute | solution.py:55
  48.1 8.3 %collective-permute-start.16 = (bf16[384,256]{1,0:T(8,128)(2,1)S(1)}, bf16[384,256]{1,0:T(8,128)(2,1)S(1)}, u32[]{:S(2)}, u32[]{:S(2)}) collective-permute-start(bf16[384,256]{1,0:T(8,128)(2,1)S(1)} %collective-permute-done.15.refs_0_), channel_id=1, source_target_pairs={{0,2},{1,15},{2,4},{3,1},{4,6},{5,3},{6,8},{7,5},{8,10},{9,7},{10,... | collective-permute-start | bytes 589832 | tf_op jit(solution)/shard_map/gram_over_columns/ppermute | solution.py:55
  51.1 13.4 %collective-permute-start.11 = (bf16[4,192,256]{2,1,0:T(8,128)(2,1)S(1)}, bf16[4,192,256]{2,1,0:T(8,128)(2,1)S(1)}, u32[]{:S(2)}, u32[]{:S(2)}) collective-permute-start(bf16[4,192,256]{2,1,0:T(8,128)(2,1)S(1)} %get-tuple-element.14.first_ref.refs_4_), channel_id=1, source_target_pairs={{0,64},{1,17},{2,66},{3,19},{4,68},{5,21},{6,70},{7,23},{8,72},{9,... | collective-permute-start | bytes 1179656 | tf_op jit(solution)/shard_map/gram_over_columns/moment_gather/ppermute | solution.py:55
  53.5 11.0 %collective-permute-start.13 = (bf16[4,192,256]{2,1,0:T(8,128)(2,1)S(1)}, bf16[4,192,256]{2,1,0:T(8,128)(2,1)S(1)}, u32[]{:S(2)}, u32[]{:S(2)}) collective-permute-start(bf16[4,192,256]{2,1,0:T(8,128)(2,1)S(1)} %get-tuple-element.15.first_ref.refs_3_), channel_id=1, source_target_pairs={{0,192},{1,49},{2,194},{3,51},{4,196},{5,53},{6,198},{7,55},{8,200... | collective-permute-start | bytes 1179656 | tf_op jit(solution)/shard_map/gram_over_columns/moment_gather/ppermute | solution.py:55
  54.5 8.9 %collective-permute-start.19 = (bf16[384,256]{1,0:T(8,128)(2,1)S(1)}, bf16[384,256]{1,0:T(8,128)(2,1)S(1)}, u32[]{:S(2)}, u32[]{:S(2)}) collective-permute-start(bf16[384,256]{1,0:T(8,128)(2,1)S(1)} %collective-permute-done.18.refs_1_), channel_id=1, source_target_pairs={{0,2},{1,15},{2,4},{3,1},{4,6},{5,3},{6,8},{7,5},{8,10},{9,7},{10,... | collective-permute-start | bytes 589832 | tf_op jit(solution)/shard_map/gram_over_columns/ppermute | solution.py:55
  56.4 9.1 %collective-permute-start.17 = (bf16[384,256]{1,0:T(8,128)(2,1)S(1)}, bf16[384,256]{1,0:T(8,128)(2,1)S(1)}, u32[]{:S(2)}, u32[]{:S(2)}) collective-permute-start(bf16[384,256]{1,0:T(8,128)(2,1)S(1)} %collective-permute-done.16.refs_0_), channel_id=1, source_target_pairs={{0,2},{1,15},{2,4},{3,1},{4,6},{5,3},{6,8},{7,5},{8,10},{9,7},{10,... | collective-permute-start | bytes 589832 | tf_op jit(solution)/shard_map/gram_over_columns/ppermute | solution.py:55
  58.3 11.3 %collective-permute-start.21 = (bf16[384,256]{1,0:T(8,128)(2,1)S(1)}, bf16[384,256]{1,0:T(8,128)(2,1)S(1)}, u32[]{:S(2)}, u32[]{:S(2)}) collective-permute-start(bf16[384,256]{1,0:T(8,128)(2,1)S(1)} %collective-permute-done.16.refs_0_), channel_id=1, source_target_pairs={{0,4},{1,13},{2,6},{3,15},{4,8},{5,1},{6,10},{7,3},{8,12},{9,5},{1... | collective-permute-start | bytes 589832 | tf_op jit(solution)/shard_map/gram_over_columns/ppermute | solution.py:55
  63.4 8.6 %collective-permute-start.20 = (bf16[384,256]{1,0:T(8,128)(2,1)S(1)}, bf16[384,256]{1,0:T(8,128)(2,1)S(1)}, u32[]{:S(2)}, u32[]{:S(2)}) collective-permute-start(bf16[384,256]{1,0:T(8,128)(2,1)S(1)} %collective-permute-done.19.refs_1_), channel_id=1, source_target_pairs={{0,2},{1,15},{2,4},{3,1},{4,6},{5,3},{6,8},{7,5},{8,10},{9,7},{10,... | collective-permute-start | bytes 589832 | tf_op jit(solution)/shard_map/gram_over_columns/ppermute | solution.py:55
  72.5 2.6 %collective-permute-start.22 = (f32[384,384]{1,0:T(8,128)S(1)}, f32[384,384]{1,0:T(8,128)S(1)}, u32[]{:S(2)}, u32[]{:S(2)}) collective-permute-start(f32[384,384]{1,0:T(8,128)S(1)} %gram.7.mine_ref), channel_id=1, source_target_pairs={{0,1},{1,0},{2,3},{3,2},{4,5},{5,4},{6,7},{7,6},{8,9},{9,8},{10,11... | collective-permute-start | bytes 1769480 | tf_op jit(solution)/shard_map/gram_over_columns/ppermute | solution.py:55
  72.6 20.7 %collective-permute-start.12 = (bf16[8,192,256]{2,1,0:T(8,128)(2,1)S(1)}, bf16[8,192,256]{2,1,0:T(8,128)(2,1)S(1)}, u32[]{:S(2)}, u32[]{:S(2)}) collective-permute-start(bf16[8,192,256]{2,1,0:T(8,128)(2,1)S(1)} %append.4.refs_1_.refs_5_), channel_id=1, source_target_pairs={{0,192},{1,49},{2,194},{3,51},{4,196},{5,53},{6,198},{7,55},{8,200... | collective-permute-start | bytes 2359304 | tf_op jit(solution)/shard_map/gram_over_columns/moment_gather/ppermute | solution.py:55
  73.7 19.5 %collective-permute-start.14 = (bf16[8,192,256]{2,1,0:T(8,128)(2,1)S(1)}, bf16[8,192,256]{2,1,0:T(8,128)(2,1)S(1)}, u32[]{:S(2)}, u32[]{:S(2)}) collective-permute-start(bf16[8,192,256]{2,1,0:T(8,128)(2,1)S(1)} %append.5.refs_0_.refs_4_), channel_id=1, source_target_pairs={{0,64},{1,17},{2,66},{3,19},{4,68},{5,21},{6,70},{7,23},{8,72},{9,... | collective-permute-start | bytes 2359304 | tf_op jit(solution)/shard_map/gram_over_columns/moment_gather/ppermute | solution.py:55
  80.1 7.2 %collective-permute-start.23 = (bf16[384,256]{1,0:T(8,128)(2,1)S(1)}, bf16[384,256]{1,0:T(8,128)(2,1)S(1)}, u32[]{:S(2)}, u32[]{:S(2)}) collective-permute-start(bf16[384,256]{1,0:T(8,128)(2,1)S(1)} %newton_schulz.1.refs_0_), channel_id=1, source_target_pairs={{0,48},{1,193},{2,50},{3,195},{4,52},{5,197},{6,54},{7,199},{8,56}... | collective-permute-start | bytes 589832 | tf_op jit(solution)/shard_map/update_gather/ppermute | solution.py:55
  81.6 5.8 %collective-permute-start.24 = (bf16[384,256]{1,0:T(8,128)(2,1)S(1)}, bf16[384,256]{1,0:T(8,128)(2,1)S(1)}, u32[]{:S(2)}, u32[]{:S(2)}) collective-permute-start(bf16[384,256]{1,0:T(8,128)(2,1)S(1)} %newton_schulz.1.refs_0_), channel_id=1, source_target_pairs={{0,16},{1,65},{2,18},{3,67},{4,20},{5,69},{6,22},{7,71},{8,24},{9,... | collective-permute-start | bytes 589832 | tf_op jit(solution)/shard_map/update_gather/ppermute | solution.py:55
  81.6 9.1 %collective-permute-start.25 = (bf16[384,256]{1,0:T(8,128)(2,1)S(1)}, bf16[384,256]{1,0:T(8,128)(2,1)S(1)}, u32[]{:S(2)}, u32[]{:S(2)}) collective-permute-start(bf16[384,256]{1,0:T(8,128)(2,1)S(1)} %newton_schulz.1.refs_0_), channel_id=1, source_target_pairs={{0,32},{1,129},{2,34},{3,131},{4,36},{5,133},{6,38},{7,135},{8,40}... | collective-permute-start | bytes 589832 | tf_op jit(solution)/shard_map/update_gather/ppermute | solution.py:55
  90.7 7.9 %collective-permute-start.28 = (bf16[4,192,256]{2,1,0:T(8,128)(2,1)S(1)}, bf16[4,192,256]{2,1,0:T(8,128)(2,1)S(1)}, u32[]{:S(2)}, u32[]{:S(2)}) collective-permute-start(bf16[4,192,256]{2,1,0:T(8,128)(2,1)S(1)} %get-tuple-element.17.first_ref), channel_id=1, source_target_pairs={{0,192},{1,49},{2,194},{3,51},{4,196},{5,53},{6,198},{7,55},{8,200... | collective-permute-start | bytes 1179656 | tf_op jit(solution)/shard_map/update_gather/ppermute | solution.py:55
  92.4 8.9 %collective-permute-start.26 = (bf16[4,192,256]{2,1,0:T(8,128)(2,1)S(1)}, bf16[4,192,256]{2,1,0:T(8,128)(2,1)S(1)}, u32[]{:S(2)}, u32[]{:S(2)}) collective-permute-start(bf16[4,192,256]{2,1,0:T(8,128)(2,1)S(1)} %get-tuple-element.16.first_ref), channel_id=1, source_target_pairs={{0,64},{1,17},{2,66},{3,19},{4,68},{5,21},{6,70},{7,23},{8,72},{9,... | collective-permute-start | bytes 1179656 | tf_op jit(solution)/shard_map/update_gather/ppermute | solution.py:55
  98.7 12.7 %collective-permute-start.29 = (bf16[8,192,256]{2,1,0:T(8,128)(2,1)S(1)}, bf16[8,192,256]{2,1,0:T(8,128)(2,1)S(1)}, u32[]{:S(2)}, u32[]{:S(2)}) collective-permute-start(bf16[8,192,256]{2,1,0:T(8,128)(2,1)S(1)} %append.7.refs_0_), channel_id=1, source_target_pairs={{0,64},{1,17},{2,66},{3,19},{4,68},{5,21},{6,70},{7,23},{8,72},{9,... | collective-permute-start | bytes 2359304 | tf_op jit(solution)/shard_map/update_gather/ppermute | solution.py:55
  101.4 12.1 %collective-permute-start.27 = (bf16[8,192,256]{2,1,0:T(8,128)(2,1)S(1)}, bf16[8,192,256]{2,1,0:T(8,128)(2,1)S(1)}, u32[]{:S(2)}, u32[]{:S(2)}) collective-permute-start(bf16[8,192,256]{2,1,0:T(8,128)(2,1)S(1)} %append.6.refs_1_), channel_id=1, source_target_pairs={{0,192},{1,49},{2,194},{3,51},{4,196},{5,53},{6,198},{7,55},{8,200... | collective-permute-start | bytes 2359304 | tf_op jit(solution)/shard_map/update_gather/ppermute | solution.py:55
  106.4 7.1 %copy-start = (bf16[16,384,256]{2,1,0:T(8,128)(2,1)S(1)}, bf16[16,384,256]{2,1,0:T(8,128)(2,1)}, u32[]{:S(2)}) copy-start(bf16[16,384,256]{2,1,0:T(8,128)(2,1)} %assemble.8.refs_2_) | copy-start | bytes 9437188
  (1 other events, 0.7 us)

commit v6 on v5

--- a/solution.py
+++ b/solution.py
@@ -87,37 +87,48 @@
     return cube_device(cube_place(lax.axis_index("dp"), core) ^ relative, core)
 
 
-def pack_kernel(places, slot_ref, gradients_ref, *out_refs):
+def pack_kernel(places, slot_ref, gradients_ref, *refs):
+    own = None
+    if len(refs) > len(places):
+        momentum_ref, *out_refs, own_ref, sem = refs
+        own = pltpu.make_async_copy(momentum_ref.at[lax.axis_index("dp")], own_ref, sem)
+        own.start()
+    else:
+        out_refs = refs
     for part, (out_ref, own_places) in enumerate(zip(out_refs, places)):
         for i, place in enumerate(own_places):
             slot = slot_ref[kernel_device(place)]
             out_ref[i] = gradients_ref[slot, part * HALF : (part + 1) * HALF]
-
-
-def pack(bucket_slot, gradients, places):
+    if own is not None:
+        own.wait()
+
+
+def pack(bucket_slot, gradients, places, momentum=()):
     width = gradients.shape[-1]
     count = sum(len(p) for p in places)
     return pl.pallas_call(
         functools.partial(pack_kernel, places),
-        out_shape=[jax.ShapeDtypeStruct((len(p), HALF, width), BF16) for p in places],
-        in_specs=[pl.BlockSpec(memory_space=pltpu.SMEM)] + vmem(1),
-        out_specs=vmem(2),
+        out_shape=[jax.ShapeDtypeStruct((len(p), HALF, width), BF16) for p in places]
+        + [jax.ShapeDtypeStruct(m.shape[1:], m.dtype) for m in momentum],
+        in_specs=[pl.BlockSpec(memory_space=pltpu.SMEM)] + vmem(1) + anywhere(len(momentum)),
+        out_specs=vmem(2 + len(momentum)),
+        scratch_shapes=[pltpu.SemaphoreType.DMA] * len(momentum),
         compiler_params=pltpu.CompilerParams(vmem_limit_bytes=16 * 1024 * 1024),
         cost_estimate=pl.CostEstimate(
             flops=0, bytes_accessed=2 * count * HALF * width * 2, transcendentals=0
         ),
         name="pack",
-    )(bucket_slot, gradients)
-
-
-def reduce_scatter(gradients, bucket_slot, sizes):
+    )(bucket_slot, gradients, *momentum)
+
+
+def reduce_scatter(gradients, momentum, bucket_slot, sizes):
     away = [places_of(first) + places_of(first, second) for first, second in HEADS]
     kept = [places_of() + places_of(second) for _, second in HEADS]
     received = [
         send(v, cube_pairs(sizes, first))
         for v, (first, _) in zip(pack(bucket_slot, gradients, away), HEADS)
     ]
-    kept = pack(bucket_slot, gradients, kept)
+    *kept, own = pack(bucket_slot, gradients, kept, [momentum])
     sent = [(m[4:].astype(F32) + o[4:].astype(F32)).astype(BF16) for m, o in zip(kept, received)]
     kept = [m[:4].astype(F32) + o[:4].astype(F32) for m, o in zip(kept, received)]
     received = [send(v, cube_pairs(sizes, second)) for v, (_, second) in zip(sent, HEADS)]
@@ -125,7 +136,7 @@
     for i in range(1, 4):
         block = [(m[i] + o[i].astype(F32)).astype(BF16) for m, o in zip(kept, received)]
         total = total + send(jnp.concatenate(block), cube_pairs(sizes, *TAIL[i])).astype(F32)
-    return total
+    return total, own
 
 
 def assemble_kernel(places, *refs):
@@ -307,13 +318,12 @@
 
 
 def per_device(sizes, gradients, momentum, bucket_slot):
-    dp = lax.axis_index("dp")
     replicas, owners = sizes
     chips = owners // 2
     with jax.named_scope("sum_over_replicas"):
-        total = reduce_scatter(gradients[0], bucket_slot, sizes)
+        total, own = reduce_scatter(gradients[0], momentum, bucket_slot, sizes)
     average = total / replicas
-    own = lax.dynamic_index_in_dim(momentum, dp, 0, keepdims=False).astype(F32)
+    own = own.astype(F32)
     moment = (momentum_decay * own + average).astype(BF16)
     direction = (average + momentum_decay * moment.astype(F32)).astype(BF16)
     swap = all_pairs(sizes, lambda x, y, z, c: (x, y, z, 1 - c))

time: 115 us -> 114 us (level)
    unnamed x6 -> x8, local copies, waits for them, and re-layouts: 2.54 us -> 2.55 us
where the time goes in v6:
time: 114 us
  waiting for transfers between devices  48.6 us (43%)
  starting transfers between devices  45.8 us (40%)
  Pallas kernels  14.9 us (13%)
  local copies, waits for them, and re-layouts  2.55 us (2%)
    ppermute x30, waiting for transfers between devices, send(): return lax.ppermute(value, ('dp', 'zero'), pairs)  48.6 us
    ppermute x30, starting transfers between devices, send(): return lax.ppermute(value, ('dp', 'zero'), pairs)  45.8 us
    pallas_call x6, Pallas kernels, assemble(): pl.pallas_call(functools.partial(assemble_kernel, places), out_shape=jax....  6.35 us
    pallas_call x1, Pallas kernels, newton_schulz(): pl.pallas_call(newton_schulz_kernel, out_shape=jax.ShapeDtypeStruct(direc...  5.09 us
    unnamed x8, local copies, waits for them, and re-layouts  2.55 us
  transfers between devices with their start and end apart: 30, of which 17 were waited for; matrix products, arithmetic and copies ran while one was open for 0% of the time, Pallas kernels for 11%

profile of v6, /device:TPU:2, one launch (start us, length us, event | category | flops | bytes accessed | tf_op | source)
XLA Modules:
  0.0 113.7 jit_solution(16377722602301888292)
XLA Ops:
  0.6 1.9 %copy-done.1 = bf16[1,16,384,256]{3,2,1,0:T(8,128)(2,1)S(1)} copy-done((bf16[1,16,384,256]{3,2,1,0:T(8,128)(2,1)S(1)}, bf16[1,16,384,256]{3,2,1,0:T(8,128)(2,1)}, u32[]{:S(2)}) %copy-start.1) | copy-done | bytes 3145752
  3.9 1.6 %collective-permute-start.2 = (bf16[8,192,256]{2,1,0:T(8,128)(2,1)S(1)}, bf16[8,192,256]{2,1,0:T(8,128)(2,1)S(1)}, u32[]{:S(2)}, u32[]{:S(2)}) collective-permute-start(bf16[8,192,256]{2,1,0:T(8,128)(2,1)S(1)} %get-tuple-element.15), channel_id=1, source_target_pairs={{0,192},{1,49},{2,194},{3,51},{4,196},{5,53},{6,198},{7,55},{8,200... | collective-permute-start | bytes 2359304 | tf_op jit(solution)/shard_map/sum_over_replicas/ppermute | solution.py:55
  5.4 1.8 %collective-permute-start = (bf16[8,192,256]{2,1,0:T(8,128)(2,1)S(1)}, bf16[8,192,256]{2,1,0:T(8,128)(2,1)S(1)}, u32[]{:S(2)}, u32[]{:S(2)}) collective-permute-start(bf16[8,192,256]{2,1,0:T(8,128)(2,1)S(1)} %get-tuple-element.13), channel_id=1, source_target_pairs={{0,64},{1,17},{2,66},{3,19},{4,68},{5,21},{6,70},{7,23},{8,72},{9,... | collective-permute-start | bytes 2359304 | tf_op jit(solution)/shard_map/sum_over_replicas/ppermute | solution.py:55
  8.2 7.8 %collective-permute-done.2 = bf16[8,192,256]{2,1,0:T(8,128)(2,1)S(1)} collective-permute-done((bf16[8,192,256]{2,1,0:T(8,128)(2,1)S(1)}, bf16[8,192,256]{2,1,0:T(8,128)(2,1)S(1)}, u32[]{:S(2)}, u32[]{:S(2)}) %collective-permute-start.2) | collective-permute-done | bytes 786464 | tf_op jit(solution)/shard_map/sum_over_replicas/ppermute | solution.py:55
  16.1 3.6 %collective-permute-start.3 = (bf16[4,192,256]{2,1,0:T(8,128)(2,1)S(1)}, bf16[4,192,256]{2,1,0:T(8,128)(2,1)S(1)}, u32[]{:S(2)}, u32[]{:S(2)}) collective-permute-start(bf16[4,192,256]{2,1,0:T(8,128)(2,1)S(1)} %get-tuple-element.22), channel_id=1, source_target_pairs={{0,64},{1,17},{2,66},{3,19},{4,68},{5,21},{6,70},{7,23},{8,72},{9,... | collective-permute-start | bytes 1179656 | tf_op jit(solution)/shard_map/sum_over_replicas/ppermute | solution.py:55
  20.4 5.1 %collective-permute-done.3 = bf16[4,192,256]{2,1,0:T(8,128)(2,1)S(1)} collective-permute-done((bf16[4,192,256]{2,1,0:T(8,128)(2,1)S(1)}, bf16[4,192,256]{2,1,0:T(8,128)(2,1)S(1)}, u32[]{:S(2)}, u32[]{:S(2)}) %collective-permute-start.3) | collective-permute-done | bytes 393248 | tf_op jit(solution)/shard_map/sum_over_replicas/ppermute | solution.py:55
  25.6 2.2 %collective-permute-done.1 = bf16[4,192,256]{2,1,0:T(8,128)(2,1)S(1)} collective-permute-done((bf16[4,192,256]{2,1,0:T(8,128)(2,1)S(1)}, bf16[4,192,256]{2,1,0:T(8,128)(2,1)S(1)}, u32[]{:S(2)}, u32[]{:S(2)}) %collective-permute-start.1) | collective-permute-done | bytes 393248 | tf_op jit(solution)/shard_map/sum_over_replicas/ppermute | solution.py:55
  27.9 1.7 %collective-permute-start.6 = (bf16[384,256]{1,0:T(8,128)(2,1)S(1)}, bf16[384,256]{1,0:T(8,128)(2,1)S(1)}, u32[]{:S(2)}, u32[]{:S(2)}) collective-permute-start(bf16[384,256]{1,0:T(8,128)(2,1)S(1)} %pad_maximum_fusion.2), channel_id=1, source_target_pairs={{0,32},{1,129},{2,34},{3,131},{4,36},{5,133},{6,38},{7,135},{8,40}... | collective-permute-start | bytes 589832 | tf_op jit(solution)/shard_map/sum_over_replicas/ppermute | solution.py:55
  30.4 1.9 %collective-permute-start.4 = (bf16[384,256]{1,0:T(8,128)(2,1)S(1)}, bf16[384,256]{1,0:T(8,128)(2,1)S(1)}, u32[]{:S(2)}, u32[]{:S(2)}) collective-permute-start(bf16[384,256]{1,0:T(8,128)(2,1)S(1)} %pad_maximum_fusion), channel_id=1, source_target_pairs={{0,48},{1,193},{2,50},{3,195},{4,52},{5,197},{6,54},{7,199},{8,56}... | collective-permute-start | bytes 589832 | tf_op jit(solution)/shard_map/sum_over_replicas/ppermute | solution.py:55
  32.3 2.9 %collective-permute-done.6 = bf16[384,256]{1,0:T(8,128)(2,1)S(1)} collective-permute-done((bf16[384,256]{1,0:T(8,128)(2,1)S(1)}, bf16[384,256]{1,0:T(8,128)(2,1)S(1)}, u32[]{:S(2)}, u32[]{:S(2)}) %collective-permute-start.6) | collective-permute-done | bytes 196640 | tf_op jit(solution)/shard_map/sum_over_replicas/ppermute | solution.py:55
  36.0 1.3 %collective-permute-done.4 = bf16[384,256]{1,0:T(8,128)(2,1)S(1)} collective-permute-done((bf16[384,256]{1,0:T(8,128)(2,1)S(1)}, bf16[384,256]{1,0:T(8,128)(2,1)S(1)}, u32[]{:S(2)}, u32[]{:S(2)}) %collective-permute-start.4) | collective-permute-done | bytes 196640 | tf_op jit(solution)/shard_map/sum_over_replicas/ppermute | solution.py:55
  37.6 2.0 %collective-permute-start.15 = (bf16[384,256]{1,0:T(8,128)(2,1)S(1)}, bf16[384,256]{1,0:T(8,128)(2,1)S(1)}, u32[]{:S(2)}, u32[]{:S(2)}) collective-permute-start(bf16[384,256]{1,0:T(8,128)(2,1)S(1)} %get-tuple-element.24.refs_0_.direction_ref), channel_id=1, source_target_pairs={{0,2},{1,15},{2,4},{3,1},{4,6},{5,3},{6,8},{7,5},{8,10},{9,7},{10,... | collective-permute-start | bytes 589832 | tf_op jit(solution)/shard_map/gram_over_columns/ppermute | solution.py:55
  39.6 1.4 %collective-permute-start.8 = (bf16[384,256]{1,0:T(8,128)(2,1)S(1)}, bf16[384,256]{1,0:T(8,128)(2,1)S(1)}, u32[]{:S(2)}, u32[]{:S(2)}) collective-permute-start(bf16[384,256]{1,0:T(8,128)(2,1)S(1)} %bitcast.20), channel_id=1, source_target_pairs={{0,48},{1,193},{2,50},{3,195},{4,52},{5,197},{6,54},{7,199},{8,56}... | collective-permute-start | bytes 589832 | tf_op jit(solution)/shard_map/gram_over_columns/moment_gather/ppermute | solution.py:55
  41.2 3.2 %collective-permute-start.10 = (bf16[384,256]{1,0:T(8,128)(2,1)S(1)}, bf16[384,256]{1,0:T(8,128)(2,1)S(1)}, u32[]{:S(2)}, u32[]{:S(2)}) collective-permute-start(bf16[384,256]{1,0:T(8,128)(2,1)S(1)} %bitcast.22), channel_id=1, source_target_pairs={{0,32},{1,129},{2,34},{3,131},{4,36},{5,133},{6,38},{7,135},{8,40}... | collective-permute-start | bytes 589832 | tf_op jit(solution)/shard_map/gram_over_columns/moment_gather/ppermute | solution.py:55
  44.4 1.9 %collective-permute-start.18 = (bf16[384,256]{1,0:T(8,128)(2,1)S(1)}, bf16[384,256]{1,0:T(8,128)(2,1)S(1)}, u32[]{:S(2)}, u32[]{:S(2)}) collective-permute-start(bf16[384,256]{1,0:T(8,128)(2,1)S(1)} %collective-permute-done.7.refs_1_), channel_id=1, source_target_pairs={{0,2},{1,15},{2,4},{3,1},{4,6},{5,3},{6,8},{7,5},{8,10},{9,7},{10,... | collective-permute-start | bytes 589832 | tf_op jit(solution)/shard_map/gram_over_columns/ppermute | solution.py:55
  48.3 1.9 %collective-permute-done.10.refs_3_ = bf16[384,256]{1,0:T(8,128)(2,1)S(1)} collective-permute-done((bf16[384,256]{1,0:T(8,128)(2,1)S(1)}, bf16[384,256]{1,0:T(8,128)(2,1)S(1)}, u32[]{:S(2)}, u32[]{:S(2)}) %collective-permute-start.10) | collective-permute-done | bytes 196640 | tf_op jit(solution)/shard_map/gram_over_columns/moment_gather/ppermute | solution.py:55
  50.2 2.4 %collective-permute-start.11 = (bf16[4,192,256]{2,1,0:T(8,128)(2,1)S(1)}, bf16[4,192,256]{2,1,0:T(8,128)(2,1)S(1)}, u32[]{:S(2)}, u32[]{:S(2)}) collective-permute-start(bf16[4,192,256]{2,1,0:T(8,128)(2,1)S(1)} %get-tuple-element.16.first_ref.refs_4_), channel_id=1, source_target_pairs={{0,64},{1,17},{2,66},{3,19},{4,68},{5,21},{6,70},{7,23},{8,72},{9,... | collective-permute-start | bytes 1179656 | tf_op jit(solution)/shard_map/gram_over_columns/moment_gather/ppermute | solution.py:55
  53.6 1.9 %collective-permute-start.19 = (bf16[384,256]{1,0:T(8,128)(2,1)S(1)}, bf16[384,256]{1,0:T(8,128)(2,1)S(1)}, u32[]{:S(2)}, u32[]{:S(2)}) collective-permute-start(bf16[384,256]{1,0:T(8,128)(2,1)S(1)} %collective-permute-done.18.refs_1_), channel_id=1, source_target_pairs={{0,2},{1,15},{2,4},{3,1},{4,6},{5,3},{6,8},{7,5},{8,10},{9,7},{10,... | collective-permute-start | bytes 589832 | tf_op jit(solution)/shard_map/gram_over_columns/ppermute | solution.py:55
  55.5 1.9 %collective-permute-start.17 = (bf16[384,256]{1,0:T(8,128)(2,1)S(1)}, bf16[384,256]{1,0:T(8,128)(2,1)S(1)}, u32[]{:S(2)}, u32[]{:S(2)}) collective-permute-start(bf16[384,256]{1,0:T(8,128)(2,1)S(1)} %collective-permute-done.16.refs_0_), channel_id=1, source_target_pairs={{0,2},{1,15},{2,4},{3,1},{4,6},{5,3},{6,8},{7,5},{8,10},{9,7},{10,... | collective-permute-start | bytes 589832 | tf_op jit(solution)/shard_map/gram_over_columns/ppermute | solution.py:55
  57.4 3.9 %collective-permute-start.21 = (bf16[384,256]{1,0:T(8,128)(2,1)S(1)}, bf16[384,256]{1,0:T(8,128)(2,1)S(1)}, u32[]{:S(2)}, u32[]{:S(2)}) collective-permute-start(bf16[384,256]{1,0:T(8,128)(2,1)S(1)} %collective-permute-done.16.refs_0_), channel_id=1, source_target_pairs={{0,4},{1,13},{2,6},{3,15},{4,8},{5,1},{6,10},{7,3},{8,12},{9,5},{1... | collective-permute-start | bytes 589832 | tf_op jit(solution)/shard_map/gram_over_columns/ppermute | solution.py:55
  64.6 4.1 %collective-permute-done.21.refs_2_ = bf16[384,256]{1,0:T(8,128)(2,1)S(1)} collective-permute-done((bf16[384,256]{1,0:T(8,128)(2,1)S(1)}, bf16[384,256]{1,0:T(8,128)(2,1)S(1)}, u32[]{:S(2)}, u32[]{:S(2)}) %collective-permute-start.21) | collective-permute-done | bytes 196640 | tf_op jit(solution)/shard_map/gram_over_columns/ppermute | solution.py:55
  68.7 2.4 %collective-permute-done.20.refs_1_ = bf16[384,256]{1,0:T(8,128)(2,1)S(1)} collective-permute-done((bf16[384,256]{1,0:T(8,128)(2,1)S(1)}, bf16[384,256]{1,0:T(8,128)(2,1)S(1)}, u32[]{:S(2)}, u32[]{:S(2)}) %collective-permute-start.20) | collective-permute-done | bytes 196640 | tf_op jit(solution)/shard_map/gram_over_columns/ppermute | solution.py:55
  72.9 1.3 %collective-permute-start.14 = (bf16[8,192,256]{2,1,0:T(8,128)(2,1)S(1)}, bf16[8,192,256]{2,1,0:T(8,128)(2,1)S(1)}, u32[]{:S(2)}, u32[]{:S(2)}) collective-permute-start(bf16[8,192,256]{2,1,0:T(8,128)(2,1)S(1)} %append.5.refs_0_.refs_4_), channel_id=1, source_target_pairs={{0,64},{1,17},{2,66},{3,19},{4,68},{5,21},{6,70},{7,23},{8,72},{9,... | collective-permute-start | bytes 2359304 | tf_op jit(solution)/shard_map/gram_over_columns/moment_gather/ppermute | solution.py:55
  74.2 5.1 %newton_schulz.1.refs_0_ = bf16[384,256]{1,0:T(8,128)(2,1)S(1)} custom-call(f32[384,384]{1,0:T(8,128)S(1)} %gram.7.mine_ref, f32[384,384]{1,0:T(8,128)S(1)} %collective-permute-done.22.other_ref, bf16[384,256]{1,0:T(8,128)(2,1)S(1)} %get-tuple-element.24.refs_0_.direction_ref), custom_call_target="tpu_custom_call" | custom-call | flops 7516192768 | bytes 2097152 | tf_op jit(solution)/shard_map/newton_schulz/pallas_call | solution.py:281
  79.3 1.4 %collective-permute-start.23 = (bf16[384,256]{1,0:T(8,128)(2,1)S(1)}, bf16[384,256]{1,0:T(8,128)(2,1)S(1)}, u32[]{:S(2)}, u32[]{:S(2)}) collective-permute-start(bf16[384,256]{1,0:T(8,128)(2,1)S(1)} %newton_schulz.1.refs_0_), channel_id=1, source_target_pairs={{0,48},{1,193},{2,50},{3,195},{4,52},{5,197},{6,54},{7,199},{8,56}... | collective-permute-start | bytes 589832 | tf_op jit(solution)/shard_map/update_gather/ppermute | solution.py:55
  80.7 3.3 %collective-permute-start.25 = (bf16[384,256]{1,0:T(8,128)(2,1)S(1)}, bf16[384,256]{1,0:T(8,128)(2,1)S(1)}, u32[]{:S(2)}, u32[]{:S(2)}) collective-permute-start(bf16[384,256]{1,0:T(8,128)(2,1)S(1)} %newton_schulz.1.refs_0_), channel_id=1, source_target_pairs={{0,32},{1,129},{2,34},{3,131},{4,36},{5,133},{6,38},{7,135},{8,40}... | collective-permute-start | bytes 589832 | tf_op jit(solution)/shard_map/update_gather/ppermute | solution.py:55
  84.1 2.4 %collective-permute-done.23.refs_1_ = bf16[384,256]{1,0:T(8,128)(2,1)S(1)} collective-permute-done((bf16[384,256]{1,0:T(8,128)(2,1)S(1)}, bf16[384,256]{1,0:T(8,128)(2,1)S(1)}, u32[]{:S(2)}, u32[]{:S(2)}) %collective-permute-start.23) | collective-permute-done | bytes 196640 | tf_op jit(solution)/shard_map/update_gather/ppermute | solution.py:55
  86.5 3.3 %collective-permute-done.25.refs_3_ = bf16[384,256]{1,0:T(8,128)(2,1)S(1)} collective-permute-done((bf16[384,256]{1,0:T(8,128)(2,1)S(1)}, bf16[384,256]{1,0:T(8,128)(2,1)S(1)}, u32[]{:S(2)}, u32[]{:S(2)}) %collective-permute-start.25) | collective-permute-done | bytes 196640 | tf_op jit(solution)/shard_map/update_gather/ppermute | solution.py:55
  89.9 1.7 %collective-permute-start.28 = (bf16[4,192,256]{2,1,0:T(8,128)(2,1)S(1)}, bf16[4,192,256]{2,1,0:T(8,128)(2,1)S(1)}, u32[]{:S(2)}, u32[]{:S(2)}) collective-permute-start(bf16[4,192,256]{2,1,0:T(8,128)(2,1)S(1)} %get-tuple-element.19.first_ref), channel_id=1, source_target_pairs={{0,192},{1,49},{2,194},{3,51},{4,196},{5,53},{6,198},{7,55},{8,200... | collective-permute-start | bytes 1179656 | tf_op jit(solution)/shard_map/update_gather/ppermute | solution.py:55
  92.4 5.4 %collective-permute-done.28.second_ref = bf16[4,192,256]{2,1,0:T(8,128)(2,1)S(1)} collective-permute-done((bf16[4,192,256]{2,1,0:T(8,128)(2,1)S(1)}, bf16[4,192,256]{2,1,0:T(8,128)(2,1)S(1)}, u32[]{:S(2)}, u32[]{:S(2)}) %collective-permute-start.28) | collective-permute-done | bytes 393248 | tf_op jit(solution)/shard_map/update_gather/ppermute | solution.py:55
  97.8 2.7 %collective-permute-start.29 = (bf16[8,192,256]{2,1,0:T(8,128)(2,1)S(1)}, bf16[8,192,256]{2,1,0:T(8,128)(2,1)S(1)}, u32[]{:S(2)}, u32[]{:S(2)}) collective-permute-start(bf16[8,192,256]{2,1,0:T(8,128)(2,1)S(1)} %append.7.refs_0_), channel_id=1, source_target_pairs={{0,64},{1,17},{2,66},{3,19},{4,68},{5,21},{6,70},{7,23},{8,72},{9,... | collective-permute-start | bytes 2359304 | tf_op jit(solution)/shard_map/update_gather/ppermute | solution.py:55
  105.5 4.9 %collective-permute-done.29.refs_0_ = bf16[8,192,256]{2,1,0:T(8,128)(2,1)S(1)} collective-permute-done((bf16[8,192,256]{2,1,0:T(8,128)(2,1)S(1)}, bf16[8,192,256]{2,1,0:T(8,128)(2,1)S(1)}, u32[]{:S(2)}, u32[]{:S(2)}) %collective-permute-start.29) | collective-permute-done | bytes 786464 | tf_op jit(solution)/shard_map/update_gather/ppermute | solution.py:55
  (64 shorter events, 22.4 us)
Async XLA Ops:
  3.2 4.1 %copy-start.2 = (bf16[16,384,256]{2,1,0:T(8,128)(2,1)S(1)}, bf16[16,384,256]{2,1,0:T(8,128)(2,1)}, u32[]{:S(2)}) copy-start(bf16[16,384,256]{2,1,0:T(8,128)(2,1)} %refs_0_.1) | copy-start | bytes 9437188
  3.9 12.1 %collective-permute-start.2 = (bf16[8,192,256]{2,1,0:T(8,128)(2,1)S(1)}, bf16[8,192,256]{2,1,0:T(8,128)(2,1)S(1)}, u32[]{:S(2)}, u32[]{:S(2)}) collective-permute-start(bf16[8,192,256]{2,1,0:T(8,128)(2,1)S(1)} %get-tuple-element.15), channel_id=1, source_target_pairs={{0,192},{1,49},{2,194},{3,51},{4,196},{5,53},{6,198},{7,55},{8,200... | collective-permute-start | bytes 2359304 | tf_op jit(solution)/shard_map/sum_over_replicas/ppermute | solution.py:55
  5.4 14.3 %collective-permute-start = (bf16[8,192,256]{2,1,0:T(8,128)(2,1)S(1)}, bf16[8,192,256]{2,1,0:T(8,128)(2,1)S(1)}, u32[]{:S(2)}, u32[]{:S(2)}) collective-permute-start(bf16[8,192,256]{2,1,0:T(8,128)(2,1)S(1)} %get-tuple-element.13), channel_id=1, source_target_pairs={{0,64},{1,17},{2,66},{3,19},{4,68},{5,21},{6,70},{7,23},{8,72},{9,... | collective-permute-start | bytes 2359304 | tf_op jit(solution)/shard_map/sum_over_replicas/ppermute | solution.py:55
  16.1 9.3 %collective-permute-start.3 = (bf16[4,192,256]{2,1,0:T(8,128)(2,1)S(1)}, bf16[4,192,256]{2,1,0:T(8,128)(2,1)S(1)}, u32[]{:S(2)}, u32[]{:S(2)}) collective-permute-start(bf16[4,192,256]{2,1,0:T(8,128)(2,1)S(1)} %get-tuple-element.22), channel_id=1, source_target_pairs={{0,64},{1,17},{2,66},{3,19},{4,68},{5,21},{6,70},{7,23},{8,72},{9,... | collective-permute-start | bytes 1179656 | tf_op jit(solution)/shard_map/sum_over_replicas/ppermute | solution.py:55
  19.9 7.9 %collective-permute-start.1 = (bf16[4,192,256]{2,1,0:T(8,128)(2,1)S(1)}, bf16[4,192,256]{2,1,0:T(8,128)(2,1)S(1)}, u32[]{:S(2)}, u32[]{:S(2)}) collective-permute-start(bf16[4,192,256]{2,1,0:T(8,128)(2,1)S(1)} %get-tuple-element.20), channel_id=1, source_target_pairs={{0,192},{1,49},{2,194},{3,51},{4,196},{5,53},{6,198},{7,55},{8,200... | collective-permute-start | bytes 1179656 | tf_op jit(solution)/shard_map/sum_over_replicas/ppermute | solution.py:55
  27.9 7.3 %collective-permute-start.6 = (bf16[384,256]{1,0:T(8,128)(2,1)S(1)}, bf16[384,256]{1,0:T(8,128)(2,1)S(1)}, u32[]{:S(2)}, u32[]{:S(2)}) collective-permute-start(bf16[384,256]{1,0:T(8,128)(2,1)S(1)} %pad_maximum_fusion.2), channel_id=1, source_target_pairs={{0,32},{1,129},{2,34},{3,131},{4,36},{5,133},{6,38},{7,135},{8,40}... | collective-permute-start | bytes 589832 | tf_op jit(solution)/shard_map/sum_over_replicas/ppermute | solution.py:55
  29.6 6.4 %collective-permute-start.5 = (bf16[384,256]{1,0:T(8,128)(2,1)S(1)}, bf16[384,256]{1,0:T(8,128)(2,1)S(1)}, u32[]{:S(2)}, u32[]{:S(2)}) collective-permute-start(bf16[384,256]{1,0:T(8,128)(2,1)S(1)} %pad_maximum_fusion.1), channel_id=1, source_target_pairs={{0,16},{1,65},{2,18},{3,67},{4,20},{5,69},{6,22},{7,71},{8,24},{9,... | collective-permute-start | bytes 589832 | tf_op jit(solution)/shard_map/sum_over_replicas/ppermute | solution.py:55
  30.4 7.0 %collective-permute-start.4 = (bf16[384,256]{1,0:T(8,128)(2,1)S(1)}, bf16[384,256]{1,0:T(8,128)(2,1)S(1)}, u32[]{:S(2)}, u32[]{:S(2)}) collective-permute-start(bf16[384,256]{1,0:T(8,128)(2,1)S(1)} %pad_maximum_fusion), channel_id=1, source_target_pairs={{0,48},{1,193},{2,50},{3,195},{4,52},{5,197},{6,54},{7,199},{8,56}... | collective-permute-start | bytes 589832 | tf_op jit(solution)/shard_map/sum_over_replicas/ppermute | solution.py:55
  37.5 2.1 %collective-permute-start.7 = (bf16[384,256]{1,0:T(8,128)(2,1)S(1)}, bf16[384,256]{1,0:T(8,128)(2,1)S(1)}, u32[]{:S(2)}, u32[]{:S(2)}) collective-permute-start(bf16[384,256]{1,0:T(8,128)(2,1)S(1)} %get-tuple-element.24.refs_0_.direction_ref), channel_id=1, source_target_pairs={{0,1},{1,0},{2,3},{3,2},{4,5},{5,4},{6,7},{7,6},{8,9},{9,8},{10,11... | collective-permute-start | bytes 589832 | tf_op jit(solution)/shard_map/gram_over_columns/ppermute | solution.py:55
  37.6 9.6 %collective-permute-start.15 = (bf16[384,256]{1,0:T(8,128)(2,1)S(1)}, bf16[384,256]{1,0:T(8,128)(2,1)S(1)}, u32[]{:S(2)}, u32[]{:S(2)}) collective-permute-start(bf16[384,256]{1,0:T(8,128)(2,1)S(1)} %get-tuple-element.24.refs_0_.direction_ref), channel_id=1, source_target_pairs={{0,2},{1,15},{2,4},{3,1},{4,6},{5,3},{6,8},{7,5},{8,10},{9,7},{10,... | collective-permute-start | bytes 589832 | tf_op jit(solution)/shard_map/gram_over_columns/ppermute | solution.py:55
  39.6 8.6 %collective-permute-start.8 = (bf16[384,256]{1,0:T(8,128)(2,1)S(1)}, bf16[384,256]{1,0:T(8,128)(2,1)S(1)}, u32[]{:S(2)}, u32[]{:S(2)}) collective-permute-start(bf16[384,256]{1,0:T(8,128)(2,1)S(1)} %bitcast.20), channel_id=1, source_target_pairs={{0,48},{1,193},{2,50},{3,195},{4,52},{5,197},{6,54},{7,199},{8,56}... | collective-permute-start | bytes 589832 | tf_op jit(solution)/shard_map/gram_over_columns/moment_gather/ppermute | solution.py:55
  41.0 7.2 %collective-permute-start.9 = (bf16[384,256]{1,0:T(8,128)(2,1)S(1)}, bf16[384,256]{1,0:T(8,128)(2,1)S(1)}, u32[]{:S(2)}, u32[]{:S(2)}) collective-permute-start(bf16[384,256]{1,0:T(8,128)(2,1)S(1)} %bitcast.21), channel_id=1, source_target_pairs={{0,16},{1,65},{2,18},{3,67},{4,20},{5,69},{6,22},{7,71},{8,24},{9,... | collective-permute-start | bytes 589832 | tf_op jit(solution)/shard_map/gram_over_columns/moment_gather/ppermute | solution.py:55
  41.2 9.0 %collective-permute-start.10 = (bf16[384,256]{1,0:T(8,128)(2,1)S(1)}, bf16[384,256]{1,0:T(8,128)(2,1)S(1)}, u32[]{:S(2)}, u32[]{:S(2)}) collective-permute-start(bf16[384,256]{1,0:T(8,128)(2,1)S(1)} %bitcast.22), channel_id=1, source_target_pairs={{0,32},{1,129},{2,34},{3,131},{4,36},{5,133},{6,38},{7,135},{8,40}... | collective-permute-start | bytes 589832 | tf_op jit(solution)/shard_map/gram_over_columns/moment_gather/ppermute | solution.py:55
  44.4 9.1 %collective-permute-start.18 = (bf16[384,256]{1,0:T(8,128)(2,1)S(1)}, bf16[384,256]{1,0:T(8,128)(2,1)S(1)}, u32[]{:S(2)}, u32[]{:S(2)}) collective-permute-start(bf16[384,256]{1,0:T(8,128)(2,1)S(1)} %collective-permute-done.7.refs_1_), channel_id=1, source_target_pairs={{0,2},{1,15},{2,4},{3,1},{4,6},{5,3},{6,8},{7,5},{8,10},{9,7},{10,... | collective-permute-start | bytes 589832 | tf_op jit(solution)/shard_map/gram_over_columns/ppermute | solution.py:55
  47.2 8.3 %collective-permute-start.16 = (bf16[384,256]{1,0:T(8,128)(2,1)S(1)}, bf16[384,256]{1,0:T(8,128)(2,1)S(1)}, u32[]{:S(2)}, u32[]{:S(2)}) collective-permute-start(bf16[384,256]{1,0:T(8,128)(2,1)S(1)} %collective-permute-done.15.refs_0_), channel_id=1, source_target_pairs={{0,2},{1,15},{2,4},{3,1},{4,6},{5,3},{6,8},{7,5},{8,10},{9,7},{10,... | collective-permute-start | bytes 589832 | tf_op jit(solution)/shard_map/gram_over_columns/ppermute | solution.py:55
  50.2 13.4 %collective-permute-start.11 = (bf16[4,192,256]{2,1,0:T(8,128)(2,1)S(1)}, bf16[4,192,256]{2,1,0:T(8,128)(2,1)S(1)}, u32[]{:S(2)}, u32[]{:S(2)}) collective-permute-start(bf16[4,192,256]{2,1,0:T(8,128)(2,1)S(1)} %get-tuple-element.16.first_ref.refs_4_), channel_id=1, source_target_pairs={{0,64},{1,17},{2,66},{3,19},{4,68},{5,21},{6,70},{7,23},{8,72},{9,... | collective-permute-start | bytes 1179656 | tf_op jit(solution)/shard_map/gram_over_columns/moment_gather/ppermute | solution.py:55
  52.6 11.0 %collective-permute-start.13 = (bf16[4,192,256]{2,1,0:T(8,128)(2,1)S(1)}, bf16[4,192,256]{2,1,0:T(8,128)(2,1)S(1)}, u32[]{:S(2)}, u32[]{:S(2)}) collective-permute-start(bf16[4,192,256]{2,1,0:T(8,128)(2,1)S(1)} %get-tuple-element.17.first_ref.refs_3_), channel_id=1, source_target_pairs={{0,192},{1,49},{2,194},{3,51},{4,196},{5,53},{6,198},{7,55},{8,200... | collective-permute-start | bytes 1179656 | tf_op jit(solution)/shard_map/gram_over_columns/moment_gather/ppermute | solution.py:55
  53.6 8.9 %collective-permute-start.19 = (bf16[384,256]{1,0:T(8,128)(2,1)S(1)}, bf16[384,256]{1,0:T(8,128)(2,1)S(1)}, u32[]{:S(2)}, u32[]{:S(2)}) collective-permute-start(bf16[384,256]{1,0:T(8,128)(2,1)S(1)} %collective-permute-done.18.refs_1_), channel_id=1, source_target_pairs={{0,2},{1,15},{2,4},{3,1},{4,6},{5,3},{6,8},{7,5},{8,10},{9,7},{10,... | collective-permute-start | bytes 589832 | tf_op jit(solution)/shard_map/gram_over_columns/ppermute | solution.py:55
  55.5 9.1 %collective-permute-start.17 = (bf16[384,256]{1,0:T(8,128)(2,1)S(1)}, bf16[384,256]{1,0:T(8,128)(2,1)S(1)}, u32[]{:S(2)}, u32[]{:S(2)}) collective-permute-start(bf16[384,256]{1,0:T(8,128)(2,1)S(1)} %collective-permute-done.16.refs_0_), channel_id=1, source_target_pairs={{0,2},{1,15},{2,4},{3,1},{4,6},{5,3},{6,8},{7,5},{8,10},{9,7},{10,... | collective-permute-start | bytes 589832 | tf_op jit(solution)/shard_map/gram_over_columns/ppermute | solution.py:55
  57.4 11.3 %collective-permute-start.21 = (bf16[384,256]{1,0:T(8,128)(2,1)S(1)}, bf16[384,256]{1,0:T(8,128)(2,1)S(1)}, u32[]{:S(2)}, u32[]{:S(2)}) collective-permute-start(bf16[384,256]{1,0:T(8,128)(2,1)S(1)} %collective-permute-done.16.refs_0_), channel_id=1, source_target_pairs={{0,4},{1,13},{2,6},{3,15},{4,8},{5,1},{6,10},{7,3},{8,12},{9,5},{1... | collective-permute-start | bytes 589832 | tf_op jit(solution)/shard_map/gram_over_columns/ppermute | solution.py:55
  62.5 8.6 %collective-permute-start.20 = (bf16[384,256]{1,0:T(8,128)(2,1)S(1)}, bf16[384,256]{1,0:T(8,128)(2,1)S(1)}, u32[]{:S(2)}, u32[]{:S(2)}) collective-permute-start(bf16[384,256]{1,0:T(8,128)(2,1)S(1)} %collective-permute-done.19.refs_1_), channel_id=1, source_target_pairs={{0,2},{1,15},{2,4},{3,1},{4,6},{5,3},{6,8},{7,5},{8,10},{9,7},{10,... | collective-permute-start | bytes 589832 | tf_op jit(solution)/shard_map/gram_over_columns/ppermute | solution.py:55
  71.6 2.6 %collective-permute-start.22 = (f32[384,384]{1,0:T(8,128)S(1)}, f32[384,384]{1,0:T(8,128)S(1)}, u32[]{:S(2)}, u32[]{:S(2)}) collective-permute-start(f32[384,384]{1,0:T(8,128)S(1)} %gram.7.mine_ref), channel_id=1, source_target_pairs={{0,1},{1,0},{2,3},{3,2},{4,5},{5,4},{6,7},{7,6},{8,9},{9,8},{10,11... | collective-permute-start | bytes 1769480 | tf_op jit(solution)/shard_map/gram_over_columns/ppermute | solution.py:55
  71.7 20.7 %collective-permute-start.12 = (bf16[8,192,256]{2,1,0:T(8,128)(2,1)S(1)}, bf16[8,192,256]{2,1,0:T(8,128)(2,1)S(1)}, u32[]{:S(2)}, u32[]{:S(2)}) collective-permute-start(bf16[8,192,256]{2,1,0:T(8,128)(2,1)S(1)} %append.4.refs_1_.refs_5_), channel_id=1, source_target_pairs={{0,192},{1,49},{2,194},{3,51},{4,196},{5,53},{6,198},{7,55},{8,200... | collective-permute-start | bytes 2359304 | tf_op jit(solution)/shard_map/gram_over_columns/moment_gather/ppermute | solution.py:55
  72.9 19.5 %collective-permute-start.14 = (bf16[8,192,256]{2,1,0:T(8,128)(2,1)S(1)}, bf16[8,192,256]{2,1,0:T(8,128)(2,1)S(1)}, u32[]{:S(2)}, u32[]{:S(2)}) collective-permute-start(bf16[8,192,256]{2,1,0:T(8,128)(2,1)S(1)} %append.5.refs_0_.refs_4_), channel_id=1, source_target_pairs={{0,64},{1,17},{2,66},{3,19},{4,68},{5,21},{6,70},{7,23},{8,72},{9,... | collective-permute-start | bytes 2359304 | tf_op jit(solution)/shard_map/gram_over_columns/moment_gather/ppermute | solution.py:55
  79.3 7.2 %collective-permute-start.23 = (bf16[384,256]{1,0:T(8,128)(2,1)S(1)}, bf16[384,256]{1,0:T(8,128)(2,1)S(1)}, u32[]{:S(2)}, u32[]{:S(2)}) collective-permute-start(bf16[384,256]{1,0:T(8,128)(2,1)S(1)} %newton_schulz.1.refs_0_), channel_id=1, source_target_pairs={{0,48},{1,193},{2,50},{3,195},{4,52},{5,197},{6,54},{7,199},{8,56}... | collective-permute-start | bytes 589832 | tf_op jit(solution)/shard_map/update_gather/ppermute | solution.py:55
  80.7 5.8 %collective-permute-start.24 = (bf16[384,256]{1,0:T(8,128)(2,1)S(1)}, bf16[384,256]{1,0:T(8,128)(2,1)S(1)}, u32[]{:S(2)}, u32[]{:S(2)}) collective-permute-start(bf16[384,256]{1,0:T(8,128)(2,1)S(1)} %newton_schulz.1.refs_0_), channel_id=1, source_target_pairs={{0,16},{1,65},{2,18},{3,67},{4,20},{5,69},{6,22},{7,71},{8,24},{9,... | collective-permute-start | bytes 589832 | tf_op jit(solution)/shard_map/update_gather/ppermute | solution.py:55
  80.7 9.1 %collective-permute-start.25 = (bf16[384,256]{1,0:T(8,128)(2,1)S(1)}, bf16[384,256]{1,0:T(8,128)(2,1)S(1)}, u32[]{:S(2)}, u32[]{:S(2)}) collective-permute-start(bf16[384,256]{1,0:T(8,128)(2,1)S(1)} %newton_schulz.1.refs_0_), channel_id=1, source_target_pairs={{0,32},{1,129},{2,34},{3,131},{4,36},{5,133},{6,38},{7,135},{8,40}... | collective-permute-start | bytes 589832 | tf_op jit(solution)/shard_map/update_gather/ppermute | solution.py:55
  89.9 7.9 %collective-permute-start.28 = (bf16[4,192,256]{2,1,0:T(8,128)(2,1)S(1)}, bf16[4,192,256]{2,1,0:T(8,128)(2,1)S(1)}, u32[]{:S(2)}, u32[]{:S(2)}) collective-permute-start(bf16[4,192,256]{2,1,0:T(8,128)(2,1)S(1)} %get-tuple-element.19.first_ref), channel_id=1, source_target_pairs={{0,192},{1,49},{2,194},{3,51},{4,196},{5,53},{6,198},{7,55},{8,200... | collective-permute-start | bytes 1179656 | tf_op jit(solution)/shard_map/update_gather/ppermute | solution.py:55
  91.5 8.9 %collective-permute-start.26 = (bf16[4,192,256]{2,1,0:T(8,128)(2,1)S(1)}, bf16[4,192,256]{2,1,0:T(8,128)(2,1)S(1)}, u32[]{:S(2)}, u32[]{:S(2)}) collective-permute-start(bf16[4,192,256]{2,1,0:T(8,128)(2,1)S(1)} %get-tuple-element.18.first_ref), channel_id=1, source_target_pairs={{0,64},{1,17},{2,66},{3,19},{4,68},{5,21},{6,70},{7,23},{8,72},{9,... | collective-permute-start | bytes 1179656 | tf_op jit(solution)/shard_map/update_gather/ppermute | solution.py:55
  97.8 12.6 %collective-permute-start.29 = (bf16[8,192,256]{2,1,0:T(8,128)(2,1)S(1)}, bf16[8,192,256]{2,1,0:T(8,128)(2,1)S(1)}, u32[]{:S(2)}, u32[]{:S(2)}) collective-permute-start(bf16[8,192,256]{2,1,0:T(8,128)(2,1)S(1)} %append.7.refs_0_), channel_id=1, source_target_pairs={{0,64},{1,17},{2,66},{3,19},{4,68},{5,21},{6,70},{7,23},{8,72},{9,... | collective-permute-start | bytes 2359304 | tf_op jit(solution)/shard_map/update_gather/ppermute | solution.py:55
  100.5 12.1 %collective-permute-start.27 = (bf16[8,192,256]{2,1,0:T(8,128)(2,1)S(1)}, bf16[8,192,256]{2,1,0:T(8,128)(2,1)S(1)}, u32[]{:S(2)}, u32[]{:S(2)}) collective-permute-start(bf16[8,192,256]{2,1,0:T(8,128)(2,1)S(1)} %append.6.refs_1_), channel_id=1, source_target_pairs={{0,192},{1,49},{2,194},{3,51},{4,196},{5,53},{6,198},{7,55},{8,200... | collective-permute-start | bytes 2359304 | tf_op jit(solution)/shard_map/update_gather/ppermute | solution.py:55
  105.5 7.1 %copy-start = (bf16[16,384,256]{2,1,0:T(8,128)(2,1)S(1)}, bf16[16,384,256]{2,1,0:T(8,128)(2,1)}, u32[]{:S(2)}) copy-start(bf16[16,384,256]{2,1,0:T(8,128)(2,1)} %assemble.8.refs_2_) | copy-start | bytes 9437188
  (2 other events, 2.5 us)

commit v7 on v6

--- a/solution.py
+++ b/solution.py
@@ -342,7 +342,8 @@
         same, cross = send(same, ring), send(cross, ring)
         gram = gram_of([same, cross], gram, four)
         same, cross, opposite = send(same, ring), send(cross, ring), send(same, skip)
-        gram = gram_of([same, cross, opposite], gram, eight)
+        gram = gram_of([same, opposite], gram, eight)
+        gram = gram_of([cross], gram)
         other = send(gram, swap)
     update = newton_schulz(gram, other, direction)
     with jax.named_scope("update_gather"):

time: 114 us -> 119 us (1.044)
  waiting for transfers between devices: 48.6 us -> 53.1 us
    ppermute x30, waiting for transfers between devices: 48.6 us -> 53.1 us  [send(): return lax.ppermute(value, ('dp', 'zero'), pairs)]
  transfers between devices with their start and end apart: 30 -> 30, of which waited for: 17 -> 19; matrix products, arithmetic and copies ran while one was open for 0% -> 0% of each run, Pallas kernels for 11% -> 11%
where the time goes in v7:
time: 119 us; the launch traced here: 118 us
  waiting for transfers between devices  53.1 us (45%)
  starting transfers between devices  45.5 us (38%)
  Pallas kernels  15.1 us (13%)
  local copies, waits for them, and re-layouts  2.55 us (2%)
    ppermute x30, waiting for transfers between devices, send(): return lax.ppermute(value, ('dp', 'zero'), pairs)  53.1 us
    ppermute x30, starting transfers between devices, send(): return lax.ppermute(value, ('dp', 'zero'), pairs)  45.5 us
    pallas_call x6, Pallas kernels, assemble(): pl.pallas_call(functools.partial(assemble_kernel, places), out_shape=jax....  6.35 us
    pallas_call x1, Pallas kernels, newton_schulz(): pl.pallas_call(newton_schulz_kernel, out_shape=jax.ShapeDtypeStruct(direc...  5.09 us
    unnamed x8, local copies, waits for them, and re-layouts  2.55 us
  transfers between devices with their start and end apart: 30, of which 19 were waited for; matrix products, arithmetic and copies ran while one was open for 0% of the time, Pallas kernels for 11%

profile of v7, /device:TPU:2, one launch (start us, length us, event | category | flops | bytes accessed | tf_op | source)
XLA Modules:
  0.0 118.1 jit_solution(5799066712293529888)
XLA Ops:
  0.6 1.9 %copy-done.1 = bf16[1,16,384,256]{3,2,1,0:T(8,128)(2,1)S(1)} copy-done((bf16[1,16,384,256]{3,2,1,0:T(8,128)(2,1)S(1)}, bf16[1,16,384,256]{3,2,1,0:T(8,128)(2,1)}, u32[]{:S(2)}) %copy-start.1) | copy-done | bytes 3145752
  3.9 1.6 %collective-permute-start.2 = (bf16[8,192,256]{2,1,0:T(8,128)(2,1)S(1)}, bf16[8,192,256]{2,1,0:T(8,128)(2,1)S(1)}, u32[]{:S(2)}, u32[]{:S(2)}) collective-permute-start(bf16[8,192,256]{2,1,0:T(8,128)(2,1)S(1)} %get-tuple-element.15), channel_id=1, source_target_pairs={{0,192},{1,49},{2,194},{3,51},{4,196},{5,53},{6,198},{7,55},{8,200... | collective-permute-start | bytes 2359304 | tf_op jit(solution)/shard_map/sum_over_replicas/ppermute | solution.py:55
  5.4 1.8 %collective-permute-start = (bf16[8,192,256]{2,1,0:T(8,128)(2,1)S(1)}, bf16[8,192,256]{2,1,0:T(8,128)(2,1)S(1)}, u32[]{:S(2)}, u32[]{:S(2)}) collective-permute-start(bf16[8,192,256]{2,1,0:T(8,128)(2,1)S(1)} %get-tuple-element.13), channel_id=1, source_target_pairs={{0,64},{1,17},{2,66},{3,19},{4,68},{5,21},{6,70},{7,23},{8,72},{9,... | collective-permute-start | bytes 2359304 | tf_op jit(solution)/shard_map/sum_over_replicas/ppermute | solution.py:55
  8.2 7.8 %collective-permute-done.2 = bf16[8,192,256]{2,1,0:T(8,128)(2,1)S(1)} collective-permute-done((bf16[8,192,256]{2,1,0:T(8,128)(2,1)S(1)}, bf16[8,192,256]{2,1,0:T(8,128)(2,1)S(1)}, u32[]{:S(2)}, u32[]{:S(2)}) %collective-permute-start.2) | collective-permute-done | bytes 786464 | tf_op jit(solution)/shard_map/sum_over_replicas/ppermute | solution.py:55
  16.1 3.6 %collective-permute-start.3 = (bf16[4,192,256]{2,1,0:T(8,128)(2,1)S(1)}, bf16[4,192,256]{2,1,0:T(8,128)(2,1)S(1)}, u32[]{:S(2)}, u32[]{:S(2)}) collective-permute-start(bf16[4,192,256]{2,1,0:T(8,128)(2,1)S(1)} %get-tuple-element.22), channel_id=1, source_target_pairs={{0,64},{1,17},{2,66},{3,19},{4,68},{5,21},{6,70},{7,23},{8,72},{9,... | collective-permute-start | bytes 1179656 | tf_op jit(solution)/shard_map/sum_over_replicas/ppermute | solution.py:55
  20.4 5.1 %collective-permute-done.3 = bf16[4,192,256]{2,1,0:T(8,128)(2,1)S(1)} collective-permute-done((bf16[4,192,256]{2,1,0:T(8,128)(2,1)S(1)}, bf16[4,192,256]{2,1,0:T(8,128)(2,1)S(1)}, u32[]{:S(2)}, u32[]{:S(2)}) %collective-permute-start.3) | collective-permute-done | bytes 393248 | tf_op jit(solution)/shard_map/sum_over_replicas/ppermute | solution.py:55
  25.6 2.2 %collective-permute-done.1 = bf16[4,192,256]{2,1,0:T(8,128)(2,1)S(1)} collective-permute-done((bf16[4,192,256]{2,1,0:T(8,128)(2,1)S(1)}, bf16[4,192,256]{2,1,0:T(8,128)(2,1)S(1)}, u32[]{:S(2)}, u32[]{:S(2)}) %collective-permute-start.1) | collective-permute-done | bytes 393248 | tf_op jit(solution)/shard_map/sum_over_replicas/ppermute | solution.py:55
  27.9 1.7 %collective-permute-start.6 = (bf16[384,256]{1,0:T(8,128)(2,1)S(1)}, bf16[384,256]{1,0:T(8,128)(2,1)S(1)}, u32[]{:S(2)}, u32[]{:S(2)}) collective-permute-start(bf16[384,256]{1,0:T(8,128)(2,1)S(1)} %pad_maximum_fusion.2), channel_id=1, source_target_pairs={{0,32},{1,129},{2,34},{3,131},{4,36},{5,133},{6,38},{7,135},{8,40}... | collective-permute-start | bytes 589832 | tf_op jit(solution)/shard_map/sum_over_replicas/ppermute | solution.py:55
  30.4 1.9 %collective-permute-start.4 = (bf16[384,256]{1,0:T(8,128)(2,1)S(1)}, bf16[384,256]{1,0:T(8,128)(2,1)S(1)}, u32[]{:S(2)}, u32[]{:S(2)}) collective-permute-start(bf16[384,256]{1,0:T(8,128)(2,1)S(1)} %pad_maximum_fusion), channel_id=1, source_target_pairs={{0,48},{1,193},{2,50},{3,195},{4,52},{5,197},{6,54},{7,199},{8,56}... | collective-permute-start | bytes 589832 | tf_op jit(solution)/shard_map/sum_over_replicas/ppermute | solution.py:55
  32.3 2.9 %collective-permute-done.6 = bf16[384,256]{1,0:T(8,128)(2,1)S(1)} collective-permute-done((bf16[384,256]{1,0:T(8,128)(2,1)S(1)}, bf16[384,256]{1,0:T(8,128)(2,1)S(1)}, u32[]{:S(2)}, u32[]{:S(2)}) %collective-permute-start.6) | collective-permute-done | bytes 196640 | tf_op jit(solution)/shard_map/sum_over_replicas/ppermute | solution.py:55
  37.6 1.4 %collective-permute-done.7.refs_1_ = bf16[384,256]{1,0:T(8,128)(2,1)S(1)} collective-permute-done((bf16[384,256]{1,0:T(8,128)(2,1)S(1)}, bf16[384,256]{1,0:T(8,128)(2,1)S(1)}, u32[]{:S(2)}, u32[]{:S(2)}) %collective-permute-start.7) | collective-permute-done | bytes 196640 | tf_op jit(solution)/shard_map/gram_over_columns/ppermute | solution.py:55
  39.1 1.9 %collective-permute-start.8 = (bf16[384,256]{1,0:T(8,128)(2,1)S(1)}, bf16[384,256]{1,0:T(8,128)(2,1)S(1)}, u32[]{:S(2)}, u32[]{:S(2)}) collective-permute-start(bf16[384,256]{1,0:T(8,128)(2,1)S(1)} %bitcast.20), channel_id=1, source_target_pairs={{0,48},{1,193},{2,50},{3,195},{4,52},{5,197},{6,54},{7,199},{8,56}... | collective-permute-start | bytes 589832 | tf_op jit(solution)/shard_map/gram_over_columns/moment_gather/ppermute | solution.py:55
  41.0 2.9 %collective-permute-start.10 = (bf16[384,256]{1,0:T(8,128)(2,1)S(1)}, bf16[384,256]{1,0:T(8,128)(2,1)S(1)}, u32[]{:S(2)}, u32[]{:S(2)}) collective-permute-start(bf16[384,256]{1,0:T(8,128)(2,1)S(1)} %bitcast.22), channel_id=1, source_target_pairs={{0,32},{1,129},{2,34},{3,131},{4,36},{5,133},{6,38},{7,135},{8,40}... | collective-permute-start | bytes 589832 | tf_op jit(solution)/shard_map/gram_over_columns/moment_gather/ppermute | solution.py:55
  43.8 1.9 %collective-permute-start.18 = (bf16[384,256]{1,0:T(8,128)(2,1)S(1)}, bf16[384,256]{1,0:T(8,128)(2,1)S(1)}, u32[]{:S(2)}, u32[]{:S(2)}) collective-permute-start(bf16[384,256]{1,0:T(8,128)(2,1)S(1)} %get-tuple-element.24.refs_0_.direction_ref), channel_id=1, source_target_pairs={{0,2},{1,15},{2,4},{3,1},{4,6},{5,3},{6,8},{7,5},{8,10},{9,7},{10,... | collective-permute-start | bytes 589832 | tf_op jit(solution)/shard_map/gram_over_columns/ppermute | solution.py:55
  45.8 1.9 %collective-permute-start.15 = (bf16[384,256]{1,0:T(8,128)(2,1)S(1)}, bf16[384,256]{1,0:T(8,128)(2,1)S(1)}, u32[]{:S(2)}, u32[]{:S(2)}) collective-permute-start(bf16[384,256]{1,0:T(8,128)(2,1)S(1)} %collective-permute-done.7.refs_1_), channel_id=1, source_target_pairs={{0,2},{1,15},{2,4},{3,1},{4,6},{5,3},{6,8},{7,5},{8,10},{9,7},{10,... | collective-permute-start | bytes 589832 | tf_op jit(solution)/shard_map/gram_over_columns/ppermute | solution.py:55
  47.7 1.9 %collective-permute-done.10.refs_3_ = bf16[384,256]{1,0:T(8,128)(2,1)S(1)} collective-permute-done((bf16[384,256]{1,0:T(8,128)(2,1)S(1)}, bf16[384,256]{1,0:T(8,128)(2,1)S(1)}, u32[]{:S(2)}, u32[]{:S(2)}) %collective-permute-start.10) | collective-permute-done | bytes 196640 | tf_op jit(solution)/shard_map/gram_over_columns/moment_gather/ppermute | solution.py:55
  49.6 2.4 %collective-permute-start.11 = (bf16[4,192,256]{2,1,0:T(8,128)(2,1)S(1)}, bf16[4,192,256]{2,1,0:T(8,128)(2,1)S(1)}, u32[]{:S(2)}, u32[]{:S(2)}) collective-permute-start(bf16[4,192,256]{2,1,0:T(8,128)(2,1)S(1)} %get-tuple-element.16.first_ref.refs_4_), channel_id=1, source_target_pairs={{0,64},{1,17},{2,66},{3,19},{4,68},{5,21},{6,70},{7,23},{8,72},{9,... | collective-permute-start | bytes 1179656 | tf_op jit(solution)/shard_map/gram_over_columns/moment_gather/ppermute | solution.py:55
  53.3 1.6 %collective-permute-start.19 = (bf16[384,256]{1,0:T(8,128)(2,1)S(1)}, bf16[384,256]{1,0:T(8,128)(2,1)S(1)}, u32[]{:S(2)}, u32[]{:S(2)}) collective-permute-start(bf16[384,256]{1,0:T(8,128)(2,1)S(1)} %collective-permute-done.18.refs_0_), channel_id=1, source_target_pairs={{0,2},{1,15},{2,4},{3,1},{4,6},{5,3},{6,8},{7,5},{8,10},{9,7},{10,... | collective-permute-start | bytes 589832 | tf_op jit(solution)/shard_map/gram_over_columns/ppermute | solution.py:55
  56.8 5.7 %collective-permute-done.19.refs_0_ = bf16[384,256]{1,0:T(8,128)(2,1)S(1)} collective-permute-done((bf16[384,256]{1,0:T(8,128)(2,1)S(1)}, bf16[384,256]{1,0:T(8,128)(2,1)S(1)}, u32[]{:S(2)}, u32[]{:S(2)}) %collective-permute-start.19) | collective-permute-done | bytes 196640 | tf_op jit(solution)/shard_map/gram_over_columns/ppermute | solution.py:55
  62.5 2.0 %collective-permute-start.21 = (bf16[384,256]{1,0:T(8,128)(2,1)S(1)}, bf16[384,256]{1,0:T(8,128)(2,1)S(1)}, u32[]{:S(2)}, u32[]{:S(2)}) collective-permute-start(bf16[384,256]{1,0:T(8,128)(2,1)S(1)} %collective-permute-done.19.refs_0_), channel_id=1, source_target_pairs={{0,4},{1,13},{2,6},{3,15},{4,8},{5,1},{6,10},{7,3},{8,12},{9,5},{1... | collective-permute-start | bytes 589832 | tf_op jit(solution)/shard_map/gram_over_columns/ppermute | solution.py:55
  64.6 3.6 %collective-permute-start.17 = (bf16[384,256]{1,0:T(8,128)(2,1)S(1)}, bf16[384,256]{1,0:T(8,128)(2,1)S(1)}, u32[]{:S(2)}, u32[]{:S(2)}) collective-permute-start(bf16[384,256]{1,0:T(8,128)(2,1)S(1)} %collective-permute-done.16.refs_1_), channel_id=1, source_target_pairs={{0,2},{1,15},{2,4},{3,1},{4,6},{5,3},{6,8},{7,5},{8,10},{9,7},{10,... | collective-permute-start | bytes 589832 | tf_op jit(solution)/shard_map/gram_over_columns/ppermute | solution.py:55
  69.4 3.0 %collective-permute-done.21.refs_1_ = bf16[384,256]{1,0:T(8,128)(2,1)S(1)} collective-permute-done((bf16[384,256]{1,0:T(8,128)(2,1)S(1)}, bf16[384,256]{1,0:T(8,128)(2,1)S(1)}, u32[]{:S(2)}, u32[]{:S(2)}) %collective-permute-start.21) | collective-permute-done | bytes 196640 | tf_op jit(solution)/shard_map/gram_over_columns/ppermute | solution.py:55
  72.9 2.8 %collective-permute-done.17.refs_0_ = bf16[384,256]{1,0:T(8,128)(2,1)S(1)} collective-permute-done((bf16[384,256]{1,0:T(8,128)(2,1)S(1)}, bf16[384,256]{1,0:T(8,128)(2,1)S(1)}, u32[]{:S(2)}, u32[]{:S(2)}) %collective-permute-start.17) | collective-permute-done | bytes 196640 | tf_op jit(solution)/shard_map/gram_over_columns/ppermute | solution.py:55
  78.6 5.1 %newton_schulz.1.refs_0_ = bf16[384,256]{1,0:T(8,128)(2,1)S(1)} custom-call(f32[384,384]{1,0:T(8,128)S(1)} %gram.9.mine_ref, f32[384,384]{1,0:T(8,128)S(1)} %collective-permute-done.22.other_ref, bf16[384,256]{1,0:T(8,128)(2,1)S(1)} %get-tuple-element.24.refs_0_.direction_ref), custom_call_target="tpu_custom_call" | custom-call | flops 7516192768 | bytes 2097152 | tf_op jit(solution)/shard_map/newton_schulz/pallas_call | solution.py:281
  83.7 1.4 %collective-permute-start.23 = (bf16[384,256]{1,0:T(8,128)(2,1)S(1)}, bf16[384,256]{1,0:T(8,128)(2,1)S(1)}, u32[]{:S(2)}, u32[]{:S(2)}) collective-permute-start(bf16[384,256]{1,0:T(8,128)(2,1)S(1)} %newton_schulz.1.refs_0_), channel_id=1, source_target_pairs={{0,48},{1,193},{2,50},{3,195},{4,52},{5,197},{6,54},{7,199},{8,56}... | collective-permute-start | bytes 589832 | tf_op jit(solution)/shard_map/update_gather/ppermute | solution.py:55
  85.2 3.3 %collective-permute-start.25 = (bf16[384,256]{1,0:T(8,128)(2,1)S(1)}, bf16[384,256]{1,0:T(8,128)(2,1)S(1)}, u32[]{:S(2)}, u32[]{:S(2)}) collective-permute-start(bf16[384,256]{1,0:T(8,128)(2,1)S(1)} %newton_schulz.1.refs_0_), channel_id=1, source_target_pairs={{0,32},{1,129},{2,34},{3,131},{4,36},{5,133},{6,38},{7,135},{8,40}... | collective-permute-start | bytes 589832 | tf_op jit(solution)/shard_map/update_gather/ppermute | solution.py:55
  88.5 2.4 %collective-permute-done.23.refs_1_ = bf16[384,256]{1,0:T(8,128)(2,1)S(1)} collective-permute-done((bf16[384,256]{1,0:T(8,128)(2,1)S(1)}, bf16[384,256]{1,0:T(8,128)(2,1)S(1)}, u32[]{:S(2)}, u32[]{:S(2)}) %collective-permute-start.23) | collective-permute-done | bytes 196640 | tf_op jit(solution)/shard_map/update_gather/ppermute | solution.py:55
  90.9 3.3 %collective-permute-done.25.refs_3_ = bf16[384,256]{1,0:T(8,128)(2,1)S(1)} collective-permute-done((bf16[384,256]{1,0:T(8,128)(2,1)S(1)}, bf16[384,256]{1,0:T(8,128)(2,1)S(1)}, u32[]{:S(2)}, u32[]{:S(2)}) %collective-permute-start.25) | collective-permute-done | bytes 196640 | tf_op jit(solution)/shard_map/update_gather/ppermute | solution.py:55
  94.3 1.7 %collective-permute-start.28 = (bf16[4,192,256]{2,1,0:T(8,128)(2,1)S(1)}, bf16[4,192,256]{2,1,0:T(8,128)(2,1)S(1)}, u32[]{:S(2)}, u32[]{:S(2)}) collective-permute-start(bf16[4,192,256]{2,1,0:T(8,128)(2,1)S(1)} %get-tuple-element.19.first_ref), channel_id=1, source_target_pairs={{0,192},{1,49},{2,194},{3,51},{4,196},{5,53},{6,198},{7,55},{8,200... | collective-permute-start | bytes 1179656 | tf_op jit(solution)/shard_map/update_gather/ppermute | solution.py:55
  96.8 5.4 %collective-permute-done.28.second_ref = bf16[4,192,256]{2,1,0:T(8,128)(2,1)S(1)} collective-permute-done((bf16[4,192,256]{2,1,0:T(8,128)(2,1)S(1)}, bf16[4,192,256]{2,1,0:T(8,128)(2,1)S(1)}, u32[]{:S(2)}, u32[]{:S(2)}) %collective-permute-start.28) | collective-permute-done | bytes 393248 | tf_op jit(solution)/shard_map/update_gather/ppermute | solution.py:55
  102.2 2.7 %collective-permute-start.29 = (bf16[8,192,256]{2,1,0:T(8,128)(2,1)S(1)}, bf16[8,192,256]{2,1,0:T(8,128)(2,1)S(1)}, u32[]{:S(2)}, u32[]{:S(2)}) collective-permute-start(bf16[8,192,256]{2,1,0:T(8,128)(2,1)S(1)} %append.7.refs_0_), channel_id=1, source_target_pairs={{0,64},{1,17},{2,66},{3,19},{4,68},{5,21},{6,70},{7,23},{8,72},{9,... | collective-permute-start | bytes 2359304 | tf_op jit(solution)/shard_map/update_gather/ppermute | solution.py:55
  110.0 4.9 %collective-permute-done.29.refs_0_ = bf16[8,192,256]{2,1,0:T(8,128)(2,1)S(1)} collective-permute-done((bf16[8,192,256]{2,1,0:T(8,128)(2,1)S(1)}, bf16[8,192,256]{2,1,0:T(8,128)(2,1)S(1)}, u32[]{:S(2)}, u32[]{:S(2)}) %collective-permute-start.29) | collective-permute-done | bytes 786464 | tf_op jit(solution)/shard_map/update_gather/ppermute | solution.py:55
  (65 shorter events, 23.5 us)
Async XLA Ops:
  3.2 4.1 %copy-start.2 = (bf16[16,384,256]{2,1,0:T(8,128)(2,1)S(1)}, bf16[16,384,256]{2,1,0:T(8,128)(2,1)}, u32[]{:S(2)}) copy-start(bf16[16,384,256]{2,1,0:T(8,128)(2,1)} %refs_0_.1) | copy-start | bytes 9437188
  3.9 12.1 %collective-permute-start.2 = (bf16[8,192,256]{2,1,0:T(8,128)(2,1)S(1)}, bf16[8,192,256]{2,1,0:T(8,128)(2,1)S(1)}, u32[]{:S(2)}, u32[]{:S(2)}) collective-permute-start(bf16[8,192,256]{2,1,0:T(8,128)(2,1)S(1)} %get-tuple-element.15), channel_id=1, source_target_pairs={{0,192},{1,49},{2,194},{3,51},{4,196},{5,53},{6,198},{7,55},{8,200... | collective-permute-start | bytes 2359304 | tf_op jit(solution)/shard_map/sum_over_replicas/ppermute | solution.py:55
  5.4 14.3 %collective-permute-start = (bf16[8,192,256]{2,1,0:T(8,128)(2,1)S(1)}, bf16[8,192,256]{2,1,0:T(8,128)(2,1)S(1)}, u32[]{:S(2)}, u32[]{:S(2)}) collective-permute-start(bf16[8,192,256]{2,1,0:T(8,128)(2,1)S(1)} %get-tuple-element.13), channel_id=1, source_target_pairs={{0,64},{1,17},{2,66},{3,19},{4,68},{5,21},{6,70},{7,23},{8,72},{9,... | collective-permute-start | bytes 2359304 | tf_op jit(solution)/shard_map/sum_over_replicas/ppermute | solution.py:55
  16.1 9.3 %collective-permute-start.3 = (bf16[4,192,256]{2,1,0:T(8,128)(2,1)S(1)}, bf16[4,192,256]{2,1,0:T(8,128)(2,1)S(1)}, u32[]{:S(2)}, u32[]{:S(2)}) collective-permute-start(bf16[4,192,256]{2,1,0:T(8,128)(2,1)S(1)} %get-tuple-element.22), channel_id=1, source_target_pairs={{0,64},{1,17},{2,66},{3,19},{4,68},{5,21},{6,70},{7,23},{8,72},{9,... | collective-permute-start | bytes 1179656 | tf_op jit(solution)/shard_map/sum_over_replicas/ppermute | solution.py:55
  19.9 7.9 %collective-permute-start.1 = (bf16[4,192,256]{2,1,0:T(8,128)(2,1)S(1)}, bf16[4,192,256]{2,1,0:T(8,128)(2,1)S(1)}, u32[]{:S(2)}, u32[]{:S(2)}) collective-permute-start(bf16[4,192,256]{2,1,0:T(8,128)(2,1)S(1)} %get-tuple-element.20), channel_id=1, source_target_pairs={{0,192},{1,49},{2,194},{3,51},{4,196},{5,53},{6,198},{7,55},{8,200... | collective-permute-start | bytes 1179656 | tf_op jit(solution)/shard_map/sum_over_replicas/ppermute | solution.py:55
  27.9 7.3 %collective-permute-start.6 = (bf16[384,256]{1,0:T(8,128)(2,1)S(1)}, bf16[384,256]{1,0:T(8,128)(2,1)S(1)}, u32[]{:S(2)}, u32[]{:S(2)}) collective-permute-start(bf16[384,256]{1,0:T(8,128)(2,1)S(1)} %pad_maximum_fusion.2), channel_id=1, source_target_pairs={{0,32},{1,129},{2,34},{3,131},{4,36},{5,133},{6,38},{7,135},{8,40}... | collective-permute-start | bytes 589832 | tf_op jit(solution)/shard_map/sum_over_replicas/ppermute | solution.py:55
  29.6 6.4 %collective-permute-start.5 = (bf16[384,256]{1,0:T(8,128)(2,1)S(1)}, bf16[384,256]{1,0:T(8,128)(2,1)S(1)}, u32[]{:S(2)}, u32[]{:S(2)}) collective-permute-start(bf16[384,256]{1,0:T(8,128)(2,1)S(1)} %pad_maximum_fusion.1), channel_id=1, source_target_pairs={{0,16},{1,65},{2,18},{3,67},{4,20},{5,69},{6,22},{7,71},{8,24},{9,... | collective-permute-start | bytes 589832 | tf_op jit(solution)/shard_map/sum_over_replicas/ppermute | solution.py:55
  30.4 7.0 %collective-permute-start.4 = (bf16[384,256]{1,0:T(8,128)(2,1)S(1)}, bf16[384,256]{1,0:T(8,128)(2,1)S(1)}, u32[]{:S(2)}, u32[]{:S(2)}) collective-permute-start(bf16[384,256]{1,0:T(8,128)(2,1)S(1)} %pad_maximum_fusion), channel_id=1, source_target_pairs={{0,48},{1,193},{2,50},{3,195},{4,52},{5,197},{6,54},{7,199},{8,56}... | collective-permute-start | bytes 589832 | tf_op jit(solution)/shard_map/sum_over_replicas/ppermute | solution.py:55
  37.5 1.5 %collective-permute-start.7 = (bf16[384,256]{1,0:T(8,128)(2,1)S(1)}, bf16[384,256]{1,0:T(8,128)(2,1)S(1)}, u32[]{:S(2)}, u32[]{:S(2)}) collective-permute-start(bf16[384,256]{1,0:T(8,128)(2,1)S(1)} %get-tuple-element.24.refs_0_.direction_ref), channel_id=1, source_target_pairs={{0,1},{1,0},{2,3},{3,2},{4,5},{5,4},{6,7},{7,6},{8,9},{9,8},{10,11... | collective-permute-start | bytes 589832 | tf_op jit(solution)/shard_map/gram_over_columns/ppermute | solution.py:55
  39.1 8.6 %collective-permute-start.8 = (bf16[384,256]{1,0:T(8,128)(2,1)S(1)}, bf16[384,256]{1,0:T(8,128)(2,1)S(1)}, u32[]{:S(2)}, u32[]{:S(2)}) collective-permute-start(bf16[384,256]{1,0:T(8,128)(2,1)S(1)} %bitcast.20), channel_id=1, source_target_pairs={{0,48},{1,193},{2,50},{3,195},{4,52},{5,197},{6,54},{7,199},{8,56}... | collective-permute-start | bytes 589832 | tf_op jit(solution)/shard_map/gram_over_columns/moment_gather/ppermute | solution.py:55
  41.0 6.7 %collective-permute-start.9 = (bf16[384,256]{1,0:T(8,128)(2,1)S(1)}, bf16[384,256]{1,0:T(8,128)(2,1)S(1)}, u32[]{:S(2)}, u32[]{:S(2)}) collective-permute-start(bf16[384,256]{1,0:T(8,128)(2,1)S(1)} %bitcast.21), channel_id=1, source_target_pairs={{0,16},{1,65},{2,18},{3,67},{4,20},{5,69},{6,22},{7,71},{8,24},{9,... | collective-permute-start | bytes 589832 | tf_op jit(solution)/shard_map/gram_over_columns/moment_gather/ppermute | solution.py:55
  41.0 8.6 %collective-permute-start.10 = (bf16[384,256]{1,0:T(8,128)(2,1)S(1)}, bf16[384,256]{1,0:T(8,128)(2,1)S(1)}, u32[]{:S(2)}, u32[]{:S(2)}) collective-permute-start(bf16[384,256]{1,0:T(8,128)(2,1)S(1)} %bitcast.22), channel_id=1, source_target_pairs={{0,32},{1,129},{2,34},{3,131},{4,36},{5,133},{6,38},{7,135},{8,40}... | collective-permute-start | bytes 589832 | tf_op jit(solution)/shard_map/gram_over_columns/moment_gather/ppermute | solution.py:55
  43.8 9.5 %collective-permute-start.18 = (bf16[384,256]{1,0:T(8,128)(2,1)S(1)}, bf16[384,256]{1,0:T(8,128)(2,1)S(1)}, u32[]{:S(2)}, u32[]{:S(2)}) collective-permute-start(bf16[384,256]{1,0:T(8,128)(2,1)S(1)} %get-tuple-element.24.refs_0_.direction_ref), channel_id=1, source_target_pairs={{0,2},{1,15},{2,4},{3,1},{4,6},{5,3},{6,8},{7,5},{8,10},{9,7},{10,... | collective-permute-start | bytes 589832 | tf_op jit(solution)/shard_map/gram_over_columns/ppermute | solution.py:55
  45.8 9.7 %collective-permute-start.15 = (bf16[384,256]{1,0:T(8,128)(2,1)S(1)}, bf16[384,256]{1,0:T(8,128)(2,1)S(1)}, u32[]{:S(2)}, u32[]{:S(2)}) collective-permute-start(bf16[384,256]{1,0:T(8,128)(2,1)S(1)} %collective-permute-done.7.refs_1_), channel_id=1, source_target_pairs={{0,2},{1,15},{2,4},{3,1},{4,6},{5,3},{6,8},{7,5},{8,10},{9,7},{10,... | collective-permute-start | bytes 589832 | tf_op jit(solution)/shard_map/gram_over_columns/ppermute | solution.py:55
  49.6 19.6 %collective-permute-start.11 = (bf16[4,192,256]{2,1,0:T(8,128)(2,1)S(1)}, bf16[4,192,256]{2,1,0:T(8,128)(2,1)S(1)}, u32[]{:S(2)}, u32[]{:S(2)}) collective-permute-start(bf16[4,192,256]{2,1,0:T(8,128)(2,1)S(1)} %get-tuple-element.16.first_ref.refs_4_), channel_id=1, source_target_pairs={{0,64},{1,17},{2,66},{3,19},{4,68},{5,21},{6,70},{7,23},{8,72},{9,... | collective-permute-start | bytes 1179656 | tf_op jit(solution)/shard_map/gram_over_columns/moment_gather/ppermute | solution.py:55
  52.1 17.3 %collective-permute-start.13 = (bf16[4,192,256]{2,1,0:T(8,128)(2,1)S(1)}, bf16[4,192,256]{2,1,0:T(8,128)(2,1)S(1)}, u32[]{:S(2)}, u32[]{:S(2)}) collective-permute-start(bf16[4,192,256]{2,1,0:T(8,128)(2,1)S(1)} %get-tuple-element.17.first_ref.refs_3_), channel_id=1, source_target_pairs={{0,192},{1,49},{2,194},{3,51},{4,196},{5,53},{6,198},{7,55},{8,200... | collective-permute-start | bytes 1179656 | tf_op jit(solution)/shard_map/gram_over_columns/moment_gather/ppermute | solution.py:55
  53.3 9.1 %collective-permute-start.19 = (bf16[384,256]{1,0:T(8,128)(2,1)S(1)}, bf16[384,256]{1,0:T(8,128)(2,1)S(1)}, u32[]{:S(2)}, u32[]{:S(2)}) collective-permute-start(bf16[384,256]{1,0:T(8,128)(2,1)S(1)} %collective-permute-done.18.refs_0_), channel_id=1, source_target_pairs={{0,2},{1,15},{2,4},{3,1},{4,6},{5,3},{6,8},{7,5},{8,10},{9,7},{10,... | collective-permute-start | bytes 589832 | tf_op jit(solution)/shard_map/gram_over_columns/ppermute | solution.py:55
  55.4 9.1 %collective-permute-start.16 = (bf16[384,256]{1,0:T(8,128)(2,1)S(1)}, bf16[384,256]{1,0:T(8,128)(2,1)S(1)}, u32[]{:S(2)}, u32[]{:S(2)}) collective-permute-start(bf16[384,256]{1,0:T(8,128)(2,1)S(1)} %collective-permute-done.15.refs_1_), channel_id=1, source_target_pairs={{0,2},{1,15},{2,4},{3,1},{4,6},{5,3},{6,8},{7,5},{8,10},{9,7},{10,... | collective-permute-start | bytes 589832 | tf_op jit(solution)/shard_map/gram_over_columns/ppermute | solution.py:55
  62.5 6.9 %collective-permute-start.20 = (bf16[384,256]{1,0:T(8,128)(2,1)S(1)}, bf16[384,256]{1,0:T(8,128)(2,1)S(1)}, u32[]{:S(2)}, u32[]{:S(2)}) collective-permute-start(bf16[384,256]{1,0:T(8,128)(2,1)S(1)} %collective-permute-done.19.refs_0_), channel_id=1, source_target_pairs={{0,2},{1,15},{2,4},{3,1},{4,6},{5,3},{6,8},{7,5},{8,10},{9,7},{10,... | collective-permute-start | bytes 589832 | tf_op jit(solution)/shard_map/gram_over_columns/ppermute | solution.py:55
  62.5 10.0 %collective-permute-start.21 = (bf16[384,256]{1,0:T(8,128)(2,1)S(1)}, bf16[384,256]{1,0:T(8,128)(2,1)S(1)}, u32[]{:S(2)}, u32[]{:S(2)}) collective-permute-start(bf16[384,256]{1,0:T(8,128)(2,1)S(1)} %collective-permute-done.19.refs_0_), channel_id=1, source_target_pairs={{0,4},{1,13},{2,6},{3,15},{4,8},{5,1},{6,10},{7,3},{8,12},{9,5},{1... | collective-permute-start | bytes 589832 | tf_op jit(solution)/shard_map/gram_over_columns/ppermute | solution.py:55
  64.6 11.1 %collective-permute-start.17 = (bf16[384,256]{1,0:T(8,128)(2,1)S(1)}, bf16[384,256]{1,0:T(8,128)(2,1)S(1)}, u32[]{:S(2)}, u32[]{:S(2)}) collective-permute-start(bf16[384,256]{1,0:T(8,128)(2,1)S(1)} %collective-permute-done.16.refs_1_), channel_id=1, source_target_pairs={{0,2},{1,15},{2,4},{3,1},{4,6},{5,3},{6,8},{7,5},{8,10},{9,7},{10,... | collective-permute-start | bytes 589832 | tf_op jit(solution)/shard_map/gram_over_columns/ppermute | solution.py:55
  76.0 2.6 %collective-permute-start.22 = (f32[384,384]{1,0:T(8,128)S(1)}, f32[384,384]{1,0:T(8,128)S(1)}, u32[]{:S(2)}, u32[]{:S(2)}) collective-permute-start(f32[384,384]{1,0:T(8,128)S(1)} %gram.9.mine_ref), channel_id=1, source_target_pairs={{0,1},{1,0},{2,3},{3,2},{4,5},{5,4},{6,7},{7,6},{8,9},{9,8},{10,11... | collective-permute-start | bytes 1769480 | tf_op jit(solution)/shard_map/gram_over_columns/ppermute | solution.py:55
  76.1 20.7 %collective-permute-start.12 = (bf16[8,192,256]{2,1,0:T(8,128)(2,1)S(1)}, bf16[8,192,256]{2,1,0:T(8,128)(2,1)S(1)}, u32[]{:S(2)}, u32[]{:S(2)}) collective-permute-start(bf16[8,192,256]{2,1,0:T(8,128)(2,1)S(1)} %append.4.refs_1_.refs_4_), channel_id=1, source_target_pairs={{0,192},{1,49},{2,194},{3,51},{4,196},{5,53},{6,198},{7,55},{8,200... | collective-permute-start | bytes 2359304 | tf_op jit(solution)/shard_map/gram_over_columns/moment_gather/ppermute | solution.py:55
  77.3 19.5 %collective-permute-start.14 = (bf16[8,192,256]{2,1,0:T(8,128)(2,1)S(1)}, bf16[8,192,256]{2,1,0:T(8,128)(2,1)S(1)}, u32[]{:S(2)}, u32[]{:S(2)}) collective-permute-start(bf16[8,192,256]{2,1,0:T(8,128)(2,1)S(1)} %append.5.refs_0_.refs_3_), channel_id=1, source_target_pairs={{0,64},{1,17},{2,66},{3,19},{4,68},{5,21},{6,70},{7,23},{8,72},{9,... | collective-permute-start | bytes 2359304 | tf_op jit(solution)/shard_map/gram_over_columns/moment_gather/ppermute | solution.py:55
  83.7 7.2 %collective-permute-start.23 = (bf16[384,256]{1,0:T(8,128)(2,1)S(1)}, bf16[384,256]{1,0:T(8,128)(2,1)S(1)}, u32[]{:S(2)}, u32[]{:S(2)}) collective-permute-start(bf16[384,256]{1,0:T(8,128)(2,1)S(1)} %newton_schulz.1.refs_0_), channel_id=1, source_target_pairs={{0,48},{1,193},{2,50},{3,195},{4,52},{5,197},{6,54},{7,199},{8,56}... | collective-permute-start | bytes 589832 | tf_op jit(solution)/shard_map/update_gather/ppermute | solution.py:55
  85.1 5.8 %collective-permute-start.24 = (bf16[384,256]{1,0:T(8,128)(2,1)S(1)}, bf16[384,256]{1,0:T(8,128)(2,1)S(1)}, u32[]{:S(2)}, u32[]{:S(2)}) collective-permute-start(bf16[384,256]{1,0:T(8,128)(2,1)S(1)} %newton_schulz.1.refs_0_), channel_id=1, source_target_pairs={{0,16},{1,65},{2,18},{3,67},{4,20},{5,69},{6,22},{7,71},{8,24},{9,... | collective-permute-start | bytes 589832 | tf_op jit(solution)/shard_map/update_gather/ppermute | solution.py:55
  85.2 9.1 %collective-permute-start.25 = (bf16[384,256]{1,0:T(8,128)(2,1)S(1)}, bf16[384,256]{1,0:T(8,128)(2,1)S(1)}, u32[]{:S(2)}, u32[]{:S(2)}) collective-permute-start(bf16[384,256]{1,0:T(8,128)(2,1)S(1)} %newton_schulz.1.refs_0_), channel_id=1, source_target_pairs={{0,32},{1,129},{2,34},{3,131},{4,36},{5,133},{6,38},{7,135},{8,40}... | collective-permute-start | bytes 589832 | tf_op jit(solution)/shard_map/update_gather/ppermute | solution.py:55
  94.3 7.9 %collective-permute-start.28 = (bf16[4,192,256]{2,1,0:T(8,128)(2,1)S(1)}, bf16[4,192,256]{2,1,0:T(8,128)(2,1)S(1)}, u32[]{:S(2)}, u32[]{:S(2)}) collective-permute-start(bf16[4,192,256]{2,1,0:T(8,128)(2,1)S(1)} %get-tuple-element.19.first_ref), channel_id=1, source_target_pairs={{0,192},{1,49},{2,194},{3,51},{4,196},{5,53},{6,198},{7,55},{8,200... | collective-permute-start | bytes 1179656 | tf_op jit(solution)/shard_map/update_gather/ppermute | solution.py:55
  96.0 8.9 %collective-permute-start.26 = (bf16[4,192,256]{2,1,0:T(8,128)(2,1)S(1)}, bf16[4,192,256]{2,1,0:T(8,128)(2,1)S(1)}, u32[]{:S(2)}, u32[]{:S(2)}) collective-permute-start(bf16[4,192,256]{2,1,0:T(8,128)(2,1)S(1)} %get-tuple-element.18.first_ref), channel_id=1, source_target_pairs={{0,64},{1,17},{2,66},{3,19},{4,68},{5,21},{6,70},{7,23},{8,72},{9,... | collective-permute-start | bytes 1179656 | tf_op jit(solution)/shard_map/update_gather/ppermute | solution.py:55
  102.2 12.6 %collective-permute-start.29 = (bf16[8,192,256]{2,1,0:T(8,128)(2,1)S(1)}, bf16[8,192,256]{2,1,0:T(8,128)(2,1)S(1)}, u32[]{:S(2)}, u32[]{:S(2)}) collective-permute-start(bf16[8,192,256]{2,1,0:T(8,128)(2,1)S(1)} %append.7.refs_0_), channel_id=1, source_target_pairs={{0,64},{1,17},{2,66},{3,19},{4,68},{5,21},{6,70},{7,23},{8,72},{9,... | collective-permute-start | bytes 2359304 | tf_op jit(solution)/shard_map/update_gather/ppermute | solution.py:55
  104.9 12.1 %collective-permute-start.27 = (bf16[8,192,256]{2,1,0:T(8,128)(2,1)S(1)}, bf16[8,192,256]{2,1,0:T(8,128)(2,1)S(1)}, u32[]{:S(2)}, u32[]{:S(2)}) collective-permute-start(bf16[8,192,256]{2,1,0:T(8,128)(2,1)S(1)} %append.6.refs_1_), channel_id=1, source_target_pairs={{0,192},{1,49},{2,194},{3,51},{4,196},{5,53},{6,198},{7,55},{8,200... | collective-permute-start | bytes 2359304 | tf_op jit(solution)/shard_map/update_gather/ppermute | solution.py:55
  110.0 7.1 %copy-start = (bf16[16,384,256]{2,1,0:T(8,128)(2,1)S(1)}, bf16[16,384,256]{2,1,0:T(8,128)(2,1)}, u32[]{:S(2)}) copy-start(bf16[16,384,256]{2,1,0:T(8,128)(2,1)} %assemble.8.refs_2_) | copy-start | bytes 9437188
  (2 other events, 2.5 us)
